TPU v7x, 512 devices: a whole 4x4x16 slice. The times are simulated.
512 devices in a mesh: pp: 8 (over y, z_hi), ep: 64 (over x, z_lo, core).
Axes of the slice: x: 4, y: 4, z: 16 (z_hi: 2, z_lo: 8; z = z_hi * 8 + z_lo), core: 2. Of those that a mesh axis runs over, the one named last changes fastest.
Arguments:
- carried: bfloat16 [8, 4096, 3584], P('pp', 'ep'), may hold values from -6 to 6
- saved: bfloat16 [8, 4096, 3584], P('pp', 'ep'), may hold values from -6 to 6
- grads_prev: bfloat16 [8, 4096, 3584], P('pp', 'ep'), may hold values from -6 to 6
- routes_fwd: int32 [8, 4096, 1], P('pp', 'ep'), may hold values from 0 to 7; in each aligned block of 64 rows (0 to 63, 64 to 127, ..., all dimensions but the last counted through in order) at most 8 rows name the same one
- gates_fwd: float32 [8, 4096, 1], P('pp', 'ep'), may hold values from 0.1 to 1
- routes_bwd: int32 [8, 4096, 1], P('pp', 'ep'), may hold values from 0 to 7; in each aligned block of 64 rows (0 to 63, 64 to 127, ..., all dimensions but the last counted through in order) at most 8 rows name the same one
- gates_bwd: float32 [8, 4096, 1], P('pp', 'ep'), may hold values from 0.1 to 1
- w_gate: bfloat16 [8, 64, 3584, 128], P('pp', 'ep'), may hold values from -0.09375 to 0.09375
- w_up: bfloat16 [8, 64, 3584, 128], P('pp', 'ep'), may hold values from -0.09375 to 0.09375
- w_down: bfloat16 [8, 64, 128, 3584], P('pp', 'ep'), may hold values from -0.1875 to 0.1875
Outputs:
- acts: bfloat16 [8, 4096, 3584], P('pp', 'ep')
- input_grads: bfloat16 [8, 4096, 3584], P('pp', 'ep')
Inputs may be any that keep to these rules, and one draw needn't show every extreme that they name: `routes_fwd`: in the rows of one device every expert is named by exactly 8 routes. `routes_bwd`: in the rows of one device every expert is named by exactly 8 routes.
All inputs are finite; a program needn't handle non-finite values.
Results may differ from a plain program's by a relative error of at most 0.01.
Values may be sent and summed in bfloat16 or wider, within the bound.
No kernel may reach another device: no remote copies, remote signals or barrier semaphores. Data moves between devices by JAX's collectives and lax.ppermute only.
A program may use at most 64 MiB of HBM per device.

v0:
```python
import jax
import jax.numpy as jnp
from jax import lax
from jax.sharding import PartitionSpec as P

W = 8


epsilon = 1e-06


def shifted(x, axis, by):
    length = lax.axis_size(axis)
    return lax.ppermute(x, axis, [(i, (i + by) % length) for i in range(length)])


def normalize(activations):
    values = activations.astype(jnp.float32)
    rms_scale = lax.rsqrt(jnp.mean(values * values, axis=-1, keepdims=True) + epsilon)
    return (values * rms_scale, rms_scale)


def slot_positions(routes, expert_count, slot_depth):
    flat_routes = routes.reshape(-1)
    onehot = (flat_routes[:, None] == jnp.arange(expert_count, dtype=jnp.int32)[None, :]).astype(
        jnp.int32
    )
    ranked = jnp.cumsum(onehot, axis=0) - 1
    return flat_routes * slot_depth + jnp.sum(ranked * onehot, axis=1)


def spread_rows(token_rows, slot_index, expert_count, slot_depth, device_count):
    feature_count = token_rows.shape[1]
    packed = (
        jnp.zeros((expert_count * slot_depth, feature_count), token_rows.dtype)
        .at[slot_index]
        .set(token_rows)
    )
    packed = packed.reshape(expert_count, 1, slot_depth, feature_count)
    copies = jnp.broadcast_to(
        packed, (expert_count, device_count // expert_count, slot_depth, feature_count)
    )
    return copies.reshape(device_count, slot_depth, feature_count)


def collect_rows(returned, slot_index, expert_count, slot_depth, token_count, route_count):
    feature_count = returned.shape[2]
    blocked = returned.reshape(expert_count, -1, slot_depth, feature_count)
    summed = jnp.sum(blocked, axis=1, dtype=jnp.float32).reshape(
        expert_count * slot_depth, feature_count
    )
    return summed[slot_index].reshape(token_count, route_count, feature_count)


def expert_out(expert_rows, gate_weights, up_weights, down_weights):
    flat_rows = expert_rows.reshape(-1, expert_rows.shape[2])
    gate_pre = jnp.dot(flat_rows, gate_weights, preferred_element_type=jnp.float32)
    up_pre = jnp.dot(flat_rows, up_weights, preferred_element_type=jnp.float32)
    hidden = (jax.nn.silu(gate_pre) * up_pre).astype(jnp.bfloat16)
    result = jnp.dot(hidden, down_weights, preferred_element_type=jnp.float32).astype(jnp.bfloat16)
    return result.reshape(expert_rows.shape)


def expert_grad(expert_rows, cotangents, gate_weights, up_weights, down_weights):
    flat_rows = expert_rows.reshape(-1, expert_rows.shape[2])
    flat_cot = cotangents.reshape(flat_rows.shape)
    gate_pre = jnp.dot(flat_rows, gate_weights, preferred_element_type=jnp.float32)
    up_pre = jnp.dot(flat_rows, up_weights, preferred_element_type=jnp.float32)
    hidden_grad = jnp.dot(flat_cot, down_weights.T, preferred_element_type=jnp.float32)
    sigmoid_val = jax.nn.sigmoid(gate_pre)
    gate_grad = (
        hidden_grad * up_pre * sigmoid_val * (1.0 + gate_pre * (1.0 - sigmoid_val))
    ).astype(jnp.bfloat16)
    up_grad = (hidden_grad * jax.nn.silu(gate_pre)).astype(jnp.bfloat16)
    summed = jnp.dot(gate_grad, gate_weights.T, preferred_element_type=jnp.float32) + jnp.dot(
        up_grad, up_weights.T, preferred_element_type=jnp.float32
    )
    return summed.astype(jnp.bfloat16).reshape(expert_rows.shape)


def body(
    carried, saved, grads_prev, routes_fwd, gates_fwd, routes_bwd, gates_bwd, w_gate, w_up, w_down
):
    device_count = lax.axis_size("ep")
    expert_count = device_count // W
    route_count = routes_fwd.shape[2]
    gate_weights = w_gate[0, 0]
    up_weights = w_up[0, 0]
    down_weights = w_down[0, 0]
    section_input = shifted(carried[0], "pp", 1)
    cotangent = shifted(grads_prev[0], "pp", -1)
    forward_count = section_input.shape[0]
    backward_count = cotangent.shape[0]
    forward_depth = forward_count * route_count // expert_count
    backward_depth = backward_count * route_count // expert_count
    feature_count = section_input.shape[1]
    normed_fwd, scale_fwd = normalize(section_input)
    forward_slots = slot_positions(routes_fwd[0], expert_count, forward_depth)
    send_fwd = spread_rows(
        jnp.repeat(normed_fwd.astype(jnp.bfloat16), route_count, axis=0),
        forward_slots,
        expert_count,
        forward_depth,
        device_count,
    )
    normed_bwd, scale_bwd = normalize(saved[0])
    backward_slots = slot_positions(routes_bwd[0], expert_count, backward_depth)
    send_saved = spread_rows(
        jnp.repeat(normed_bwd.astype(jnp.bfloat16), route_count, axis=0),
        backward_slots,
        expert_count,
        backward_depth,
        device_count,
    )
    gated = (
        (gates_bwd[0][:, :, None] * cotangent.astype(jnp.float32)[:, None, :])
        .astype(jnp.bfloat16)
        .reshape(-1, feature_count)
    )
    send_cot = spread_rows(gated, backward_slots, expert_count, backward_depth, device_count)
    recv_fwd = lax.all_to_all(send_fwd, "ep", split_axis=0, concat_axis=0, tiled=True)
    back_fwd = lax.all_to_all(
        expert_out(recv_fwd, gate_weights, up_weights, down_weights),
        "ep",
        split_axis=0,
        concat_axis=0,
        tiled=True,
    )
    recv_saved, recv_cot = (
        lax.all_to_all(send_saved, "ep", split_axis=0, concat_axis=0, tiled=True),
        lax.all_to_all(send_cot, "ep", split_axis=0, concat_axis=0, tiled=True),
    )
    back_bwd = lax.all_to_all(
        expert_grad(recv_saved, recv_cot, gate_weights, up_weights, down_weights),
        "ep",
        split_axis=0,
        concat_axis=0,
        tiled=True,
    )
    picked_fwd = collect_rows(
        back_fwd, forward_slots, expert_count, forward_depth, forward_count, route_count
    )
    mixture = jnp.einsum("tk,tkd->td", gates_fwd[0], picked_fwd)
    output_act = (section_input.astype(jnp.float32) + mixture).astype(jnp.bfloat16)
    picked_bwd = collect_rows(
        back_bwd, backward_slots, expert_count, backward_depth, backward_count, route_count
    )
    summed = jnp.sum(picked_bwd, axis=1)
    projection = jnp.mean(normed_bwd * summed, axis=-1, keepdims=True)
    output_grad = (
        cotangent.astype(jnp.float32) + scale_bwd * (summed - normed_bwd * projection)
    ).astype(jnp.bfloat16)
    return (output_act[None], output_grad[None])


def solution(mesh):
    return jax.shard_map(
        body,
        mesh=mesh,
        in_specs=(
            P("pp", "ep", None),
            P("pp", "ep", None),
            P("pp", "ep", None),
            P("pp", "ep", None),
            P("pp", "ep", None),
            P("pp", "ep", None),
            P("pp", "ep", None),
            P("pp", "ep", None, None),
            P("pp", "ep", None, None),
            P("pp", "ep", None, None),
        ),
        out_specs=(P("pp", "ep", None), P("pp", "ep", None)),
        check_vma=False,
    )
```

profile of v0, /device:TPU:24, one launch (start us, length us, event | category | flops | bytes accessed | tf_op | source)
XLA Modules:
  0.0 964.8 jit_solution(17239811288074545735)
XLA Ops:
  3.1 1.2 fusion.41
  4.3 1.9 scatter_custom_fusion.2
  6.2 2.1 broadcast_in_dim.44
  8.3 16.4 %all-to-all-start.3 = ((bf16[64,8,3584]{2,1,0:T(8,128)(2,1)}), bf16[64,8,3584]{2,1,0:T(8,128)(2,1)}, u32[]{:S(2)}, u32[]{:S(2)}) async-start(bf16[64,8,3584]{2,1,0:T(8,128)(2,1)} %bitcast.108), calls=%async_computation.3 | async-start | bytes 7340032 | tf_op jit(solution)/shard_map/all_to_all | solution.py:130
  24.6 8.4 collective-permute-start.1
  33.0 87.2 %collective-permute-done.1 = bf16[64,3584]{1,0:T(8,128)(2,1)S(1)} collective-permute-done((bf16[64,3584]{1,0:T(8,128)(2,1)S(1)}, bf16[64,3584]{1,0:T(8,128)(2,1)S(1)}, u32[]{:S(2)}, u32[]{:S(2)}) %collective-permute-start.1) | collective-permute-done | bytes 458784 | tf_op jit(solution)/shard_map/ppermute | solution.py:14
  120.2 1.4 scatter_custom_fusion.1
  121.6 102.6 %all-to-all-done.3 = bf16[64,8,3584]{2,1,0:T(8,128)(2,1)} async-done(((bf16[64,8,3584]{2,1,0:T(8,128)(2,1)}), bf16[64,8,3584]{2,1,0:T(8,128)(2,1)}, u32[]{:S(2)}, u32[]{:S(2)}) %all-to-all-start.3) | async-done | bytes 3670048 | tf_op jit(solution)/shard_map/all_to_all | solution.py:130
  224.3 2.1 broadcast_in_dim.20
  226.4 11.8 %all-to-all-start.2 = ((bf16[64,8,3584]{2,1,0:T(8,128)(2,1)}), bf16[64,8,3584]{2,1,0:T(8,128)(2,1)}, u32[]{:S(2)}, u32[]{:S(2)}) async-start(bf16[64,8,3584]{2,1,0:T(8,128)(2,1)} %bitcast.106), calls=%async_computation.2 | async-start | bytes 7340032 | tf_op jit(solution)/shard_map/all_to_all | solution.py:131
  238.2 8.2 collective-permute-start
  246.7 87.1 %collective-permute-done = bf16[64,3584]{1,0:T(8,128)(2,1)S(1)} collective-permute-done((bf16[64,3584]{1,0:T(8,128)(2,1)S(1)}, bf16[64,3584]{1,0:T(8,128)(2,1)S(1)}, u32[]{:S(2)}, u32[]{:S(2)}) %collective-permute-start) | collective-permute-done | bytes 458784 | tf_op jit(solution)/shard_map/ppermute | solution.py:14
  334.1 1.4 scatter_custom_fusion
  335.5 102.3 %all-to-all-done.2 = bf16[64,8,3584]{2,1,0:T(8,128)(2,1)} async-done(((bf16[64,8,3584]{2,1,0:T(8,128)(2,1)}), bf16[64,8,3584]{2,1,0:T(8,128)(2,1)}, u32[]{:S(2)}, u32[]{:S(2)}) %all-to-all-start.2) | async-done | bytes 3670048 | tf_op jit(solution)/shard_map/all_to_all | solution.py:131
  437.8 2.0 broadcast_in_dim.17
  439.9 12.0 %all-to-all-start = ((bf16[64,8,3584]{2,1,0:T(8,128)(2,1)}), bf16[64,8,3584]{2,1,0:T(8,128)(2,1)}, u32[]{:S(2)}, u32[]{:S(2)}) async-start(bf16[64,8,3584]{2,1,0:T(8,128)(2,1)} %bitcast.107), calls=%async_computation | async-start | bytes 7340032 | tf_op jit(solution)/shard_map/all_to_all | solution.py:121
  451.9 3.2 fusion.2
  455.1 3.1 fusion.6
  458.3 8.9 fusion.34
  467.2 6.1 fusion.1
  473.3 138.7 %all-to-all-done = bf16[64,8,3584]{2,1,0:T(8,128)(2,1)} async-done(((bf16[64,8,3584]{2,1,0:T(8,128)(2,1)}), bf16[64,8,3584]{2,1,0:T(8,128)(2,1)}, u32[]{:S(2)}, u32[]{:S(2)}) %all-to-all-start) | async-done | bytes 3670048 | tf_op jit(solution)/shard_map/all_to_all | solution.py:121
  612.0 11.7 %all-to-all-start.4 = ((bf16[64,8,3584]{2,1,0:T(8,128)(2,1)}), bf16[64,8,3584]{2,1,0:T(8,128)(2,1)}, u32[]{:S(2)}, u32[]{:S(2)}) async-start(bf16[64,8,3584]{2,1,0:T(8,128)(2,1)} %fusion.1), calls=%async_computation.4 | async-start | bytes 7340032 | tf_op jit(solution)/shard_map/all_to_all | solution.py:133
  623.7 3.1 fusion.10
  626.8 7.8 fusion
  634.6 149.4 %all-to-all-done.4 = bf16[64,8,3584]{2,1,0:T(8,128)(2,1)} async-done(((bf16[64,8,3584]{2,1,0:T(8,128)(2,1)}), bf16[64,8,3584]{2,1,0:T(8,128)(2,1)}, u32[]{:S(2)}, u32[]{:S(2)}) %all-to-all-start.4) | async-done | bytes 3670048 | tf_op jit(solution)/shard_map/all_to_all | solution.py:133
  784.0 11.9 %all-to-all-start.1 = ((bf16[64,8,3584]{2,1,0:T(8,128)(2,1)}), bf16[64,8,3584]{2,1,0:T(8,128)(2,1)}, u32[]{:S(2)}, u32[]{:S(2)}) async-start(bf16[64,8,3584]{2,1,0:T(8,128)(2,1)} %fusion), calls=%async_computation.1 | async-start | bytes 7340032 | tf_op jit(solution)/shard_map/all_to_all | solution.py:122
  795.9 2.6 convert_reduce_fusion
  799.9 156.1 %all-to-all-done.1 = bf16[64,8,3584]{2,1,0:T(8,128)(2,1)} async-done(((bf16[64,8,3584]{2,1,0:T(8,128)(2,1)}), bf16[64,8,3584]{2,1,0:T(8,128)(2,1)}, u32[]{:S(2)}, u32[]{:S(2)}) %all-to-all-start.1) | async-done | bytes 3670048 | tf_op jit(solution)/shard_map/all_to_all | solution.py:122
  956.0 2.6 convert_reduce_fusion.1
  958.7 1.8 gather_fusion
  960.4 2.1 fusion.61
  962.5 2.2 fusion.58
  (38 shorter events, 4.3 us)
Async XLA Ops:
  0.6 457.6 %copy-start = (bf16[1,1,3584,128]{3,2,1,0:T(8,128)(2,1)S(1)}, bf16[1,1,3584,128]{3,2,1,0:T(8,128)(2,1)}, u32[]{:S(2)}) copy-start(bf16[1,1,3584,128]{3,2,1,0:T(8,128)(2,1)} %param.18) | copy-start | bytes 2752516
  8.3 16.4 %copy-start.9 = (bf16[1,64,3584]{2,1,0:T(8,128)(2,1)S(1)}, bf16[1,64,3584]{2,1,0:T(8,128)(2,1)}, u32[]{:S(2)}) copy-start(bf16[1,64,3584]{2,1,0:T(8,128)(2,1)} %param.12) | copy-start | bytes 1376260
  8.3 111.9 %copy-start.7 = (f32[1,64,1]{1,2,0:T(1,128)S(1)}, f32[1,64,1]{1,2,0:T(1,128)}, u32[]{:S(2)}) copy-start(f32[1,64,1]{1,2,0:T(1,128)} %param.16) | copy-start | bytes 772
  8.3 216.0 %all-to-all-start.3 = ((bf16[64,8,3584]{2,1,0:T(8,128)(2,1)}), bf16[64,8,3584]{2,1,0:T(8,128)(2,1)}, u32[]{:S(2)}, u32[]{:S(2)}) async-start(bf16[64,8,3584]{2,1,0:T(8,128)(2,1)} %bitcast.108), calls=%async_computation.3 | async-start | bytes 7340032 | tf_op jit(solution)/shard_map/all_to_all | solution.py:130
  24.6 95.6 %collective-permute-start.1 = (bf16[64,3584]{1,0:T(8,128)(2,1)S(1)}, bf16[64,3584]{1,0:T(8,128)(2,1)S(1)}, u32[]{:S(2)}, u32[]{:S(2)}) collective-permute-start(bf16[64,3584]{1,0:T(8,128)(2,1)S(1)} %bitcast.118), channel_id=1, source_target_pairs={{0,448},{64,0},{128,64},{192,128},{256,192},{320,256},{384,320},{4... | collective-permute-start | bytes 1376264 | tf_op jit(solution)/shard_map/ppermute | solution.py:14
  120.2 106.2 %copy-start.5 = (bf16[64,3584]{1,0:T(8,128)(2,1)}, bf16[64,3584]{1,0:T(8,128)(2,1)S(1)}, u32[]{:S(2)}) copy-start(bf16[64,3584]{1,0:T(8,128)(2,1)S(1)} %collective-permute-done.1) | copy-start | bytes 1376260
  226.4 11.8 %copy-start.10 = (bf16[1,64,3584]{2,1,0:T(8,128)(2,1)S(1)}, bf16[1,64,3584]{2,1,0:T(8,128)(2,1)}, u32[]{:S(2)}) copy-start(bf16[1,64,3584]{2,1,0:T(8,128)(2,1)} %param.10) | copy-start | bytes 1376260
  226.4 20.0 %copy-start.6 = (s32[1,64,1]{1,2,0:T(1,128)S(1)}, s32[1,64,1]{1,2,0:T(1,128)}, u32[]{:S(2)}) copy-start(s32[1,64,1]{1,2,0:T(1,128)} %param.13) | copy-start | bytes 772
  226.4 211.5 %all-to-all-start.2 = ((bf16[64,8,3584]{2,1,0:T(8,128)(2,1)}), bf16[64,8,3584]{2,1,0:T(8,128)(2,1)}, u32[]{:S(2)}, u32[]{:S(2)}) async-start(bf16[64,8,3584]{2,1,0:T(8,128)(2,1)} %bitcast.106), calls=%async_computation.2 | async-start | bytes 7340032 | tf_op jit(solution)/shard_map/all_to_all | solution.py:131
  238.2 95.7 %collective-permute-start = (bf16[64,3584]{1,0:T(8,128)(2,1)S(1)}, bf16[64,3584]{1,0:T(8,128)(2,1)S(1)}, u32[]{:S(2)}, u32[]{:S(2)}) collective-permute-start(bf16[64,3584]{1,0:T(8,128)(2,1)S(1)} %bitcast.119), channel_id=1, source_target_pairs={{0,64},{64,128},{128,192},{192,256},{256,320},{320,384},{384,448},... | collective-permute-start | bytes 1376264 | tf_op jit(solution)/shard_map/ppermute | solution.py:14
  333.9 106.0 %copy-start.3 = (bf16[64,3584]{1,0:T(8,128)(2,1)}, bf16[64,3584]{1,0:T(8,128)(2,1)S(1)}, u32[]{:S(2)}) copy-start(bf16[64,3584]{1,0:T(8,128)(2,1)S(1)} %collective-permute-done) | copy-start | bytes 1376260
  439.9 12.0 %copy-start.1 = (bf16[1,1,3584,128]{3,2,1,0:T(8,128)(2,1)S(1)}, bf16[1,1,3584,128]{3,2,1,0:T(8,128)(2,1)}, u32[]{:S(2)}) copy-start(bf16[1,1,3584,128]{3,2,1,0:T(8,128)(2,1)} %param.17) | copy-start | bytes 2752516
  439.9 172.1 %all-to-all-start = ((bf16[64,8,3584]{2,1,0:T(8,128)(2,1)}), bf16[64,8,3584]{2,1,0:T(8,128)(2,1)}, u32[]{:S(2)}, u32[]{:S(2)}) async-start(bf16[64,8,3584]{2,1,0:T(8,128)(2,1)} %bitcast.107), calls=%async_computation | async-start | bytes 7340032 | tf_op jit(solution)/shard_map/all_to_all | solution.py:121
  451.9 3.2 copy-start.4
  612.0 172.0 %all-to-all-start.4 = ((bf16[64,8,3584]{2,1,0:T(8,128)(2,1)}), bf16[64,8,3584]{2,1,0:T(8,128)(2,1)}, u32[]{:S(2)}, u32[]{:S(2)}) async-start(bf16[64,8,3584]{2,1,0:T(8,128)(2,1)} %fusion.1), calls=%async_computation.4 | async-start | bytes 7340032 | tf_op jit(solution)/shard_map/all_to_all | solution.py:133
  784.0 172.0 %all-to-all-start.1 = ((bf16[64,8,3584]{2,1,0:T(8,128)(2,1)}), bf16[64,8,3584]{2,1,0:T(8,128)(2,1)}, u32[]{:S(2)}, u32[]{:S(2)}) async-start(bf16[64,8,3584]{2,1,0:T(8,128)(2,1)} %fusion), calls=%async_computation.1 | async-start | bytes 7340032 | tf_op jit(solution)/shard_map/all_to_all | solution.py:122
  798.6 1.0 copy-start.2
  958.6 3.9 copy-start.8
where the time goes:
time: 970 us; the launch traced here: 965 us
  waiting for transfers between devices  823 us (85%)
  starting transfers between devices  80.3 us (8%)
  matrix products  32.4 us (3%)
  other arithmetic  18.8 us (2%)
    ppermute x2, waiting for transfers between devices, shifted(): lax.ppermute(x, axis, [(i, (i + by) % length) for i in range(length)])  174 us
    all_to_all x1, waiting for transfers between devices, body(): lax.all_to_all(expert_out(recv_fwd, gate_weights, up_weights, down_weight...  156 us
    all_to_all x1, waiting for transfers between devices, body(): lax.all_to_all(expert_grad(recv_saved, recv_cot, gate_weights, up_weights...  149 us
    all_to_all x1, waiting for transfers between devices, body(): lax.all_to_all(send_fwd, 'ep', split_axis=0, concat_axis=0, tiled=True)  139 us
    all_to_all x1, waiting for transfers between devices, body(): lax.all_to_all(send_saved, 'ep', split_axis=0, concat_axis=0, tiled=True)  103 us
    all_to_all x1, waiting for transfers between devices, body(): lax.all_to_all(send_cot, 'ep', split_axis=0, concat_axis=0, tiled=True)  102 us
  transfers between devices with their start and end apart: 7, of which 7 were waited for; matrix products, arithmetic and copies ran while one was open for 4% of the time, Pallas kernels for 0%

commit v1 on v0

v1 whole, which is shorter than its diff:
```python
import jax
import jax.numpy as jnp
from jax import lax
from jax.sharding import Mesh
from jax.sharding import PartitionSpec as P

AXES = ("y", "zh", "x", "zq", "zr", "c")
SIZES = (4, 2, 4, 2, 4, 2)
PP = ("y", "zh")
EP = ("x", "zq", "zr", "c")
Z16 = ("zh", "zq", "zr")
Z8 = ("zq", "zr")
EXPERTS = 8
DEPTH = 8
ROWS = EXPERTS * DEPTH
LANES = 128


epsilon = 1e-06


def normalize(activations):
    values = activations.astype(jnp.float32)
    rms_scale = lax.rsqrt(jnp.mean(values * values, axis=-1, keepdims=True) + epsilon)
    return (values * rms_scale, rms_scale)


def slot_matrix(routes):
    same = routes[:, None] == routes[None, :]
    order = jnp.arange(ROWS, dtype=jnp.int32)
    earlier = order[None, :] < order[:, None]
    rank = jnp.sum((same & earlier).astype(jnp.int32), axis=1)
    place = (routes % 2) * 4 + routes // 2
    slots = place * DEPTH + rank
    return (order[:, None] == slots[None, :]).astype(jnp.bfloat16)


def reorder(matrix, rows):
    return jnp.dot(matrix, rows, preferred_element_type=jnp.float32).astype(jnp.bfloat16)


def gate_lanes(gates):
    first = gates.astype(jnp.bfloat16)
    left = gates - first.astype(jnp.float32)
    second = left.astype(jnp.bfloat16)
    third = (left - second.astype(jnp.float32)).astype(jnp.bfloat16)
    three = jnp.stack([first, second, third], axis=1)
    return jnp.pad(three, ((0, 0), (0, LANES - 3)))


def gate_of(lanes):
    wide = lanes[:, :3].astype(jnp.float32)
    return (wide[:, 2:3] + wide[:, 1:2]) + wide[:, 0:1]


def rotated(x, axis, by):
    length = lax.axis_size(axis)
    return lax.ppermute(x, axis, [(i, (i + by) % length) for i in range(length)])


def gather_x(rows):
    return [rows] + [rotated(rows, "x", j) for j in (1, 2, 3)]


def scatter_sum_x(parts):
    own = parts[:ROWS]
    sent = parts.astype(jnp.bfloat16)
    total = own.astype(jnp.bfloat16).astype(jnp.float32)
    for j in (1, 2, 3):
        total = total + rotated(sent[j * ROWS : (j + 1) * ROWS], "x", -j).astype(jnp.float32)
    return total


def nt(a, b):
    return lax.dot_general(a, b, (((1,), (1,)), ((), ())), preferred_element_type=jnp.float32)


def expert_out(rows, gate_weights, up_weights, down_weights):
    gate_pre = nt(rows, gate_weights)
    up_pre = nt(rows, up_weights)
    hidden = (jax.nn.silu(gate_pre) * up_pre).astype(jnp.bfloat16)
    return jnp.dot(hidden, down_weights, preferred_element_type=jnp.float32)


def expert_grad(rows, cotangents, gate_weights, up_weights, down_weights):
    gate_pre = nt(rows, gate_weights)
    up_pre = nt(rows, up_weights)
    hidden_grad = nt(cotangents, down_weights)
    sigmoid_val = jax.nn.sigmoid(gate_pre)
    gate_grad = (
        hidden_grad * up_pre * sigmoid_val * (1.0 + gate_pre * (1.0 - sigmoid_val))
    ).astype(jnp.bfloat16)
    up_grad = (hidden_grad * jax.nn.silu(gate_pre)).astype(jnp.bfloat16)
    return jnp.dot(gate_grad, gate_weights, preferred_element_type=jnp.float32) + jnp.dot(
        up_grad, up_weights, preferred_element_type=jnp.float32
    )


def weights_along_x(w_gate, w_up, w_down):
    x, zr = lax.axis_index("x"), lax.axis_index("zr")
    stacked = jnp.stack([w_gate.T, w_up.T, w_down])
    units = stacked.shape[1] // 4
    pieces = stacked.reshape(3, 4, units, stacked.shape[2])

    def piece(index):
        return lax.dynamic_index_in_dim(pieces, index, axis=1, keepdims=False)

    along_x = jnp.stack(
        [piece(x)] + [rotated(piece((x + k) % 4), "x", k) for k in (1, 2, 3)]
    )

    def block(index):
        return lax.dynamic_index_in_dim(along_x, index % 4, axis=0, keepdims=False)

    return [block(x - zr - m + 8) for m in range(4)]


def weights_along_z(blocks):
    return blocks[:1] + [rotated(blocks[m], "zr", m) for m in (1, 2, 3)]


def weights_of_chip(blocks):
    mine = jnp.concatenate(blocks, axis=1)
    other = lax.ppermute(mine, "c", [(0, 1), (1, 0)])
    both = jnp.concatenate([mine, other], axis=1)
    return both[0], both[1], both[2]


def body(
    carried, saved, grads_prev, routes_fwd, gates_fwd, routes_bwd, gates_bwd, w_gate, w_up, w_down
):
    high = lax.axis_index("zh")
    features = carried.shape[2]
    own_fwd, own_bwd = routes_fwd[0, :, 0], routes_bwd[0, :, 0]
    flat = jnp.stack(
        [own_fwd.astype(jnp.float32), gates_fwd[0, :, 0], own_bwd.astype(jnp.float32), gates_bwd[0, :, 0]]
    )
    is_high = high == 1
    along_y = jnp.where(is_high, carried[0], grads_prev[0])
    flat, along_y = lax.optimization_barrier((flat, along_y))
    flat = lax.ppermute(flat, "zh", [(0, 1), (1, 0)])
    mid_fwd, mid_bwd = flat[0].astype(jnp.int32), flat[2].astype(jnp.int32)
    moves = []
    for y in range(4):
        moves.append((y * 2 + 1, ((y + 1) % 4) * 2 + 1))
        moves.append((y * 2, ((y + 3) % 4) * 2))
    along_y = lax.ppermute(along_y, PP, moves)
    fwd_rows = jnp.where(is_high, along_y, carried[0])
    cot_rows = jnp.where(is_high, grads_prev[0], along_y)

    blocks = weights_along_x(w_gate[0, 0], w_up[0, 0], w_down[0, 0])

    def dispatch(own, cross):
        both = jnp.concatenate(
            [jnp.where(is_high, cross, own), jnp.where(is_high, own, cross)], axis=0
        ).reshape(2 * EXPERTS, DEPTH, features + LANES)
        got = lax.all_to_all(both, Z16, split_axis=0, concat_axis=0, tiled=True)
        got = got.reshape(2, ROWS, features + LANES)
        return jnp.where(is_high, got[1], got[0]), jnp.where(is_high, got[0], got[1])

    def give_back(rows):
        got = lax.all_to_all(
            rows.reshape(EXPERTS, DEPTH, features), Z8, split_axis=0, concat_axis=0, tiled=True
        )
        return got.reshape(ROWS, features)

    home_bwd = slot_matrix(own_bwd)
    send_saved = jnp.pad(reorder(home_bwd, saved[0]), ((0, 0), (0, LANES)))
    send_cot = reorder(
        slot_matrix(mid_bwd), jnp.concatenate([cot_rows, gate_lanes(flat[3])], axis=1)
    )
    got_saved, got_cot = dispatch(send_saved, send_cot)
    blocks = weights_along_z(blocks)
    send_fwd = reorder(
        slot_matrix(mid_fwd), jnp.concatenate([fwd_rows, gate_lanes(flat[1])], axis=1)
    )
    send_fwd, blocks = lax.optimization_barrier((send_fwd, blocks))
    _, got_fwd = dispatch(jnp.zeros_like(send_fwd), send_fwd)

    normed_bwd, scale_bwd = normalize(got_saved[:, :features])
    cotangent = got_cot[:, :features].astype(jnp.float32)
    gated = (gate_of(got_cot[:, features:]) * cotangent).astype(jnp.bfloat16)
    gathered = [
        rows.reshape(2, ROWS, features)
        for rows in gather_x(jnp.concatenate([normed_bwd.astype(jnp.bfloat16), gated], axis=0))
    ]
    all_normed = jnp.concatenate([rows[0] for rows in gathered], axis=0)
    all_gated = jnp.concatenate([rows[1] for rows in gathered], axis=0)
    gate_weights, up_weights, down_weights = weights_of_chip(blocks)
    parts = expert_grad(
        all_normed,
        all_gated,
        gate_weights,
        up_weights,
        down_weights,
    )
    summed = scatter_sum_x(parts)
    projection = jnp.mean(normed_bwd * summed, axis=-1, keepdims=True)
    grads = (cotangent + scale_bwd * (summed - normed_bwd * projection)).astype(jnp.bfloat16)
    output_grad = reorder(home_bwd.T, give_back(grads))

    section_input = got_fwd[:, :features]
    normed_fwd, _ = normalize(section_input)
    parts = expert_out(
        jnp.concatenate(gather_x(normed_fwd.astype(jnp.bfloat16)), axis=0),
        gate_weights, up_weights, down_weights
    )
    mixture = gate_of(got_fwd[:, features:]) * scatter_sum_x(parts)
    acts = (section_input.astype(jnp.float32) + mixture).astype(jnp.bfloat16)
    output_act = reorder(slot_matrix(own_fwd).T, give_back(acts))
    return (output_act[None], output_grad[None])


def solution(mesh):
    fine = Mesh(mesh.devices.reshape(SIZES), AXES)
    rows = P(PP, EP, None)
    weights = P(PP, EP, None, None)
    return jax.shard_map(
        body,
        mesh=fine,
        in_specs=(rows,) * 7 + (weights,) * 3,
        out_specs=(rows, rows),
        check_vma=False,
    )
```

time: 970 us -> 379 us (0.39)
  waiting for transfers between devices: 823 us -> 188 us
  starting transfers between devices: 80.3 us -> 115 us
  local copies, waits for them, and re-layouts: 9.02 us -> 18.8 us
    all_to_all x5 -> x4, waiting for transfers between devices: 649 us -> 43.3 us  [the longest x2 23.7 us: give_back(): lax.all_to_all(rows.reshape(EXPERTS, DEPTH, features), Z8, split_axis=0,...]
    ppermute x2 -> x21, starting transfers between devices: 16.6 us -> 76.7 us  [the longest x18 56.4 us: rotated(): lax.ppermute(x, axis, [(i, (i + by) % length) for i in range(length)])]
    ppermute x2 -> x21, waiting for transfers between devices: 174 us -> 145 us  [the longest x18 145 us: rotated(): lax.ppermute(x, axis, [(i, (i + by) % length) for i in range(length)])]
    all_to_all x5 -> x4, starting transfers between devices: 63.7 us -> 38.1 us  [the longest x2 19.1 us: give_back(): lax.all_to_all(rows.reshape(EXPERTS, DEPTH, features), Z8, split_axis=0,...]
    dot_general x6 -> x11, matrix products: 32.4 us -> 28.3 us  [the longest x3 6.96 us: nt(): lax.dot_general(a, b, (((1,), (1,)), ((), ())), preferred_element_type=jn...]
  transfers between devices with their start and end apart: 7 -> 25, of which waited for: 7 -> 14; matrix products, arithmetic and copies ran while one was open for 4% -> 16% of each run, Pallas kernels for 0% -> 0%
where the time goes in v1:
time: 379 us; the launch traced here: 372 us
  waiting for transfers between devices  188 us (50%)
  starting transfers between devices  115 us (30%)
  matrix products  28.3 us (7%)
  other arithmetic  21 us (6%)
  local copies, waits for them, and re-layouts  18.8 us (5%)
    ppermute x18, waiting for transfers between devices, rotated(): lax.ppermute(x, axis, [(i, (i + by) % length) for i in range(length)])  145 us
    ppermute x18, starting transfers between devices, rotated(): lax.ppermute(x, axis, [(i, (i + by) % length) for i in range(length)])  56.4 us
    all_to_all x2, waiting for transfers between devices, give_back(): lax.all_to_all(rows.reshape(EXPERTS, DEPTH, features), Z8, split_axis=0,...  23.7 us
    all_to_all x2, waiting for transfers between devices, dispatch(): got = lax.all_to_all(both, Z16, split_axis=0, concat_axis=0, tiled=True)  19.6 us
    all_to_all x2, starting transfers between devices, give_back(): lax.all_to_all(rows.reshape(EXPERTS, DEPTH, features), Z8, split_axis=0,...  19.1 us
    all_to_all x2, starting transfers between devices, dispatch(): got = lax.all_to_all(both, Z16, split_axis=0, concat_axis=0, tiled=True)  18.9 us
    ppermute x1, starting transfers between devices, body(): flat = lax.ppermute(flat, 'zh', [(0, 1), (1, 0)])  15.7 us
    unnamed x32, local copies, waits for them, and re-layouts  8.82 us
  transfers between devices with their start and end apart: 25, of which 14 were waited for; matrix products, arithmetic and copies ran while one was open for 16% of the time, Pallas kernels for 0%

profile of v1, /device:TPU:24, one launch (start us, length us, event | category | flops | bytes accessed | tf_op | source)
XLA Modules:
  0.0 372.4 jit_solution(3777709713231874394)
XLA Ops:
  4.1 15.7 %collective-permute-start = (f32[4,64]{1,0:T(4,128)S(1)}, f32[4,64]{1,0:T(4,128)S(1)}, u32[]{:S(2)}, u32[]{:S(2)}) collective-permute-start(f32[4,64]{1,0:T(4,128)S(1)} %pad_maximum_fusion.15), channel_id=1, source_target_pairs={{0,64},{64,0},{1,65},{65,1},{2,66},{66,2},{3,67},{67,3},{4,68},{68... | collective-permute-start | bytes 3080 | tf_op jit(solution)/shard_map/ppermute | solution.py:141
  27.1 4.7 %collective-permute-start.4 = (bf16[3,32,3584]{2,1,0:T(8,128)(2,1)}, bf16[3,32,3584]{2,1,0:T(8,128)(2,1)}, u32[]{:S(2)}, u32[]{:S(2)}) collective-permute-start(bf16[3,32,3584]{2,1,0:T(8,128)(2,1)} %get-tuple-element.21), channel_id=1, source_target_pairs={{0,48},{16,0},{32,16},{48,32},{1,49},{17,1},{33,17},{49,33},{2,50}... | collective-permute-start | bytes 2064392 | tf_op jit(solution)/shard_map/ppermute | solution.py:58
  41.7 19.3 %collective-permute-done.4 = bf16[3,32,3584]{2,1,0:T(8,128)(2,1)} collective-permute-done((bf16[3,32,3584]{2,1,0:T(8,128)(2,1)}, bf16[3,32,3584]{2,1,0:T(8,128)(2,1)}, u32[]{:S(2)}, u32[]{:S(2)}) %collective-permute-start.4) | collective-permute-done | bytes 688160 | tf_op jit(solution)/shard_map/ppermute | solution.py:58
  61.0 5.4 %collective-permute-done.2 = bf16[3,32,3584]{2,1,0:T(8,128)(2,1)} collective-permute-done((bf16[3,32,3584]{2,1,0:T(8,128)(2,1)S(1)}, bf16[3,32,3584]{2,1,0:T(8,128)(2,1)}, u32[]{:S(2)}, u32[]{:S(2)}) %collective-permute-start.2) | collective-permute-done | bytes 688160 | tf_op jit(solution)/shard_map/ppermute | solution.py:58
  69.6 2.9 collective-permute-start.5
  72.5 3.4 collective-permute-start.6
  75.9 3.8 %collective-permute-start.7 = (bf16[3,32,3584]{2,1,0:T(8,128)(2,1)}, bf16[3,32,3584]{2,1,0:T(8,128)(2,1)S(1)}, u32[]{:S(2)}, u32[]{:S(2)}) collective-permute-start(bf16[3,32,3584]{2,1,0:T(8,128)(2,1)} %get-tuple-element.16), channel_id=1, source_target_pairs={{0,6},{2,0},{4,2},{6,4},{1,7},{3,1},{5,3},{7,5},{8,14},{10,8},{12,... | collective-permute-start | bytes 2064392 | tf_op jit(solution)/shard_map/ppermute | solution.py:58
  80.7 4.7 %all-to-all-start.2 = ((bf16[16,8,3712]{2,1,0:T(8,128)(2,1)}), bf16[16,8,3712]{2,1,0:T(8,128)(2,1)S(1)}, u32[]{:S(2)}, u32[]{:S(2)}) async-start(bf16[16,8,3712]{2,1,0:T(8,128)(2,1)} %maximum_bitcast_fusion.1), calls=%async_computation.2 | async-start | bytes 1900544 | tf_op jit(solution)/shard_map/all_to_all | solution.py:157
  85.6 15.9 %collective-permute-done.5 = bf16[3,32,3584]{2,1,0:T(8,128)(2,1)} collective-permute-done((bf16[3,32,3584]{2,1,0:T(8,128)(2,1)}, bf16[3,32,3584]{2,1,0:T(8,128)(2,1)}, u32[]{:S(2)}, u32[]{:S(2)}) %collective-permute-start.5) | collective-permute-done | bytes 688160 | tf_op jit(solution)/shard_map/ppermute | solution.py:58
  101.5 31.8 %collective-permute-done.6 = bf16[3,32,3584]{2,1,0:T(8,128)(2,1)} collective-permute-done((bf16[3,32,3584]{2,1,0:T(8,128)(2,1)}, bf16[3,32,3584]{2,1,0:T(8,128)(2,1)}, u32[]{:S(2)}, u32[]{:S(2)}) %collective-permute-start.6) | collective-permute-done | bytes 688160 | tf_op jit(solution)/shard_map/ppermute | solution.py:58
  133.3 5.8 %collective-permute-done.7 = bf16[3,32,3584]{2,1,0:T(8,128)(2,1)S(1)} collective-permute-done((bf16[3,32,3584]{2,1,0:T(8,128)(2,1)}, bf16[3,32,3584]{2,1,0:T(8,128)(2,1)S(1)}, u32[]{:S(2)}, u32[]{:S(2)}) %collective-permute-start.7) | collective-permute-done | bytes 688160 | tf_op jit(solution)/shard_map/ppermute | solution.py:58
  139.2 3.1 pad_maximum_fusion.2
  150.2 19.6 %all-to-all-done.2 = bf16[16,8,3712]{2,1,0:T(8,128)(2,1)S(1)} async-done(((bf16[16,8,3712]{2,1,0:T(8,128)(2,1)}), bf16[16,8,3712]{2,1,0:T(8,128)(2,1)S(1)}, u32[]{:S(2)}, u32[]{:S(2)}) %all-to-all-start.2) | async-done | bytes 950304 | tf_op jit(solution)/shard_map/all_to_all | solution.py:157
  169.8 14.3 %all-to-all-start = ((bf16[16,8,3712]{2,1,0:T(8,128)(2,1)}), bf16[16,8,3712]{2,1,0:T(8,128)(2,1)S(1)}, u32[]{:S(2)}, u32[]{:S(2)}) async-start(bf16[16,8,3712]{2,1,0:T(8,128)(2,1)} %maximum_bitcast_fusion), calls=%async_computation | async-start | bytes 1900544 | tf_op jit(solution)/shard_map/all_to_all | solution.py:157
  190.5 3.3 collective-permute-start.15
  193.9 3.5 constant_dynamic-update-slice_fusion
  197.3 12.8 %collective-permute-done.17 = bf16[128,3584]{1,0:T(8,128)(2,1)S(1)} collective-permute-done((bf16[128,3584]{1,0:T(8,128)(2,1)S(1)}, bf16[128,3584]{1,0:T(8,128)(2,1)S(1)}, u32[]{:S(2)}, u32[]{:S(2)}) %collective-permute-start.17) | collective-permute-done | bytes 917536 | tf_op jit(solution)/shard_map/ppermute | solution.py:58
  210.2 4.3 %collective-permute-done.16 = bf16[128,3584]{1,0:T(8,128)(2,1)S(1)} collective-permute-done((bf16[128,3584]{1,0:T(8,128)(2,1)S(1)}, bf16[128,3584]{1,0:T(8,128)(2,1)S(1)}, u32[]{:S(2)}, u32[]{:S(2)}) %collective-permute-start.16) | collective-permute-done | bytes 917536 | tf_op jit(solution)/shard_map/ppermute | solution.py:58
  214.6 14.4 %collective-permute-done.15 = bf16[128,3584]{1,0:T(8,128)(2,1)S(1)} collective-permute-done((bf16[128,3584]{1,0:T(8,128)(2,1)S(1)}, bf16[128,3584]{1,0:T(8,128)(2,1)S(1)}, u32[]{:S(2)}, u32[]{:S(2)}) %collective-permute-start.15) | collective-permute-done | bytes 917536 | tf_op jit(solution)/shard_map/ppermute | solution.py:58
  234.3 4.0 %fusion.13 = f32[256,3584]{1,0:T(8,128)} fusion(bf16[3,256,3584]{2,1,0:T(8,128)(2,1)} %constant_dynamic-update-slice_fusion, f32[256,256]{1,0:T(8,128)S(1)} %fusion.3, f32[256,256]{1,0:T(8,128)S(1)} %fusion.11), kind=kOutput, calls=%fused_computation.28 | convolution fusion | flops 470155264 | bytes 6029312 | tf_op jit(solution)/shard_map/dot_general | solution.py:94
  238.4 6.7 %fusion = bf16[256,3584]{1,0:T(8,128)(2,1)} fusion(f32[256,3584]{1,0:T(8,128)} %fusion.13, bf16[3,256,3584]{2,1,0:T(8,128)(2,1)} %constant_dynamic-update-slice_fusion, f32[256,256]{1,0:T(8,128)S(1)} %fusion.3, bf16[64,3584]{1,0:T(8,128)(2,1)S(1)} %get-tuple-element.38, bf16[64,3584]{1,0:T(8,128)(2,1)S(1)} %get-tuple-element.36, ...), kind=kOutput, calls=%fused_computation.1 | convolution fusion | flops 949354496 | bytes 11534336 | tf_op jit(solution)/shard_map/dot_general | solution.py:94
  249.4 4.0 %collective-permute-start.19 = (bf16[64,3584]{1,0:T(8,128)(2,1)}, bf16[64,3584]{1,0:T(8,128)(2,1)S(1)}, u32[]{:S(2)}, u32[]{:S(2)}) collective-permute-start(bf16[64,3584]{1,0:T(8,128)(2,1)} %get-tuple-element.26), channel_id=1, source_target_pairs={{0,32},{16,48},{32,0},{48,16},{1,33},{17,49},{33,1},{49,17},{2,34}... | collective-permute-start | bytes 1376264 | tf_op jit(solution)/shard_map/ppermute | solution.py:58
  253.4 3.3 collective-permute-start.18
  259.9 4.0 %collective-permute-start.9 = (bf16[64,3584]{1,0:T(8,128)(2,1)S(1)}, bf16[64,3584]{1,0:T(8,128)(2,1)}, u32[]{:S(2)}, u32[]{:S(2)}) collective-permute-start(bf16[64,3584]{1,0:T(8,128)(2,1)S(1)} %fusion.32), channel_id=1, source_target_pairs={{0,32},{16,48},{32,0},{48,16},{1,33},{17,49},{33,1},{49,17},{2,34}... | collective-permute-start | bytes 1376264 | tf_op jit(solution)/shard_map/ppermute | solution.py:58
  263.9 19.1 %collective-permute-done.20 = bf16[64,3584]{1,0:T(8,128)(2,1)S(1)} collective-permute-done((bf16[64,3584]{1,0:T(8,128)(2,1)}, bf16[64,3584]{1,0:T(8,128)(2,1)S(1)}, u32[]{:S(2)}, u32[]{:S(2)}) %collective-permute-start.20) | collective-permute-done | bytes 458784 | tf_op jit(solution)/shard_map/ppermute | solution.py:58
  288.6 9.5 %all-to-all-start.3 = ((bf16[8,8,3584]{2,1,0:T(8,128)(2,1)}), bf16[8,8,3584]{2,1,0:T(8,128)(2,1)S(1)}, u32[]{:S(2)}, u32[]{:S(2)}) async-start(bf16[8,8,3584]{2,1,0:T(8,128)(2,1)} %fusion.46), calls=%async_computation.3 | async-start | bytes 917504 | tf_op jit(solution)/shard_map/all_to_all | solution.py:162
  300.6 5.7 %convolution_convert_fusion = bf16[256,3584]{1,0:T(8,128)(2,1)} fusion(bf16[3,256,3584]{2,1,0:T(8,128)(2,1)} %constant_dynamic-update-slice_fusion, f32[256,256]{1,0:T(8,128)S(1)} %fusion.12, bf16[64,3584]{1,0:T(8,128)(2,1)S(1)} %collective-permute-done.10, bf16[64,3584]{1,0:T(8,128)(2,1)} %collective-permute-done.9, ...), kind=kOutput, calls=%fused_computation.2 | convolution fusion | flops 948174848 | bytes 7602176 | tf_op jit(solution)/shard_map/dot_general | solution.py:82
  309.7 6.6 %collective-permute-start.13 = (bf16[64,3584]{1,0:T(8,128)(2,1)S(1)}, bf16[64,3584]{1,0:T(8,128)(2,1)S(1)}, u32[]{:S(2)}, u32[]{:S(2)}) collective-permute-start(bf16[64,3584]{1,0:T(8,128)(2,1)S(1)} %get-tuple-element.29), channel_id=1, source_target_pairs={{0,32},{16,48},{32,0},{48,16},{1,33},{17,49},{33,1},{49,17},{2,34}... | collective-permute-start | bytes 1376264 | tf_op jit(solution)/shard_map/ppermute | solution.py:58
  318.4 5.0 %collective-permute-done.14 = bf16[64,3584]{1,0:T(8,128)(2,1)S(1)} collective-permute-done((bf16[64,3584]{1,0:T(8,128)(2,1)S(1)}, bf16[64,3584]{1,0:T(8,128)(2,1)S(1)}, u32[]{:S(2)}, u32[]{:S(2)}) %collective-permute-start.14) | collective-permute-done | bytes 458784 | tf_op jit(solution)/shard_map/ppermute | solution.py:58
  323.4 9.7 %collective-permute-done.13 = bf16[64,3584]{1,0:T(8,128)(2,1)S(1)} collective-permute-done((bf16[64,3584]{1,0:T(8,128)(2,1)S(1)}, bf16[64,3584]{1,0:T(8,128)(2,1)S(1)}, u32[]{:S(2)}, u32[]{:S(2)}) %collective-permute-start.13) | collective-permute-done | bytes 458784 | tf_op jit(solution)/shard_map/ppermute | solution.py:58
  336.7 9.6 %all-to-all-start.1 = ((bf16[8,8,3584]{2,1,0:T(8,128)(2,1)}), bf16[8,8,3584]{2,1,0:T(8,128)(2,1)S(1)}, u32[]{:S(2)}, u32[]{:S(2)}) async-start(bf16[8,8,3584]{2,1,0:T(8,128)(2,1)} %fusion.45), calls=%async_computation.1 | async-start | bytes 917504 | tf_op jit(solution)/shard_map/all_to_all | solution.py:162
  347.6 23.7 %all-to-all-done.1 = bf16[8,8,3584]{2,1,0:T(8,128)(2,1)S(1)} async-done(((bf16[8,8,3584]{2,1,0:T(8,128)(2,1)}), bf16[8,8,3584]{2,1,0:T(8,128)(2,1)S(1)}, u32[]{:S(2)}, u32[]{:S(2)}) %all-to-all-start.1) | async-done | bytes 458784 | tf_op jit(solution)/shard_map/all_to_all | solution.py:162
  (109 shorter events, 71.5 us)
Async XLA Ops:
  0.6 36.9 %copy-start = (bf16[1,64,3584]{2,1,0:T(8,128)(2,1)S(1)}, bf16[1,64,3584]{2,1,0:T(8,128)(2,1)}, u32[]{:S(2)}) copy-start(bf16[1,64,3584]{2,1,0:T(8,128)(2,1)} %param.11) | copy-start | bytes 1376260
  0.6 23.3 %copy-start.7 = (bf16[1,1,3584,128]{3,2,1,0:T(8,128)(2,1)S(1)}, bf16[1,1,3584,128]{3,2,1,0:T(8,128)(2,1)}, u32[]{:S(2)}) copy-start(bf16[1,1,3584,128]{3,2,1,0:T(8,128)(2,1)} %param.17) | copy-start | bytes 2752516
  4.1 34.5 %collective-permute-start = (f32[4,64]{1,0:T(4,128)S(1)}, f32[4,64]{1,0:T(4,128)S(1)}, u32[]{:S(2)}, u32[]{:S(2)}) collective-permute-start(f32[4,64]{1,0:T(4,128)S(1)} %pad_maximum_fusion.15), channel_id=1, source_target_pairs={{0,64},{64,0},{1,65},{65,1},{2,66},{66,2},{3,67},{67,3},{4,68},{68... | collective-permute-start | bytes 3080 | tf_op jit(solution)/shard_map/ppermute | solution.py:141
  19.8 19.5 %collective-permute-start.1 = (bf16[64,3584]{1,0:T(8,128)(2,1)}, bf16[64,3584]{1,0:T(8,128)(2,1)}, u32[]{:S(2)}, u32[]{:S(2)}) collective-permute-start(bf16[64,3584]{1,0:T(8,128)(2,1)} %bitcast_select_fusion.1), channel_id=1, source_target_pairs={{64,192},{0,384},{192,320},{128,0},{320,448},{256,128},{448,64},{3... | collective-permute-start | bytes 1376264 | tf_op jit(solution)/shard_map/ppermute | solution.py:147
  26.0 13.3 %copy-start.5 = (bf16[1,64,3584]{2,1,0:T(8,128)(2,1)S(1)}, bf16[1,64,3584]{2,1,0:T(8,128)(2,1)}, u32[]{:S(2)}) copy-start(bf16[1,64,3584]{2,1,0:T(8,128)(2,1)} %param.12) | copy-start | bytes 1376260
  26.0 13.3 %copy-start.6 = (bf16[1,64,3584]{2,1,0:T(8,128)(2,1)S(1)}, bf16[1,64,3584]{2,1,0:T(8,128)(2,1)}, u32[]{:S(2)}) copy-start(bf16[1,64,3584]{2,1,0:T(8,128)(2,1)} %param.10) | copy-start | bytes 1376260
  27.1 33.9 %collective-permute-start.4 = (bf16[3,32,3584]{2,1,0:T(8,128)(2,1)}, bf16[3,32,3584]{2,1,0:T(8,128)(2,1)}, u32[]{:S(2)}, u32[]{:S(2)}) collective-permute-start(bf16[3,32,3584]{2,1,0:T(8,128)(2,1)} %get-tuple-element.21), channel_id=1, source_target_pairs={{0,48},{16,0},{32,16},{48,32},{1,49},{17,1},{33,17},{49,33},{2,50}... | collective-permute-start | bytes 2064392 | tf_op jit(solution)/shard_map/ppermute | solution.py:58
  31.8 29.2 %collective-permute-start.3 = (bf16[3,32,3584]{2,1,0:T(8,128)(2,1)S(1)}, bf16[3,32,3584]{2,1,0:T(8,128)(2,1)}, u32[]{:S(2)}, u32[]{:S(2)}) collective-permute-start(bf16[3,32,3584]{2,1,0:T(8,128)(2,1)S(1)} %get-tuple-element.22), channel_id=1, source_target_pairs={{0,32},{16,48},{32,0},{48,16},{1,33},{17,49},{33,1},{49,17},{2,34}... | collective-permute-start | bytes 2064392 | tf_op jit(solution)/shard_map/ppermute | solution.py:58
  34.5 31.9 %collective-permute-start.2 = (bf16[3,32,3584]{2,1,0:T(8,128)(2,1)S(1)}, bf16[3,32,3584]{2,1,0:T(8,128)(2,1)}, u32[]{:S(2)}, u32[]{:S(2)}) collective-permute-start(bf16[3,32,3584]{2,1,0:T(8,128)(2,1)S(1)} %get-tuple-element.23), channel_id=1, source_target_pairs={{0,16},{16,32},{32,48},{48,0},{1,17},{17,33},{33,49},{49,1},{2,18}... | collective-permute-start | bytes 2064392 | tf_op jit(solution)/shard_map/ppermute | solution.py:58
  69.6 32.0 %collective-permute-start.5 = (bf16[3,32,3584]{2,1,0:T(8,128)(2,1)}, bf16[3,32,3584]{2,1,0:T(8,128)(2,1)}, u32[]{:S(2)}, u32[]{:S(2)}) collective-permute-start(bf16[3,32,3584]{2,1,0:T(8,128)(2,1)} %get-tuple-element.18), channel_id=1, source_target_pairs={{0,2},{2,4},{4,6},{6,0},{1,3},{3,5},{5,7},{7,1},{8,10},{10,12},{12... | collective-permute-start | bytes 2064392 | tf_op jit(solution)/shard_map/ppermute | solution.py:58
  72.5 60.9 %collective-permute-start.6 = (bf16[3,32,3584]{2,1,0:T(8,128)(2,1)}, bf16[3,32,3584]{2,1,0:T(8,128)(2,1)}, u32[]{:S(2)}, u32[]{:S(2)}) collective-permute-start(bf16[3,32,3584]{2,1,0:T(8,128)(2,1)} %get-tuple-element.17), channel_id=1, source_target_pairs={{0,4},{2,6},{4,0},{6,2},{1,5},{3,7},{5,1},{7,3},{8,12},{10,14},{12... | collective-permute-start | bytes 2064392 | tf_op jit(solution)/shard_map/ppermute | solution.py:58
  75.9 63.3 %collective-permute-start.7 = (bf16[3,32,3584]{2,1,0:T(8,128)(2,1)}, bf16[3,32,3584]{2,1,0:T(8,128)(2,1)S(1)}, u32[]{:S(2)}, u32[]{:S(2)}) collective-permute-start(bf16[3,32,3584]{2,1,0:T(8,128)(2,1)} %get-tuple-element.16), channel_id=1, source_target_pairs={{0,6},{2,0},{4,2},{6,4},{1,7},{3,1},{5,3},{7,5},{8,14},{10,8},{12,... | collective-permute-start | bytes 2064392 | tf_op jit(solution)/shard_map/ppermute | solution.py:58
  80.7 89.1 %all-to-all-start.2 = ((bf16[16,8,3712]{2,1,0:T(8,128)(2,1)}), bf16[16,8,3712]{2,1,0:T(8,128)(2,1)S(1)}, u32[]{:S(2)}, u32[]{:S(2)}) async-start(bf16[16,8,3712]{2,1,0:T(8,128)(2,1)} %maximum_bitcast_fusion.1), calls=%async_computation.2 | async-start | bytes 1900544 | tf_op jit(solution)/shard_map/all_to_all | solution.py:157
  142.2 51.6 %collective-permute-start.11 = (bf16[3,128,3584]{2,1,0:T(8,128)(2,1)}, bf16[3,128,3584]{2,1,0:T(8,128)(2,1)}, u32[]{:S(2)}, u32[]{:S(2)}) collective-permute-start(bf16[3,128,3584]{2,1,0:T(8,128)(2,1)} %pad_maximum_fusion.2), channel_id=1, source_target_pairs={{0,1},{1,0},{2,3},{3,2},{4,5},{5,4},{6,7},{7,6},{8,9},{9,8},{10,11... | collective-permute-start | bytes 8257544 | tf_op jit(solution)/shard_map/ppermute | solution.py:124
  169.8 86.9 %all-to-all-start = ((bf16[16,8,3712]{2,1,0:T(8,128)(2,1)}), bf16[16,8,3712]{2,1,0:T(8,128)(2,1)S(1)}, u32[]{:S(2)}, u32[]{:S(2)}) async-start(bf16[16,8,3712]{2,1,0:T(8,128)(2,1)} %maximum_bitcast_fusion), calls=%async_computation | async-start | bytes 1900544 | tf_op jit(solution)/shard_map/all_to_all | solution.py:157
  184.9 25.2 %collective-permute-start.17 = (bf16[128,3584]{1,0:T(8,128)(2,1)S(1)}, bf16[128,3584]{1,0:T(8,128)(2,1)S(1)}, u32[]{:S(2)}, u32[]{:S(2)}) collective-permute-start(bf16[128,3584]{1,0:T(8,128)(2,1)S(1)} %pad_maximum_fusion.5), channel_id=1, source_target_pairs={{0,48},{16,0},{32,16},{48,32},{1,49},{17,1},{33,17},{49,33},{2,50}... | collective-permute-start | bytes 2752520 | tf_op jit(solution)/shard_map/ppermute | solution.py:58
  187.8 26.7 %collective-permute-start.16 = (bf16[128,3584]{1,0:T(8,128)(2,1)S(1)}, bf16[128,3584]{1,0:T(8,128)(2,1)S(1)}, u32[]{:S(2)}, u32[]{:S(2)}) collective-permute-start(bf16[128,3584]{1,0:T(8,128)(2,1)S(1)} %pad_maximum_fusion.5), channel_id=1, source_target_pairs={{0,32},{16,48},{32,0},{48,16},{1,33},{17,49},{33,1},{49,17},{2,34}... | collective-permute-start | bytes 2752520 | tf_op jit(solution)/shard_map/ppermute | solution.py:58
  190.5 38.5 %collective-permute-start.15 = (bf16[128,3584]{1,0:T(8,128)(2,1)S(1)}, bf16[128,3584]{1,0:T(8,128)(2,1)S(1)}, u32[]{:S(2)}, u32[]{:S(2)}) collective-permute-start(bf16[128,3584]{1,0:T(8,128)(2,1)S(1)} %pad_maximum_fusion.5), channel_id=1, source_target_pairs={{0,16},{16,32},{32,48},{48,0},{1,17},{17,33},{33,49},{49,1},{2,18}... | collective-permute-start | bytes 2752520 | tf_op jit(solution)/shard_map/ppermute | solution.py:58
  247.5 35.4 %collective-permute-start.20 = (bf16[64,3584]{1,0:T(8,128)(2,1)}, bf16[64,3584]{1,0:T(8,128)(2,1)S(1)}, u32[]{:S(2)}, u32[]{:S(2)}) collective-permute-start(bf16[64,3584]{1,0:T(8,128)(2,1)} %get-tuple-element.25), channel_id=1, source_target_pairs={{0,16},{16,32},{32,48},{48,0},{1,17},{17,33},{33,49},{49,1},{2,18}... | collective-permute-start | bytes 1376264 | tf_op jit(solution)/shard_map/ppermute | solution.py:58
  249.4 35.4 %collective-permute-start.19 = (bf16[64,3584]{1,0:T(8,128)(2,1)}, bf16[64,3584]{1,0:T(8,128)(2,1)S(1)}, u32[]{:S(2)}, u32[]{:S(2)}) collective-permute-start(bf16[64,3584]{1,0:T(8,128)(2,1)} %get-tuple-element.26), channel_id=1, source_target_pairs={{0,32},{16,48},{32,0},{48,16},{1,33},{17,49},{33,1},{49,17},{2,34}... | collective-permute-start | bytes 1376264 | tf_op jit(solution)/shard_map/ppermute | solution.py:58
  253.4 31.4 %collective-permute-start.18 = (bf16[64,3584]{1,0:T(8,128)(2,1)}, bf16[64,3584]{1,0:T(8,128)(2,1)}, u32[]{:S(2)}, u32[]{:S(2)}) collective-permute-start(bf16[64,3584]{1,0:T(8,128)(2,1)} %get-tuple-element.24), channel_id=1, source_target_pairs={{0,48},{16,0},{32,16},{48,32},{1,49},{17,1},{33,17},{49,33},{2,50}... | collective-permute-start | bytes 1376264 | tf_op jit(solution)/shard_map/ppermute | solution.py:58
  256.7 28.2 %copy-start.2 = (bf16[256,3584]{1,0:T(8,128)(2,1)S(1)}, bf16[256,3584]{1,0:T(8,128)(2,1)}, u32[]{:S(2)}) copy-start(bf16[256,3584]{1,0:T(8,128)(2,1)} %fusion) | copy-start | bytes 5505028
  257.2 41.0 %collective-permute-start.10 = (bf16[64,3584]{1,0:T(8,128)(2,1)S(1)}, bf16[64,3584]{1,0:T(8,128)(2,1)S(1)}, u32[]{:S(2)}, u32[]{:S(2)}) collective-permute-start(bf16[64,3584]{1,0:T(8,128)(2,1)S(1)} %fusion.32), channel_id=1, source_target_pairs={{0,48},{16,0},{32,16},{48,32},{1,49},{17,1},{33,17},{49,33},{2,50}... | collective-permute-start | bytes 1376264 | tf_op jit(solution)/shard_map/ppermute | solution.py:58
  259.9 38.3 %collective-permute-start.9 = (bf16[64,3584]{1,0:T(8,128)(2,1)S(1)}, bf16[64,3584]{1,0:T(8,128)(2,1)}, u32[]{:S(2)}, u32[]{:S(2)}) collective-permute-start(bf16[64,3584]{1,0:T(8,128)(2,1)S(1)} %fusion.32), channel_id=1, source_target_pairs={{0,32},{16,48},{32,0},{48,16},{1,33},{17,49},{33,1},{49,17},{2,34}... | collective-permute-start | bytes 1376264 | tf_op jit(solution)/shard_map/ppermute | solution.py:58
  282.9 15.2 %collective-permute-start.8 = (bf16[64,3584]{1,0:T(8,128)(2,1)S(1)}, bf16[64,3584]{1,0:T(8,128)(2,1)}, u32[]{:S(2)}, u32[]{:S(2)}) collective-permute-start(bf16[64,3584]{1,0:T(8,128)(2,1)S(1)} %fusion.32), channel_id=1, source_target_pairs={{0,16},{16,32},{32,48},{48,0},{1,17},{17,33},{33,49},{49,1},{2,18}... | collective-permute-start | bytes 1376264 | tf_op jit(solution)/shard_map/ppermute | solution.py:58
  288.6 48.1 %all-to-all-start.3 = ((bf16[8,8,3584]{2,1,0:T(8,128)(2,1)}), bf16[8,8,3584]{2,1,0:T(8,128)(2,1)S(1)}, u32[]{:S(2)}, u32[]{:S(2)}) async-start(bf16[8,8,3584]{2,1,0:T(8,128)(2,1)} %fusion.46), calls=%async_computation.3 | async-start | bytes 917504 | tf_op jit(solution)/shard_map/all_to_all | solution.py:162
  306.4 39.9 %copy-start.11 = (s32[1,64,1]{1,2,0:T(1,128)S(1)}, s32[1,64,1]{1,2,0:T(1,128)}, u32[]{:S(2)}) copy-start(s32[1,64,1]{1,2,0:T(1,128)} %param.13) | copy-start | bytes 772
  307.8 15.7 %collective-permute-start.14 = (bf16[64,3584]{1,0:T(8,128)(2,1)S(1)}, bf16[64,3584]{1,0:T(8,128)(2,1)S(1)}, u32[]{:S(2)}, u32[]{:S(2)}) collective-permute-start(bf16[64,3584]{1,0:T(8,128)(2,1)S(1)} %get-tuple-element.28), channel_id=1, source_target_pairs={{0,16},{16,32},{32,48},{48,0},{1,17},{17,33},{33,49},{49,1},{2,18}... | collective-permute-start | bytes 1376264 | tf_op jit(solution)/shard_map/ppermute | solution.py:58
  309.7 23.5 %collective-permute-start.13 = (bf16[64,3584]{1,0:T(8,128)(2,1)S(1)}, bf16[64,3584]{1,0:T(8,128)(2,1)S(1)}, u32[]{:S(2)}, u32[]{:S(2)}) collective-permute-start(bf16[64,3584]{1,0:T(8,128)(2,1)S(1)} %get-tuple-element.29), channel_id=1, source_target_pairs={{0,32},{16,48},{32,0},{48,16},{1,33},{17,49},{33,1},{49,17},{2,34}... | collective-permute-start | bytes 1376264 | tf_op jit(solution)/shard_map/ppermute | solution.py:58
  316.3 18.3 %collective-permute-start.12 = (bf16[64,3584]{1,0:T(8,128)(2,1)S(1)}, bf16[64,3584]{1,0:T(8,128)(2,1)S(1)}, u32[]{:S(2)}, u32[]{:S(2)}) collective-permute-start(bf16[64,3584]{1,0:T(8,128)(2,1)S(1)} %get-tuple-element.27), channel_id=1, source_target_pairs={{0,48},{16,0},{32,16},{48,32},{1,49},{17,1},{33,17},{49,33},{2,50}... | collective-permute-start | bytes 1376264 | tf_op jit(solution)/shard_map/ppermute | solution.py:58
  318.2 54.2 %copy-start.1 = (bf16[1,64,3584]{2,1,0:T(8,128)(2,1)S(1)}, bf16[1,64,3584]{2,1,0:T(8,128)(2,1)}, u32[]{:S(2)}) copy-start(bf16[1,64,3584]{2,1,0:T(8,128)(2,1)} %param.11) | copy-start | bytes 1376260
  336.7 34.7 %all-to-all-start.1 = ((bf16[8,8,3584]{2,1,0:T(8,128)(2,1)}), bf16[8,8,3584]{2,1,0:T(8,128)(2,1)S(1)}, u32[]{:S(2)}, u32[]{:S(2)}) async-start(bf16[8,8,3584]{2,1,0:T(8,128)(2,1)} %fusion.45), calls=%async_computation.1 | async-start | bytes 917504 | tf_op jit(solution)/shard_map/all_to_all | solution.py:162
  (5 other events, 20.3 us)

commit v2 on v1

--- a/solution.py
+++ b/solution.py
@@ -59,7 +59,7 @@
 
 
 def gather_x(rows):
-    return [rows] + [rotated(rows, "x", j) for j in (1, 2, 3)]
+    return jnp.concatenate([rows] + [rotated(rows, "x", j) for j in (1, 2, 3)], axis=0)
 
 
 def scatter_sum_x(parts):
@@ -137,14 +137,14 @@
     )
     is_high = high == 1
     along_y = jnp.where(is_high, carried[0], grads_prev[0])
-    flat, along_y = lax.optimization_barrier((flat, along_y))
-    flat = lax.ppermute(flat, "zh", [(0, 1), (1, 0)])
-    mid_fwd, mid_bwd = flat[0].astype(jnp.int32), flat[2].astype(jnp.int32)
     moves = []
     for y in range(4):
         moves.append((y * 2 + 1, ((y + 1) % 4) * 2 + 1))
         moves.append((y * 2, ((y + 3) % 4) * 2))
     along_y = lax.ppermute(along_y, PP, moves)
+    flat, along_y = lax.optimization_barrier((flat, along_y))
+    flat = lax.ppermute(flat, "zh", [(0, 1), (1, 0)])
+    mid_fwd, mid_bwd = flat[0].astype(jnp.int32), flat[2].astype(jnp.int32)
     fwd_rows = jnp.where(is_high, along_y, carried[0])
     cot_rows = jnp.where(is_high, grads_prev[0], along_y)
 
@@ -154,7 +154,9 @@
         both = jnp.concatenate(
             [jnp.where(is_high, cross, own), jnp.where(is_high, own, cross)], axis=0
         ).reshape(2 * EXPERTS, DEPTH, features + LANES)
-        got = lax.all_to_all(both, Z16, split_axis=0, concat_axis=0, tiled=True)
+        return lax.all_to_all(both, Z16, split_axis=0, concat_axis=0, tiled=True)
+
+    def sides(got):
         got = got.reshape(2, ROWS, features + LANES)
         return jnp.where(is_high, got[1], got[0]), jnp.where(is_high, got[0], got[1])
 
@@ -166,30 +168,36 @@
 
     home_bwd = slot_matrix(own_bwd)
     send_saved = jnp.pad(reorder(home_bwd, saved[0]), ((0, 0), (0, LANES)))
+    send_fwd = reorder(
+        slot_matrix(mid_fwd), jnp.concatenate([fwd_rows, gate_lanes(flat[1])], axis=1)
+    )
+    got_saved, got_fwd = sides(dispatch(send_saved, send_fwd))
+    blocks = weights_along_z(blocks)
     send_cot = reorder(
         slot_matrix(mid_bwd), jnp.concatenate([cot_rows, gate_lanes(flat[3])], axis=1)
     )
-    got_saved, got_cot = dispatch(send_saved, send_cot)
-    blocks = weights_along_z(blocks)
-    send_fwd = reorder(
-        slot_matrix(mid_fwd), jnp.concatenate([fwd_rows, gate_lanes(flat[1])], axis=1)
-    )
-    send_fwd, blocks = lax.optimization_barrier((send_fwd, blocks))
-    _, got_fwd = dispatch(jnp.zeros_like(send_fwd), send_fwd)
-
+    got_cot = dispatch(jnp.zeros_like(send_cot), send_cot)
+    gate_weights, up_weights, down_weights = weights_of_chip(blocks)
+
+    section_input = got_fwd[:, :features]
+    normed_fwd, _ = normalize(section_input)
+    parts = expert_out(
+        gather_x(normed_fwd.astype(jnp.bfloat16)), gate_weights, up_weights, down_weights
+    )
     normed_bwd, scale_bwd = normalize(got_saved[:, :features])
+    all_normed = gather_x(normed_bwd.astype(jnp.bfloat16))
+    mixed = scatter_sum_x(parts)
+    mixed, all_normed, got_cot = lax.optimization_barrier((mixed, all_normed, got_cot))
+    _, got_cot = sides(got_cot)
+    mixture = gate_of(got_fwd[:, features:]) * mixed
+    acts = (section_input.astype(jnp.float32) + mixture).astype(jnp.bfloat16)
+    output_act = reorder(slot_matrix(own_fwd).T, give_back(acts))
+
     cotangent = got_cot[:, :features].astype(jnp.float32)
     gated = (gate_of(got_cot[:, features:]) * cotangent).astype(jnp.bfloat16)
-    gathered = [
-        rows.reshape(2, ROWS, features)
-        for rows in gather_x(jnp.concatenate([normed_bwd.astype(jnp.bfloat16), gated], axis=0))
-    ]
-    all_normed = jnp.concatenate([rows[0] for rows in gathered], axis=0)
-    all_gated = jnp.concatenate([rows[1] for rows in gathered], axis=0)
-    gate_weights, up_weights, down_weights = weights_of_chip(blocks)
     parts = expert_grad(
         all_normed,
-        all_gated,
+        gather_x(gated),
         gate_weights,
         up_weights,
         down_weights,
@@ -198,16 +206,6 @@
     projection = jnp.mean(normed_bwd * summed, axis=-1, keepdims=True)
     grads = (cotangent + scale_bwd * (summed - normed_bwd * projection)).astype(jnp.bfloat16)
     output_grad = reorder(home_bwd.T, give_back(grads))
-
-    section_input = got_fwd[:, :features]
-    normed_fwd, _ = normalize(section_input)
-    parts = expert_out(
-        jnp.concatenate(gather_x(normed_fwd.astype(jnp.bfloat16)), axis=0),
-        gate_weights, up_weights, down_weights
-    )
-    mixture = gate_of(got_fwd[:, features:]) * scatter_sum_x(parts)
-    acts = (section_input.astype(jnp.float32) + mixture).astype(jnp.bfloat16)
-    output_act = reorder(slot_matrix(own_fwd).T, give_back(acts))
     return (output_act[None], output_grad[None])
 
 

time: 379 us -> 374 us (0.987); the launches traced: 372 us -> 372 us
  starting transfers between devices: 115 us -> 139 us
  waiting for transfers between devices: 188 us -> 167 us
    ppermute x18 -> x21, waiting for transfers between devices: 145 us -> 119 us  [rotated(): lax.ppermute(x, axis, [(i, (i + by) % length) for i in range(length)])]
    all_to_all x2, waiting for transfers between devices: 19.6 us -> 0.01 us  [dispatch(): return lax.all_to_all(both, Z16, split_axis=0, concat_axis=0, tiled=True)]
    all_to_all x2, starting transfers between devices: 18.9 us -> 34.6 us  [dispatch(): return lax.all_to_all(both, Z16, split_axis=0, concat_axis=0, tiled=True)]
    ppermute x18 -> x21, starting transfers between devices: 56.4 us -> 70.9 us  [rotated(): lax.ppermute(x, axis, [(i, (i + by) % length) for i in range(length)])]
    all_to_all x2, waiting for transfers between devices: 23.7 us -> 36.6 us  [give_back(): lax.all_to_all(rows.reshape(EXPERTS, DEPTH, features), Z8, split_axis=0,...]
    ppermute x1, waiting for transfers between devices: 0.01 us -> 10.7 us  [body(): along_y = lax.ppermute(along_y, PP, moves)]
    all_to_all x2, starting transfers between devices: 19.1 us -> 14.1 us  [give_back(): lax.all_to_all(rows.reshape(EXPERTS, DEPTH, features), Z8, split_axis=0,...]
    unnamed x32 -> x48, local copies, waits for them, and re-layouts: 8.82 us -> 9.93 us
  transfers between devices with their start and end apart: 25 -> 28, of which waited for: 14 -> 14; matrix products, arithmetic and copies ran while one was open for 16% -> 11% of each run, Pallas kernels for 0% -> 0%
where the time goes in v2:
time: 374 us; the launch traced here: 372 us
  waiting for transfers between devices  167 us (45%)
  starting transfers between devices  139 us (37%)
  matrix products  27.3 us (7%)
  other arithmetic  19.9 us (5%)
  local copies, waits for them, and re-layouts  17.5 us (5%)
    ppermute x21, waiting for transfers between devices, rotated(): lax.ppermute(x, axis, [(i, (i + by) % length) for i in range(length)])  119 us
    ppermute x21, starting transfers between devices, rotated(): lax.ppermute(x, axis, [(i, (i + by) % length) for i in range(length)])  70.9 us
    all_to_all x2, waiting for transfers between devices, give_back(): lax.all_to_all(rows.reshape(EXPERTS, DEPTH, features), Z8, split_axis=0,...  36.6 us
    all_to_all x2, starting transfers between devices, dispatch(): return lax.all_to_all(both, Z16, split_axis=0, concat_axis=0, tiled=True)  34.6 us
    ppermute x1, starting transfers between devices, body(): flat = lax.ppermute(flat, 'zh', [(0, 1), (1, 0)])  14.5 us
    all_to_all x2, starting transfers between devices, give_back(): lax.all_to_all(rows.reshape(EXPERTS, DEPTH, features), Z8, split_axis=0,...  14.1 us
    ppermute x1, waiting for transfers between devices, body(): along_y = lax.ppermute(along_y, PP, moves)  10.7 us
    unnamed x48, local copies, waits for them, and re-layouts  9.93 us
  transfers between devices with their start and end apart: 28, of which 14 were waited for; matrix products, arithmetic and copies ran while one was open for 11% of the time, Pallas kernels for 0%

profile of v2, /device:TPU:24, one launch (start us, length us, event | category | flops | bytes accessed | tf_op | source)
XLA Modules:
  0.0 371.7 jit_solution(7282753643777332313)
XLA Ops:
  5.5 4.7 %collective-permute-start.7 = (bf16[3,32,3584]{2,1,0:T(8,128)(2,1)}, bf16[3,32,3584]{2,1,0:T(8,128)(2,1)}, u32[]{:S(2)}, u32[]{:S(2)}) collective-permute-start(bf16[3,32,3584]{2,1,0:T(8,128)(2,1)} %get-tuple-element.18), channel_id=1, source_target_pairs={{0,48},{16,0},{32,16},{48,32},{1,49},{17,1},{33,17},{49,33},{2,50}... | collective-permute-start | bytes 2064392 | tf_op jit(solution)/shard_map/ppermute | solution.py:58
  20.6 10.7 %collective-permute-done = bf16[64,3584]{1,0:T(8,128)(2,1)S(1)} collective-permute-done((bf16[64,3584]{1,0:T(8,128)(2,1)}, bf16[64,3584]{1,0:T(8,128)(2,1)S(1)}, u32[]{:S(2)}, u32[]{:S(2)}) %collective-permute-start) | collective-permute-done | bytes 458784 | tf_op jit(solution)/shard_map/ppermute | solution.py:144
  31.3 14.5 %collective-permute-start.1 = (f32[4,64]{1,0:T(4,128)S(1)}, f32[4,64]{1,0:T(4,128)S(1)}, u32[]{:S(2)}, u32[]{:S(2)}) collective-permute-start(f32[4,64]{1,0:T(4,128)S(1)} %pad_maximum_fusion.11), channel_id=1, source_target_pairs={{0,64},{64,0},{1,65},{65,1},{2,66},{66,2},{3,67},{67,3},{4,68},{68... | collective-permute-start | bytes 3080 | tf_op jit(solution)/shard_map/ppermute | solution.py:146
  50.4 12.1 %all-to-all-start = ((bf16[16,8,3712]{2,1,0:T(8,128)(2,1)}), bf16[16,8,3712]{2,1,0:T(8,128)(2,1)S(1)}, u32[]{:S(2)}, u32[]{:S(2)}) async-start(bf16[16,8,3712]{2,1,0:T(8,128)(2,1)} %maximum_bitcast_fusion), calls=%async_computation | async-start | bytes 1900544 | tf_op jit(solution)/shard_map/all_to_all | solution.py:157
  64.9 3.8 %collective-permute-start.8 = (bf16[3,32,3584]{2,1,0:T(8,128)(2,1)S(1)}, bf16[3,32,3584]{2,1,0:T(8,128)(2,1)S(1)}, u32[]{:S(2)}, u32[]{:S(2)}) collective-permute-start(bf16[3,32,3584]{2,1,0:T(8,128)(2,1)S(1)} %get-tuple-element.16), channel_id=1, source_target_pairs={{0,2},{2,4},{4,6},{6,0},{1,3},{3,5},{5,7},{7,1},{8,10},{10,12},{12... | collective-permute-start | bytes 2064392 | tf_op jit(solution)/shard_map/ppermute | solution.py:58
  68.7 4.3 %collective-permute-start.9 = (bf16[3,32,3584]{2,1,0:T(8,128)(2,1)S(1)}, bf16[3,32,3584]{2,1,0:T(8,128)(2,1)S(1)}, u32[]{:S(2)}, u32[]{:S(2)}) collective-permute-start(bf16[3,32,3584]{2,1,0:T(8,128)(2,1)S(1)} %get-tuple-element.15), channel_id=1, source_target_pairs={{0,4},{2,6},{4,0},{6,2},{1,5},{3,7},{5,1},{7,3},{8,12},{10,14},{12... | collective-permute-start | bytes 2064392 | tf_op jit(solution)/shard_map/ppermute | solution.py:58
  73.0 3.4 collective-permute-start.10
  78.4 43.2 %collective-permute-done.8 = bf16[3,32,3584]{2,1,0:T(8,128)(2,1)S(1)} collective-permute-done((bf16[3,32,3584]{2,1,0:T(8,128)(2,1)S(1)}, bf16[3,32,3584]{2,1,0:T(8,128)(2,1)S(1)}, u32[]{:S(2)}, u32[]{:S(2)}) %collective-permute-start.8) | collective-permute-done | bytes 688160 | tf_op jit(solution)/shard_map/ppermute | solution.py:58
  121.6 27.5 %collective-permute-done.9 = bf16[3,32,3584]{2,1,0:T(8,128)(2,1)S(1)} collective-permute-done((bf16[3,32,3584]{2,1,0:T(8,128)(2,1)S(1)}, bf16[3,32,3584]{2,1,0:T(8,128)(2,1)S(1)}, u32[]{:S(2)}, u32[]{:S(2)}) %collective-permute-start.9) | collective-permute-done | bytes 688160 | tf_op jit(solution)/shard_map/ppermute | solution.py:58
  155.5 22.5 %all-to-all-start.1 = ((bf16[16,8,3712]{2,1,0:T(8,128)(2,1)}), bf16[16,8,3712]{2,1,0:T(8,128)(2,1)}, u32[]{:S(2)}, u32[]{:S(2)}) async-start(bf16[16,8,3712]{2,1,0:T(8,128)(2,1)} %maximum_bitcast_fusion.1), calls=%async_computation.1 | async-start | bytes 1900544 | tf_op jit(solution)/shard_map/all_to_all | solution.py:157
  178.5 4.3 %collective-permute-start.4 = (bf16[64,3584]{1,0:T(8,128)(2,1)S(1)}, bf16[64,3584]{1,0:T(8,128)(2,1)S(1)}, u32[]{:S(2)}, u32[]{:S(2)}) collective-permute-start(bf16[64,3584]{1,0:T(8,128)(2,1)S(1)} %fusion.32), channel_id=1, source_target_pairs={{0,48},{16,0},{32,16},{48,32},{1,49},{17,1},{33,17},{49,33},{2,50}... | collective-permute-start | bytes 1376264 | tf_op jit(solution)/shard_map/ppermute | solution.py:58
  182.8 3.4 collective-permute-start.3
  188.5 5.1 %collective-permute-start.17 = (bf16[64,3584]{1,0:T(8,128)(2,1)S(1)}, bf16[64,3584]{1,0:T(8,128)(2,1)S(1)}, u32[]{:S(2)}, u32[]{:S(2)}) collective-permute-start(bf16[64,3584]{1,0:T(8,128)(2,1)S(1)} %fusion.22), channel_id=1, source_target_pairs={{0,48},{16,0},{32,16},{48,32},{1,49},{17,1},{33,17},{49,33},{2,50}... | collective-permute-start | bytes 1376264 | tf_op jit(solution)/shard_map/ppermute | solution.py:58
  196.4 3.5 constant_dynamic-update-slice_fusion
  199.8 3.5 collective-permute-done.4
  203.3 3.5 collective-permute-start.15
  212.5 5.8 %convolution_convert_fusion = bf16[256,3584]{1,0:T(8,128)(2,1)} fusion(bf16[3,256,3584]{2,1,0:T(8,128)(2,1)} %constant_dynamic-update-slice_fusion, f32[256,256]{1,0:T(8,128)S(1)} %fusion.12, bf16[64,3584]{1,0:T(8,128)(2,1)} %copy-done.17, bf16[64,3584]{1,0:T(8,128)(2,1)} %copy-done.18, bf16[64,3584]{1,0:T(8,128)(2,1)} %copy-done.19, ...), kind=kOutput, calls=%fused_computation.2 | convolution fusion | flops 948174848 | bytes 7602176 | tf_op jit(solution)/shard_map/dot_general | solution.py:82
  221.7 3.9 %collective-permute-start.13 = (bf16[64,3584]{1,0:T(8,128)(2,1)S(1)}, bf16[64,3584]{1,0:T(8,128)(2,1)S(1)}, u32[]{:S(2)}, u32[]{:S(2)}) collective-permute-start(bf16[64,3584]{1,0:T(8,128)(2,1)S(1)} %get-tuple-element.26), channel_id=1, source_target_pairs={{0,32},{16,48},{32,0},{48,16},{1,33},{17,49},{33,1},{49,17},{2,34}... | collective-permute-start | bytes 1376264 | tf_op jit(solution)/shard_map/ppermute | solution.py:58
  225.6 4.4 %collective-permute-start.12 = (bf16[64,3584]{1,0:T(8,128)(2,1)S(1)}, bf16[64,3584]{1,0:T(8,128)(2,1)S(1)}, u32[]{:S(2)}, u32[]{:S(2)}) collective-permute-start(bf16[64,3584]{1,0:T(8,128)(2,1)S(1)} %get-tuple-element.24), channel_id=1, source_target_pairs={{0,48},{16,0},{32,16},{48,32},{1,49},{17,1},{33,17},{49,33},{2,50}... | collective-permute-start | bytes 1376264 | tf_op jit(solution)/shard_map/ppermute | solution.py:58
  232.2 6.6 %collective-permute-done.14 = bf16[64,3584]{1,0:T(8,128)(2,1)S(1)} collective-permute-done((bf16[64,3584]{1,0:T(8,128)(2,1)S(1)}, bf16[64,3584]{1,0:T(8,128)(2,1)S(1)}, u32[]{:S(2)}, u32[]{:S(2)}) %collective-permute-start.14) | collective-permute-done | bytes 458784 | tf_op jit(solution)/shard_map/ppermute | solution.py:58
  238.8 9.0 %collective-permute-done.13 = bf16[64,3584]{1,0:T(8,128)(2,1)S(1)} collective-permute-done((bf16[64,3584]{1,0:T(8,128)(2,1)S(1)}, bf16[64,3584]{1,0:T(8,128)(2,1)S(1)}, u32[]{:S(2)}, u32[]{:S(2)}) %collective-permute-start.13) | collective-permute-done | bytes 458784 | tf_op jit(solution)/shard_map/ppermute | solution.py:58
  252.1 4.3 %collective-permute-start.20 = (bf16[64,3584]{1,0:T(8,128)(2,1)S(1)}, bf16[64,3584]{1,0:T(8,128)(2,1)S(1)}, u32[]{:S(2)}, u32[]{:S(2)}) collective-permute-start(bf16[64,3584]{1,0:T(8,128)(2,1)S(1)} %fusion.29), channel_id=1, source_target_pairs={{0,48},{16,0},{32,16},{48,32},{1,49},{17,1},{33,17},{49,33},{2,50}... | collective-permute-start | bytes 1376264 | tf_op jit(solution)/shard_map/ppermute | solution.py:58
  263.7 12.5 %collective-permute-done.20 = bf16[64,3584]{1,0:T(8,128)(2,1)S(1)} collective-permute-done((bf16[64,3584]{1,0:T(8,128)(2,1)S(1)}, bf16[64,3584]{1,0:T(8,128)(2,1)S(1)}, u32[]{:S(2)}, u32[]{:S(2)}) %collective-permute-start.20) | collective-permute-done | bytes 458784 | tf_op jit(solution)/shard_map/ppermute | solution.py:58
  276.2 5.6 %collective-permute-done.18 = bf16[64,3584]{1,0:T(8,128)(2,1)S(1)} collective-permute-done((bf16[64,3584]{1,0:T(8,128)(2,1)S(1)}, bf16[64,3584]{1,0:T(8,128)(2,1)S(1)}, u32[]{:S(2)}, u32[]{:S(2)}) %collective-permute-start.18) | collective-permute-done | bytes 458784 | tf_op jit(solution)/shard_map/ppermute | solution.py:58
  284.7 4.0 %fusion.13 = f32[256,3584]{1,0:T(8,128)} fusion(bf16[3,256,3584]{2,1,0:T(8,128)(2,1)} %constant_dynamic-update-slice_fusion, f32[256,256]{1,0:T(8,128)S(1)} %fusion.3, f32[256,256]{1,0:T(8,128)S(1)} %fusion.11), kind=kOutput, calls=%fused_computation.28 | convolution fusion | flops 470155264 | bytes 6029312 | tf_op jit(solution)/shard_map/dot_general | solution.py:94
  288.7 5.9 %fusion = bf16[256,3584]{1,0:T(8,128)(2,1)S(1)} fusion(f32[256,3584]{1,0:T(8,128)} %fusion.13, bf16[3,256,3584]{2,1,0:T(8,128)(2,1)} %constant_dynamic-update-slice_fusion, f32[256,256]{1,0:T(8,128)} %copy-done.8, bf16[256,3584]{1,0:T(8,128)(2,1)} %copy-done.1, f32[256,256]{1,0:T(8,128)S(1)} %fusion.11), kind=kOutput, calls=%fused_computation.1 | convolution fusion | flops 942014464 | bytes 11534336 | tf_op jit(solution)/shard_map/dot_general | solution.py:94
  297.7 4.0 %collective-permute-start.22 = (bf16[64,3584]{1,0:T(8,128)(2,1)}, bf16[64,3584]{1,0:T(8,128)(2,1)}, u32[]{:S(2)}, u32[]{:S(2)}) collective-permute-start(bf16[64,3584]{1,0:T(8,128)(2,1)} %get-tuple-element.23), channel_id=1, source_target_pairs={{0,32},{16,48},{32,0},{48,16},{1,33},{17,49},{33,1},{49,17},{2,34}... | collective-permute-start | bytes 1376264 | tf_op jit(solution)/shard_map/ppermute | solution.py:58
  305.7 9.8 %all-to-all-start.2 = ((bf16[8,8,3584]{2,1,0:T(8,128)(2,1)}), bf16[8,8,3584]{2,1,0:T(8,128)(2,1)S(1)}, u32[]{:S(2)}, u32[]{:S(2)}) async-start(bf16[8,8,3584]{2,1,0:T(8,128)(2,1)} %fusion.44), calls=%async_computation.2 | async-start | bytes 917504 | tf_op jit(solution)/shard_map/all_to_all | solution.py:164
  315.5 5.9 %collective-permute-done.23 = bf16[64,3584]{1,0:T(8,128)(2,1)} collective-permute-done((bf16[64,3584]{1,0:T(8,128)(2,1)}, bf16[64,3584]{1,0:T(8,128)(2,1)}, u32[]{:S(2)}, u32[]{:S(2)}) %collective-permute-start.23) | collective-permute-done | bytes 458784 | tf_op jit(solution)/shard_map/ppermute | solution.py:58
  328.4 12.7 %all-to-all-done.2 = bf16[8,8,3584]{2,1,0:T(8,128)(2,1)S(1)} async-done(((bf16[8,8,3584]{2,1,0:T(8,128)(2,1)}), bf16[8,8,3584]{2,1,0:T(8,128)(2,1)S(1)}, u32[]{:S(2)}, u32[]{:S(2)}) %all-to-all-start.2) | async-done | bytes 458784 | tf_op jit(solution)/shard_map/all_to_all | solution.py:164
  341.1 4.3 %all-to-all-start.3 = ((bf16[8,8,3584]{2,1,0:T(8,128)(2,1)}), bf16[8,8,3584]{2,1,0:T(8,128)(2,1)S(1)}, u32[]{:S(2)}, u32[]{:S(2)}) async-start(bf16[8,8,3584]{2,1,0:T(8,128)(2,1)} %fusion.45), calls=%async_computation.3 | async-start | bytes 917504 | tf_op jit(solution)/shard_map/all_to_all | solution.py:164
  346.6 23.9 %all-to-all-done.3 = bf16[8,8,3584]{2,1,0:T(8,128)(2,1)S(1)} async-done(((bf16[8,8,3584]{2,1,0:T(8,128)(2,1)}), bf16[8,8,3584]{2,1,0:T(8,128)(2,1)S(1)}, u32[]{:S(2)}, u32[]{:S(2)}) %all-to-all-start.3) | async-done | bytes 458784 | tf_op jit(solution)/shard_map/all_to_all | solution.py:164
  (128 shorter events, 77.7 us)
Async XLA Ops:
  0.6 18.9 %copy-start = (bf16[1,64,3584]{2,1,0:T(8,128)(2,1)S(1)}, bf16[1,64,3584]{2,1,0:T(8,128)(2,1)}, u32[]{:S(2)}) copy-start(bf16[1,64,3584]{2,1,0:T(8,128)(2,1)} %param.11) | copy-start | bytes 1376260
  4.1 15.4 %copy-start.15 = (f32[1,64,1]{1,2,0:T(1,128)S(1)}, f32[1,64,1]{1,2,0:T(1,128)}, u32[]{:S(2)}) copy-start(f32[1,64,1]{1,2,0:T(1,128)} %param.16) | copy-start | bytes 772
  4.1 15.4 %copy-start.16 = (f32[1,64,1]{1,2,0:T(1,128)S(1)}, f32[1,64,1]{1,2,0:T(1,128)}, u32[]{:S(2)}) copy-start(f32[1,64,1]{1,2,0:T(1,128)} %param.14) | copy-start | bytes 772
  5.5 57.4 %collective-permute-start.7 = (bf16[3,32,3584]{2,1,0:T(8,128)(2,1)}, bf16[3,32,3584]{2,1,0:T(8,128)(2,1)}, u32[]{:S(2)}, u32[]{:S(2)}) collective-permute-start(bf16[3,32,3584]{2,1,0:T(8,128)(2,1)} %get-tuple-element.18), channel_id=1, source_target_pairs={{0,48},{16,0},{32,16},{48,32},{1,49},{17,1},{33,17},{49,33},{2,50}... | collective-permute-start | bytes 2064392 | tf_op jit(solution)/shard_map/ppermute | solution.py:58
  10.2 52.8 %collective-permute-start.6 = (bf16[3,32,3584]{2,1,0:T(8,128)(2,1)}, bf16[3,32,3584]{2,1,0:T(8,128)(2,1)}, u32[]{:S(2)}, u32[]{:S(2)}) collective-permute-start(bf16[3,32,3584]{2,1,0:T(8,128)(2,1)} %get-tuple-element.19), channel_id=1, source_target_pairs={{0,32},{16,48},{32,0},{48,16},{1,33},{17,49},{33,1},{49,17},{2,34}... | collective-permute-start | bytes 2064392 | tf_op jit(solution)/shard_map/ppermute | solution.py:58
  12.9 50.1 %collective-permute-start.5 = (bf16[3,32,3584]{2,1,0:T(8,128)(2,1)S(1)}, bf16[3,32,3584]{2,1,0:T(8,128)(2,1)}, u32[]{:S(2)}, u32[]{:S(2)}) collective-permute-start(bf16[3,32,3584]{2,1,0:T(8,128)(2,1)S(1)} %get-tuple-element.20), channel_id=1, source_target_pairs={{0,16},{16,32},{32,48},{48,0},{1,17},{17,33},{33,49},{49,1},{2,18}... | collective-permute-start | bytes 2064392 | tf_op jit(solution)/shard_map/ppermute | solution.py:58
  16.5 14.7 %collective-permute-start = (bf16[64,3584]{1,0:T(8,128)(2,1)}, bf16[64,3584]{1,0:T(8,128)(2,1)S(1)}, u32[]{:S(2)}, u32[]{:S(2)}) collective-permute-start(bf16[64,3584]{1,0:T(8,128)(2,1)} %bitcast_select_fusion.1), channel_id=1, source_target_pairs={{64,192},{0,384},{192,320},{128,0},{320,448},{256,128},{448,64},{3... | collective-permute-start | bytes 1376264 | tf_op jit(solution)/shard_map/ppermute | solution.py:144
  31.3 16.1 %collective-permute-start.1 = (f32[4,64]{1,0:T(4,128)S(1)}, f32[4,64]{1,0:T(4,128)S(1)}, u32[]{:S(2)}, u32[]{:S(2)}) collective-permute-start(f32[4,64]{1,0:T(4,128)S(1)} %pad_maximum_fusion.11), channel_id=1, source_target_pairs={{0,64},{64,0},{1,65},{65,1},{2,66},{66,2},{3,67},{67,3},{4,68},{68... | collective-permute-start | bytes 3080 | tf_op jit(solution)/shard_map/ppermute | solution.py:146
  50.4 105.1 %all-to-all-start = ((bf16[16,8,3712]{2,1,0:T(8,128)(2,1)}), bf16[16,8,3712]{2,1,0:T(8,128)(2,1)S(1)}, u32[]{:S(2)}, u32[]{:S(2)}) async-start(bf16[16,8,3712]{2,1,0:T(8,128)(2,1)} %maximum_bitcast_fusion), calls=%async_computation | async-start | bytes 1900544 | tf_op jit(solution)/shard_map/all_to_all | solution.py:157
  64.9 56.7 %collective-permute-start.8 = (bf16[3,32,3584]{2,1,0:T(8,128)(2,1)S(1)}, bf16[3,32,3584]{2,1,0:T(8,128)(2,1)S(1)}, u32[]{:S(2)}, u32[]{:S(2)}) collective-permute-start(bf16[3,32,3584]{2,1,0:T(8,128)(2,1)S(1)} %get-tuple-element.16), channel_id=1, source_target_pairs={{0,2},{2,4},{4,6},{6,0},{1,3},{3,5},{5,7},{7,1},{8,10},{10,12},{12... | collective-permute-start | bytes 2064392 | tf_op jit(solution)/shard_map/ppermute | solution.py:58
  68.7 80.3 %collective-permute-start.9 = (bf16[3,32,3584]{2,1,0:T(8,128)(2,1)S(1)}, bf16[3,32,3584]{2,1,0:T(8,128)(2,1)S(1)}, u32[]{:S(2)}, u32[]{:S(2)}) collective-permute-start(bf16[3,32,3584]{2,1,0:T(8,128)(2,1)S(1)} %get-tuple-element.15), channel_id=1, source_target_pairs={{0,4},{2,6},{4,0},{6,2},{1,5},{3,7},{5,1},{7,3},{8,12},{10,14},{12... | collective-permute-start | bytes 2064392 | tf_op jit(solution)/shard_map/ppermute | solution.py:58
  73.0 76.1 %collective-permute-start.10 = (bf16[3,32,3584]{2,1,0:T(8,128)(2,1)S(1)}, bf16[3,32,3584]{2,1,0:T(8,128)(2,1)S(1)}, u32[]{:S(2)}, u32[]{:S(2)}) collective-permute-start(bf16[3,32,3584]{2,1,0:T(8,128)(2,1)S(1)} %get-tuple-element.14), channel_id=1, source_target_pairs={{0,6},{2,0},{4,2},{6,4},{1,7},{3,1},{5,3},{7,5},{8,14},{10,8},{12,... | collective-permute-start | bytes 2064392 | tf_op jit(solution)/shard_map/ppermute | solution.py:58
  150.8 42.9 %collective-permute-start.11 = (bf16[3,128,3584]{2,1,0:T(8,128)(2,1)}, bf16[3,128,3584]{2,1,0:T(8,128)(2,1)}, u32[]{:S(2)}, u32[]{:S(2)}) collective-permute-start(bf16[3,128,3584]{2,1,0:T(8,128)(2,1)} %pad_maximum_fusion.2), channel_id=1, source_target_pairs={{0,1},{1,0},{2,3},{3,2},{4,5},{5,4},{6,7},{7,6},{8,9},{9,8},{10,11... | collective-permute-start | bytes 8257544 | tf_op jit(solution)/shard_map/ppermute | solution.py:124
  155.5 94.4 %all-to-all-start.1 = ((bf16[16,8,3712]{2,1,0:T(8,128)(2,1)}), bf16[16,8,3712]{2,1,0:T(8,128)(2,1)}, u32[]{:S(2)}, u32[]{:S(2)}) async-start(bf16[16,8,3712]{2,1,0:T(8,128)(2,1)} %maximum_bitcast_fusion.1), calls=%async_computation.1 | async-start | bytes 1900544 | tf_op jit(solution)/shard_map/all_to_all | solution.py:157
  178.5 24.8 %collective-permute-start.4 = (bf16[64,3584]{1,0:T(8,128)(2,1)S(1)}, bf16[64,3584]{1,0:T(8,128)(2,1)S(1)}, u32[]{:S(2)}, u32[]{:S(2)}) collective-permute-start(bf16[64,3584]{1,0:T(8,128)(2,1)S(1)} %fusion.32), channel_id=1, source_target_pairs={{0,48},{16,0},{32,16},{48,32},{1,49},{17,1},{33,17},{49,33},{2,50}... | collective-permute-start | bytes 1376264 | tf_op jit(solution)/shard_map/ppermute | solution.py:58
  182.8 24.1 %collective-permute-start.3 = (bf16[64,3584]{1,0:T(8,128)(2,1)S(1)}, bf16[64,3584]{1,0:T(8,128)(2,1)S(1)}, u32[]{:S(2)}, u32[]{:S(2)}) collective-permute-start(bf16[64,3584]{1,0:T(8,128)(2,1)S(1)} %fusion.32), channel_id=1, source_target_pairs={{0,32},{16,48},{32,0},{48,16},{1,33},{17,49},{33,1},{49,17},{2,34}... | collective-permute-start | bytes 1376264 | tf_op jit(solution)/shard_map/ppermute | solution.py:58
  186.2 23.3 %collective-permute-start.2 = (bf16[64,3584]{1,0:T(8,128)(2,1)S(1)}, bf16[64,3584]{1,0:T(8,128)(2,1)S(1)}, u32[]{:S(2)}, u32[]{:S(2)}) collective-permute-start(bf16[64,3584]{1,0:T(8,128)(2,1)S(1)} %fusion.32), channel_id=1, source_target_pairs={{0,16},{16,32},{32,48},{48,0},{1,17},{17,33},{33,49},{49,1},{2,18}... | collective-permute-start | bytes 1376264 | tf_op jit(solution)/shard_map/ppermute | solution.py:58
  188.5 37.1 %collective-permute-start.17 = (bf16[64,3584]{1,0:T(8,128)(2,1)S(1)}, bf16[64,3584]{1,0:T(8,128)(2,1)S(1)}, u32[]{:S(2)}, u32[]{:S(2)}) collective-permute-start(bf16[64,3584]{1,0:T(8,128)(2,1)S(1)} %fusion.22), channel_id=1, source_target_pairs={{0,48},{16,0},{32,16},{48,32},{1,49},{17,1},{33,17},{49,33},{2,50}... | collective-permute-start | bytes 1376264 | tf_op jit(solution)/shard_map/ppermute | solution.py:58
  193.7 36.3 %collective-permute-start.16 = (bf16[64,3584]{1,0:T(8,128)(2,1)S(1)}, bf16[64,3584]{1,0:T(8,128)(2,1)S(1)}, u32[]{:S(2)}, u32[]{:S(2)}) collective-permute-start(bf16[64,3584]{1,0:T(8,128)(2,1)S(1)} %fusion.22), channel_id=1, source_target_pairs={{0,32},{16,48},{32,0},{48,16},{1,33},{17,49},{33,1},{49,17},{2,34}... | collective-permute-start | bytes 1376264 | tf_op jit(solution)/shard_map/ppermute | solution.py:58
  203.3 27.5 %collective-permute-start.15 = (bf16[64,3584]{1,0:T(8,128)(2,1)S(1)}, bf16[64,3584]{1,0:T(8,128)(2,1)}, u32[]{:S(2)}, u32[]{:S(2)}) collective-permute-start(bf16[64,3584]{1,0:T(8,128)(2,1)S(1)} %fusion.22), channel_id=1, source_target_pairs={{0,16},{16,32},{32,48},{48,0},{1,17},{17,33},{33,49},{49,1},{2,18}... | collective-permute-start | bytes 1376264 | tf_op jit(solution)/shard_map/ppermute | solution.py:58
  219.8 19.0 %collective-permute-start.14 = (bf16[64,3584]{1,0:T(8,128)(2,1)S(1)}, bf16[64,3584]{1,0:T(8,128)(2,1)S(1)}, u32[]{:S(2)}, u32[]{:S(2)}) collective-permute-start(bf16[64,3584]{1,0:T(8,128)(2,1)S(1)} %get-tuple-element.25), channel_id=1, source_target_pairs={{0,16},{16,32},{32,48},{48,0},{1,17},{17,33},{33,49},{49,1},{2,18}... | collective-permute-start | bytes 1376264 | tf_op jit(solution)/shard_map/ppermute | solution.py:58
  221.7 26.1 %collective-permute-start.13 = (bf16[64,3584]{1,0:T(8,128)(2,1)S(1)}, bf16[64,3584]{1,0:T(8,128)(2,1)S(1)}, u32[]{:S(2)}, u32[]{:S(2)}) collective-permute-start(bf16[64,3584]{1,0:T(8,128)(2,1)S(1)} %get-tuple-element.26), channel_id=1, source_target_pairs={{0,32},{16,48},{32,0},{48,16},{1,33},{17,49},{33,1},{49,17},{2,34}... | collective-permute-start | bytes 1376264 | tf_op jit(solution)/shard_map/ppermute | solution.py:58
  225.6 22.2 %collective-permute-start.12 = (bf16[64,3584]{1,0:T(8,128)(2,1)S(1)}, bf16[64,3584]{1,0:T(8,128)(2,1)S(1)}, u32[]{:S(2)}, u32[]{:S(2)}) collective-permute-start(bf16[64,3584]{1,0:T(8,128)(2,1)S(1)} %get-tuple-element.24), channel_id=1, source_target_pairs={{0,48},{16,0},{32,16},{48,32},{1,49},{17,1},{33,17},{49,33},{2,50}... | collective-permute-start | bytes 1376264 | tf_op jit(solution)/shard_map/ppermute | solution.py:58
  232.2 31.5 %copy-start.1 = (bf16[256,3584]{1,0:T(8,128)(2,1)}, bf16[256,3584]{1,0:T(8,128)(2,1)S(1)}, u32[]{:S(2)}) copy-start(bf16[256,3584]{1,0:T(8,128)(2,1)S(1)} %pad_maximum_fusion.4) | copy-start | bytes 5505028
  252.1 24.1 %collective-permute-start.20 = (bf16[64,3584]{1,0:T(8,128)(2,1)S(1)}, bf16[64,3584]{1,0:T(8,128)(2,1)S(1)}, u32[]{:S(2)}, u32[]{:S(2)}) collective-permute-start(bf16[64,3584]{1,0:T(8,128)(2,1)S(1)} %fusion.29), channel_id=1, source_target_pairs={{0,48},{16,0},{32,16},{48,32},{1,49},{17,1},{33,17},{49,33},{2,50}... | collective-permute-start | bytes 1376264 | tf_op jit(solution)/shard_map/ppermute | solution.py:58
  256.4 19.8 %collective-permute-start.19 = (bf16[64,3584]{1,0:T(8,128)(2,1)S(1)}, bf16[64,3584]{1,0:T(8,128)(2,1)S(1)}, u32[]{:S(2)}, u32[]{:S(2)}) collective-permute-start(bf16[64,3584]{1,0:T(8,128)(2,1)S(1)} %fusion.29), channel_id=1, source_target_pairs={{0,32},{16,48},{32,0},{48,16},{1,33},{17,49},{33,1},{49,17},{2,34}... | collective-permute-start | bytes 1376264 | tf_op jit(solution)/shard_map/ppermute | solution.py:58
  258.6 23.2 %collective-permute-start.18 = (bf16[64,3584]{1,0:T(8,128)(2,1)S(1)}, bf16[64,3584]{1,0:T(8,128)(2,1)S(1)}, u32[]{:S(2)}, u32[]{:S(2)}) collective-permute-start(bf16[64,3584]{1,0:T(8,128)(2,1)S(1)} %fusion.29), channel_id=1, source_target_pairs={{0,16},{16,32},{32,48},{48,0},{1,17},{17,33},{33,49},{49,1},{2,18}... | collective-permute-start | bytes 1376264 | tf_op jit(solution)/shard_map/ppermute | solution.py:58
  295.8 25.7 %collective-permute-start.23 = (bf16[64,3584]{1,0:T(8,128)(2,1)}, bf16[64,3584]{1,0:T(8,128)(2,1)}, u32[]{:S(2)}, u32[]{:S(2)}) collective-permute-start(bf16[64,3584]{1,0:T(8,128)(2,1)} %get-tuple-element.22), channel_id=1, source_target_pairs={{0,16},{16,32},{32,48},{48,0},{1,17},{17,33},{33,49},{49,1},{2,18}... | collective-permute-start | bytes 1376264 | tf_op jit(solution)/shard_map/ppermute | solution.py:58
  297.7 23.8 %collective-permute-start.22 = (bf16[64,3584]{1,0:T(8,128)(2,1)}, bf16[64,3584]{1,0:T(8,128)(2,1)}, u32[]{:S(2)}, u32[]{:S(2)}) collective-permute-start(bf16[64,3584]{1,0:T(8,128)(2,1)} %get-tuple-element.23), channel_id=1, source_target_pairs={{0,32},{16,48},{32,0},{48,16},{1,33},{17,49},{33,1},{49,17},{2,34}... | collective-permute-start | bytes 1376264 | tf_op jit(solution)/shard_map/ppermute | solution.py:58
  301.7 22.3 %collective-permute-start.21 = (bf16[64,3584]{1,0:T(8,128)(2,1)}, bf16[64,3584]{1,0:T(8,128)(2,1)}, u32[]{:S(2)}, u32[]{:S(2)}) collective-permute-start(bf16[64,3584]{1,0:T(8,128)(2,1)} %get-tuple-element.21), channel_id=1, source_target_pairs={{0,48},{16,0},{32,16},{48,32},{1,49},{17,1},{33,17},{49,33},{2,50}... | collective-permute-start | bytes 1376264 | tf_op jit(solution)/shard_map/ppermute | solution.py:58
  305.7 35.3 %all-to-all-start.2 = ((bf16[8,8,3584]{2,1,0:T(8,128)(2,1)}), bf16[8,8,3584]{2,1,0:T(8,128)(2,1)S(1)}, u32[]{:S(2)}, u32[]{:S(2)}) async-start(bf16[8,8,3584]{2,1,0:T(8,128)(2,1)} %fusion.44), calls=%async_computation.2 | async-start | bytes 917504 | tf_op jit(solution)/shard_map/all_to_all | solution.py:164
  341.1 29.5 %all-to-all-start.3 = ((bf16[8,8,3584]{2,1,0:T(8,128)(2,1)}), bf16[8,8,3584]{2,1,0:T(8,128)(2,1)S(1)}, u32[]{:S(2)}, u32[]{:S(2)}) async-start(bf16[8,8,3584]{2,1,0:T(8,128)(2,1)} %fusion.45), calls=%async_computation.3 | async-start | bytes 917504 | tf_op jit(solution)/shard_map/all_to_all | solution.py:164
  (16 other events, 125.3 us)

commit v3 on v2

--- a/solution.py
+++ b/solution.py
@@ -75,24 +75,22 @@
     return lax.dot_general(a, b, (((1,), (1,)), ((), ())), preferred_element_type=jnp.float32)
 
 
-def expert_out(rows, gate_weights, up_weights, down_weights):
-    gate_pre = nt(rows, gate_weights)
-    up_pre = nt(rows, up_weights)
+def expert_out(rows, gate_up, down):
+    gate_pre, up_pre = jnp.split(nt(rows, gate_up), 2, axis=1)
     hidden = (jax.nn.silu(gate_pre) * up_pre).astype(jnp.bfloat16)
-    return jnp.dot(hidden, down_weights, preferred_element_type=jnp.float32)
-
-
-def expert_grad(rows, cotangents, gate_weights, up_weights, down_weights):
-    gate_pre = nt(rows, gate_weights)
-    up_pre = nt(rows, up_weights)
-    hidden_grad = nt(cotangents, down_weights)
+    return jnp.dot(hidden, down, preferred_element_type=jnp.float32)
+
+
+def expert_grad(rows, cotangents, gate_up, down):
+    gate_pre, up_pre = jnp.split(nt(rows, gate_up), 2, axis=1)
+    hidden_grad = nt(cotangents, down)
     sigmoid_val = jax.nn.sigmoid(gate_pre)
     gate_grad = (
         hidden_grad * up_pre * sigmoid_val * (1.0 + gate_pre * (1.0 - sigmoid_val))
     ).astype(jnp.bfloat16)
     up_grad = (hidden_grad * jax.nn.silu(gate_pre)).astype(jnp.bfloat16)
-    return jnp.dot(gate_grad, gate_weights, preferred_element_type=jnp.float32) + jnp.dot(
-        up_grad, up_weights, preferred_element_type=jnp.float32
+    return jnp.dot(
+        jnp.concatenate([gate_grad, up_grad], axis=1), gate_up, preferred_element_type=jnp.float32
     )
 
 
@@ -105,17 +103,16 @@
     def piece(index):
         return lax.dynamic_index_in_dim(pieces, index, axis=1, keepdims=False)
 
-    along_x = jnp.stack(
-        [piece(x)] + [rotated(piece((x + k) % 4), "x", k) for k in (1, 2, 3)]
-    )
-
-    def block(index):
-        return lax.dynamic_index_in_dim(along_x, index % 4, axis=0, keepdims=False)
-
-    return [block(x - zr - m + 8) for m in range(4)]
-
-
-def weights_along_z(blocks):
+    return [piece(x)] + [rotated(piece((x + k) % 4), "x", k) for k in (1, 2, 3)]
+
+
+def weights_along_z(pieces):
+    x, zr = lax.axis_index("x"), lax.axis_index("zr")
+    along_x = jnp.stack(pieces)
+    blocks = [
+        lax.dynamic_index_in_dim(along_x, (x - zr - m + 8) % 4, axis=0, keepdims=False)
+        for m in range(4)
+    ]
     return blocks[:1] + [rotated(blocks[m], "zr", m) for m in (1, 2, 3)]
 
 
@@ -123,7 +120,7 @@
     mine = jnp.concatenate(blocks, axis=1)
     other = lax.ppermute(mine, "c", [(0, 1), (1, 0)])
     both = jnp.concatenate([mine, other], axis=1)
-    return both[0], both[1], both[2]
+    return both[:2].reshape(-1, both.shape[2]), both[2]
 
 
 def body(
@@ -142,7 +139,6 @@
         moves.append((y * 2 + 1, ((y + 1) % 4) * 2 + 1))
         moves.append((y * 2, ((y + 3) % 4) * 2))
     along_y = lax.ppermute(along_y, PP, moves)
-    flat, along_y = lax.optimization_barrier((flat, along_y))
     flat = lax.ppermute(flat, "zh", [(0, 1), (1, 0)])
     mid_fwd, mid_bwd = flat[0].astype(jnp.int32), flat[2].astype(jnp.int32)
     fwd_rows = jnp.where(is_high, along_y, carried[0])
@@ -161,51 +157,46 @@
         return jnp.where(is_high, got[1], got[0]), jnp.where(is_high, got[0], got[1])
 
     def give_back(rows):
-        got = lax.all_to_all(
-            rows.reshape(EXPERTS, DEPTH, features), Z8, split_axis=0, concat_axis=0, tiled=True
-        )
-        return got.reshape(ROWS, features)
+        rows = rows.reshape(EXPERTS, DEPTH, features)
+        return lax.all_to_all(rows, Z8, split_axis=0, concat_axis=0, tiled=True)
 
     home_bwd = slot_matrix(own_bwd)
     send_saved = jnp.pad(reorder(home_bwd, saved[0]), ((0, 0), (0, LANES)))
     send_fwd = reorder(
         slot_matrix(mid_fwd), jnp.concatenate([fwd_rows, gate_lanes(flat[1])], axis=1)
     )
-    got_saved, got_fwd = sides(dispatch(send_saved, send_fwd))
+    got_first = dispatch(send_saved, send_fwd)
+    got_first, blocks = lax.optimization_barrier((got_first, blocks))
+    got_saved, got_fwd = sides(got_first)
     blocks = weights_along_z(blocks)
     send_cot = reorder(
         slot_matrix(mid_bwd), jnp.concatenate([cot_rows, gate_lanes(flat[3])], axis=1)
     )
+    send_cot, blocks = lax.optimization_barrier((send_cot, blocks))
     got_cot = dispatch(jnp.zeros_like(send_cot), send_cot)
-    gate_weights, up_weights, down_weights = weights_of_chip(blocks)
+    gate_up, down = weights_of_chip(blocks)
 
     section_input = got_fwd[:, :features]
     normed_fwd, _ = normalize(section_input)
-    parts = expert_out(
-        gather_x(normed_fwd.astype(jnp.bfloat16)), gate_weights, up_weights, down_weights
-    )
+    parts = expert_out(gather_x(normed_fwd.astype(jnp.bfloat16)), gate_up, down)
     normed_bwd, scale_bwd = normalize(got_saved[:, :features])
     all_normed = gather_x(normed_bwd.astype(jnp.bfloat16))
     mixed = scatter_sum_x(parts)
     mixed, all_normed, got_cot = lax.optimization_barrier((mixed, all_normed, got_cot))
     _, got_cot = sides(got_cot)
+    cotangent = got_cot[:, :features].astype(jnp.float32)
+    gated = (gate_of(got_cot[:, features:]) * cotangent).astype(jnp.bfloat16)
+    mixed, gated = lax.optimization_barrier((mixed, gated))
     mixture = gate_of(got_fwd[:, features:]) * mixed
     acts = (section_input.astype(jnp.float32) + mixture).astype(jnp.bfloat16)
-    output_act = reorder(slot_matrix(own_fwd).T, give_back(acts))
-
-    cotangent = got_cot[:, :features].astype(jnp.float32)
-    gated = (gate_of(got_cot[:, features:]) * cotangent).astype(jnp.bfloat16)
-    parts = expert_grad(
-        all_normed,
-        gather_x(gated),
-        gate_weights,
-        up_weights,
-        down_weights,
-    )
+    got_acts = give_back(acts)
+    parts = expert_grad(all_normed, gather_x(gated), gate_up, down)
+    parts, got_acts = lax.optimization_barrier((parts, got_acts))
     summed = scatter_sum_x(parts)
     projection = jnp.mean(normed_bwd * summed, axis=-1, keepdims=True)
     grads = (cotangent + scale_bwd * (summed - normed_bwd * projection)).astype(jnp.bfloat16)
-    output_grad = reorder(home_bwd.T, give_back(grads))
+    output_grad = reorder(home_bwd.T, give_back(grads).reshape(ROWS, features))
+    output_act = reorder(slot_matrix(own_fwd).T, got_acts.reshape(ROWS, features))
     return (output_act[None], output_grad[None])
 
 

time: 374 us -> 332 us (0.89)
  waiting for transfers between devices: 167 us -> 145 us
  matrix products: 27.3 us -> 15.2 us
  local copies, waits for them, and re-layouts: 17.5 us -> 7.46 us
    dot_general x3 -> x2, matrix products: 15.8 us -> 1.78 us  [the longest x1 1.11 us: expert_grad(): jnp.dot(jnp.concatenate([gate_grad, up_grad], axis=1), gate_up, preferred...]
    all_to_all x2, waiting for transfers between devices: 36.6 us -> 22.7 us  [give_back(): return lax.all_to_all(rows, Z8, split_axis=0, concat_axis=0, tiled=True)]
    ppermute x21, waiting for transfers between devices: 119 us -> 109 us  [rotated(): lax.ppermute(x, axis, [(i, (i + by) % length) for i in range(length)])]
    all_to_all x2, starting transfers between devices: 34.6 us -> 27.9 us  [dispatch(): return lax.all_to_all(both, Z16, split_axis=0, concat_axis=0, tiled=True)]
    unnamed x48 -> x28, local copies, waits for them, and re-layouts: 9.93 us -> 3.45 us
    all_to_all x2, starting transfers between devices: 14.1 us -> 18.6 us  [give_back(): return lax.all_to_all(rows, Z8, split_axis=0, concat_axis=0, tiled=True)]
  transfers between devices with their start and end apart: 28 -> 28, of which waited for: 14 -> 17; matrix products, arithmetic and copies ran while one was open for 11% -> 10% of each run, Pallas kernels for 0% -> 0%
where the time goes in v3:
time: 332 us; the launch traced here: 329 us
  waiting for transfers between devices  145 us (44%)
  starting transfers between devices  139 us (42%)
  other arithmetic  21.6 us (7%)
  matrix products  15.2 us (5%)
  local copies, waits for them, and re-layouts  7.46 us (2%)
    ppermute x21, waiting for transfers between devices, rotated(): lax.ppermute(x, axis, [(i, (i + by) % length) for i in range(length)])  109 us
    ppermute x21, starting transfers between devices, rotated(): lax.ppermute(x, axis, [(i, (i + by) % length) for i in range(length)])  72 us
    all_to_all x2, starting transfers between devices, dispatch(): return lax.all_to_all(both, Z16, split_axis=0, concat_axis=0, tiled=True)  27.9 us
    all_to_all x2, waiting for transfers between devices, give_back(): return lax.all_to_all(rows, Z8, split_axis=0, concat_axis=0, tiled=True)  22.7 us
    all_to_all x2, starting transfers between devices, give_back(): return lax.all_to_all(rows, Z8, split_axis=0, concat_axis=0, tiled=True)  18.6 us
    ppermute x1, starting transfers between devices, body(): flat = lax.ppermute(flat, 'zh', [(0, 1), (1, 0)])  15.7 us
    ppermute x1, waiting for transfers between devices, body(): along_y = lax.ppermute(along_y, PP, moves)  9.99 us
    dot_general x3, matrix products, nt(): lax.dot_general(a, b, (((1,), (1,)), ((), ())), preferred_element_type=jn...  8.62 us
  transfers between devices with their start and end apart: 28, of which 17 were waited for; matrix products, arithmetic and copies ran while one was open for 10% of the time, Pallas kernels for 0%

profile of v3, /device:TPU:24, one launch (start us, length us, event | category | flops | bytes accessed | tf_op | source)
XLA Modules:
  0.0 329.3 jit_solution(8917879720194190135)
XLA Ops:
  2.1 15.7 %collective-permute-start = (f32[4,64]{1,0:T(4,128)S(1)}, f32[4,64]{1,0:T(4,128)S(1)}, u32[]{:S(2)}, u32[]{:S(2)}) collective-permute-start(f32[4,64]{1,0:T(4,128)S(1)} %pad_maximum_fusion.4), channel_id=1, source_target_pairs={{0,64},{64,0},{1,65},{65,1},{2,66},{66,2},{3,67},{67,3},{4,68},{68... | collective-permute-start | bytes 3080 | tf_op jit(solution)/shard_map/ppermute | solution.py:142
  24.1 10.0 %collective-permute-done.1 = bf16[64,3584]{1,0:T(8,128)(2,1)S(1)} collective-permute-done((bf16[64,3584]{1,0:T(8,128)(2,1)S(1)}, bf16[64,3584]{1,0:T(8,128)(2,1)S(1)}, u32[]{:S(2)}, u32[]{:S(2)}) %collective-permute-start.1) | collective-permute-done | bytes 458784 | tf_op jit(solution)/shard_map/ppermute | solution.py:141
  36.6 5.1 %all-to-all-start = ((bf16[16,8,3712]{2,1,0:T(8,128)(2,1)}), bf16[16,8,3712]{2,1,0:T(8,128)(2,1)S(1)}, u32[]{:S(2)}, u32[]{:S(2)}) async-start(bf16[16,8,3712]{2,1,0:T(8,128)(2,1)} %maximum_bitcast_fusion), calls=%async_computation | async-start | bytes 1900544 | tf_op jit(solution)/shard_map/all_to_all | solution.py:153
  46.7 3.4 %collective-permute-start.2 = (bf16[3,32,3584]{2,1,0:T(8,128)(2,1)}, bf16[3,32,3584]{2,1,0:T(8,128)(2,1)}, u32[]{:S(2)}, u32[]{:S(2)}) collective-permute-start(bf16[3,32,3584]{2,1,0:T(8,128)(2,1)} %get-tuple-element.42), channel_id=1, source_target_pairs={{0,16},{16,32},{32,48},{48,0},{1,17},{17,33},{33,49},{49,1},{2,18}... | collective-permute-start | bytes 2064392 | tf_op jit(solution)/shard_map/ppermute | solution.py:58
  50.1 4.6 %collective-permute-start.3 = (bf16[3,32,3584]{2,1,0:T(8,128)(2,1)}, bf16[3,32,3584]{2,1,0:T(8,128)(2,1)}, u32[]{:S(2)}, u32[]{:S(2)}) collective-permute-start(bf16[3,32,3584]{2,1,0:T(8,128)(2,1)} %get-tuple-element.41), channel_id=1, source_target_pairs={{0,32},{16,48},{32,0},{48,16},{1,33},{17,49},{33,1},{49,17},{2,34}... | collective-permute-start | bytes 2064392 | tf_op jit(solution)/shard_map/ppermute | solution.py:58
  54.7 3.3 %collective-permute-start.4 = (bf16[3,32,3584]{2,1,0:T(8,128)(2,1)S(1)}, bf16[3,32,3584]{2,1,0:T(8,128)(2,1)}, u32[]{:S(2)}, u32[]{:S(2)}) collective-permute-start(bf16[3,32,3584]{2,1,0:T(8,128)(2,1)S(1)} %get-tuple-element.40), channel_id=1, source_target_pairs={{0,48},{16,0},{32,16},{48,32},{1,49},{17,1},{33,17},{49,33},{2,50}... | collective-permute-start | bytes 2064392 | tf_op jit(solution)/shard_map/ppermute | solution.py:58
  59.3 8.2 %collective-permute-done.2 = bf16[3,32,3584]{2,1,0:T(8,128)(2,1)} collective-permute-done((bf16[3,32,3584]{2,1,0:T(8,128)(2,1)}, bf16[3,32,3584]{2,1,0:T(8,128)(2,1)}, u32[]{:S(2)}, u32[]{:S(2)}) %collective-permute-start.2) | collective-permute-done | bytes 688160 | tf_op jit(solution)/shard_map/ppermute | solution.py:58
  67.5 14.1 %collective-permute-done.3 = bf16[3,32,3584]{2,1,0:T(8,128)(2,1)} collective-permute-done((bf16[3,32,3584]{2,1,0:T(8,128)(2,1)}, bf16[3,32,3584]{2,1,0:T(8,128)(2,1)}, u32[]{:S(2)}, u32[]{:S(2)}) %collective-permute-start.3) | collective-permute-done | bytes 688160 | tf_op jit(solution)/shard_map/ppermute | solution.py:58
  86.8 4.7 %collective-permute-start.7 = (bf16[64,3584]{1,0:T(8,128)(2,1)}, bf16[64,3584]{1,0:T(8,128)(2,1)}, u32[]{:S(2)}, u32[]{:S(2)}) collective-permute-start(bf16[64,3584]{1,0:T(8,128)(2,1)} %fusion.30), channel_id=1, source_target_pairs={{0,48},{16,0},{32,16},{48,32},{1,49},{17,1},{33,17},{49,33},{2,50}... | collective-permute-start | bytes 1376264 | tf_op jit(solution)/shard_map/ppermute | solution.py:58
  96.2 3.8 %collective-permute-start.8 = (bf16[3,32,3584]{2,1,0:T(8,128)(2,1)S(1)}, bf16[3,32,3584]{2,1,0:T(8,128)(2,1)S(1)}, u32[]{:S(2)}, u32[]{:S(2)}) collective-permute-start(bf16[3,32,3584]{2,1,0:T(8,128)(2,1)S(1)} %get-tuple-element.38), channel_id=1, source_target_pairs={{0,2},{2,4},{4,6},{6,0},{1,3},{3,5},{5,7},{7,1},{8,10},{10,12},{12... | collective-permute-start | bytes 2064392 | tf_op jit(solution)/shard_map/ppermute | solution.py:58
  100.0 3.1 collective-permute-start.9
  103.1 4.7 %collective-permute-start.10 = (bf16[3,32,3584]{2,1,0:T(8,128)(2,1)S(1)}, bf16[3,32,3584]{2,1,0:T(8,128)(2,1)S(1)}, u32[]{:S(2)}, u32[]{:S(2)}) collective-permute-start(bf16[3,32,3584]{2,1,0:T(8,128)(2,1)S(1)} %get-tuple-element.36), channel_id=1, source_target_pairs={{0,6},{2,0},{4,2},{6,4},{1,7},{3,1},{5,3},{7,5},{8,14},{10,8},{12,... | collective-permute-start | bytes 2064392 | tf_op jit(solution)/shard_map/ppermute | solution.py:58
  108.4 10.0 %collective-permute-done.8 = bf16[3,32,3584]{2,1,0:T(8,128)(2,1)S(1)} collective-permute-done((bf16[3,32,3584]{2,1,0:T(8,128)(2,1)S(1)}, bf16[3,32,3584]{2,1,0:T(8,128)(2,1)S(1)}, u32[]{:S(2)}, u32[]{:S(2)}) %collective-permute-start.8) | collective-permute-done | bytes 688160 | tf_op jit(solution)/shard_map/ppermute | solution.py:58
  121.2 23.5 %collective-permute-done.9 = bf16[3,32,3584]{2,1,0:T(8,128)(2,1)S(1)} collective-permute-done((bf16[3,32,3584]{2,1,0:T(8,128)(2,1)S(1)}, bf16[3,32,3584]{2,1,0:T(8,128)(2,1)S(1)}, u32[]{:S(2)}, u32[]{:S(2)}) %collective-permute-start.9) | collective-permute-done | bytes 688160 | tf_op jit(solution)/shard_map/ppermute | solution.py:58
  152.3 22.8 %all-to-all-start.1 = ((bf16[16,8,3712]{2,1,0:T(8,128)(2,1)}), bf16[16,8,3712]{2,1,0:T(8,128)(2,1)}, u32[]{:S(2)}, u32[]{:S(2)}) async-start(bf16[16,8,3712]{2,1,0:T(8,128)(2,1)} %maximum_bitcast_fusion.1), calls=%async_computation.1 | async-start | bytes 1900544 | tf_op jit(solution)/shard_map/all_to_all | solution.py:153
  176.3 3.5 %collective-permute-start.16 = (bf16[64,3584]{1,0:T(8,128)(2,1)S(1)}, bf16[64,3584]{1,0:T(8,128)(2,1)S(1)}, u32[]{:S(2)}, u32[]{:S(2)}) collective-permute-start(bf16[64,3584]{1,0:T(8,128)(2,1)S(1)} %fusion.20), channel_id=1, source_target_pairs={{0,32},{16,48},{32,0},{48,16},{1,33},{17,49},{33,1},{49,17},{2,34}... | collective-permute-start | bytes 1376264 | tf_op jit(solution)/shard_map/ppermute | solution.py:58
  188.1 3.0 collective-permute-start.14
  191.2 4.8 %collective-permute-start.13 = (bf16[64,3584]{1,0:T(8,128)(2,1)S(1)}, bf16[64,3584]{1,0:T(8,128)(2,1)S(1)}, u32[]{:S(2)}, u32[]{:S(2)}) collective-permute-start(bf16[64,3584]{1,0:T(8,128)(2,1)S(1)} %get-tuple-element.49), channel_id=1, source_target_pairs={{0,32},{16,48},{32,0},{48,16},{1,33},{17,49},{33,1},{49,17},{2,34}... | collective-permute-start | bytes 1376264 | tf_op jit(solution)/shard_map/ppermute | solution.py:58
  195.9 3.5 %collective-permute-start.12 = (bf16[64,3584]{1,0:T(8,128)(2,1)S(1)}, bf16[64,3584]{1,0:T(8,128)(2,1)S(1)}, u32[]{:S(2)}, u32[]{:S(2)}) collective-permute-start(bf16[64,3584]{1,0:T(8,128)(2,1)S(1)} %get-tuple-element.47), channel_id=1, source_target_pairs={{0,48},{16,0},{32,16},{48,32},{1,49},{17,1},{33,17},{49,33},{2,50}... | collective-permute-start | bytes 1376264 | tf_op jit(solution)/shard_map/ppermute | solution.py:58
  204.6 8.0 %collective-permute-done.14 = bf16[64,3584]{1,0:T(8,128)(2,1)S(1)} collective-permute-done((bf16[64,3584]{1,0:T(8,128)(2,1)S(1)}, bf16[64,3584]{1,0:T(8,128)(2,1)S(1)}, u32[]{:S(2)}, u32[]{:S(2)}) %collective-permute-start.14) | collective-permute-done | bytes 458784 | tf_op jit(solution)/shard_map/ppermute | solution.py:58
  212.6 9.2 %collective-permute-done.13 = bf16[64,3584]{1,0:T(8,128)(2,1)S(1)} collective-permute-done((bf16[64,3584]{1,0:T(8,128)(2,1)S(1)}, bf16[64,3584]{1,0:T(8,128)(2,1)S(1)}, u32[]{:S(2)}, u32[]{:S(2)}) %collective-permute-start.13) | collective-permute-done | bytes 458784 | tf_op jit(solution)/shard_map/ppermute | solution.py:58
  225.1 9.0 %all-to-all-start.2 = ((bf16[8,8,3584]{2,1,0:T(8,128)(2,1)}), bf16[8,8,3584]{2,1,0:T(8,128)(2,1)}, u32[]{:S(2)}, u32[]{:S(2)}) async-start(bf16[8,8,3584]{2,1,0:T(8,128)(2,1)} %fusion.42), calls=%async_computation.2 | async-start | bytes 917504 | tf_op jit(solution)/shard_map/all_to_all | solution.py:161
  236.0 3.5 %collective-permute-start.19 = (bf16[64,3584]{1,0:T(8,128)(2,1)S(1)}, bf16[64,3584]{1,0:T(8,128)(2,1)S(1)}, u32[]{:S(2)}, u32[]{:S(2)}) collective-permute-start(bf16[64,3584]{1,0:T(8,128)(2,1)S(1)} %fusion.27), channel_id=1, source_target_pairs={{0,32},{16,48},{32,0},{48,16},{1,33},{17,49},{33,1},{49,17},{2,34}... | collective-permute-start | bytes 1376264 | tf_op jit(solution)/shard_map/ppermute | solution.py:58
  239.6 3.3 %collective-permute-start.18 = (bf16[64,3584]{1,0:T(8,128)(2,1)S(1)}, bf16[64,3584]{1,0:T(8,128)(2,1)S(1)}, u32[]{:S(2)}, u32[]{:S(2)}) collective-permute-start(bf16[64,3584]{1,0:T(8,128)(2,1)S(1)} %fusion.27), channel_id=1, source_target_pairs={{0,16},{16,32},{32,48},{48,0},{1,17},{17,33},{33,49},{49,1},{2,18}... | collective-permute-start | bytes 1376264 | tf_op jit(solution)/shard_map/ppermute | solution.py:58
  242.9 3.7 %fusion.94 = f32[256,512]{1,0:T(8,128)S(1)} fusion(bf16[256,3584]{1,0:T(8,128)(2,1)} %pad_maximum_fusion.3, bf16[512,3584]{1,0:T(8,128)(2,1)} %bitcast.124), kind=kOutput, calls=%fused_computation.196 | convolution fusion | flops 939524096 | bytes 6029312 | tf_op jit(solution)/shard_map/dot_general | solution.py:75
  249.4 3.5 %collective-permute-done.19 = bf16[64,3584]{1,0:T(8,128)(2,1)S(1)} collective-permute-done((bf16[64,3584]{1,0:T(8,128)(2,1)S(1)}, bf16[64,3584]{1,0:T(8,128)(2,1)S(1)}, u32[]{:S(2)}, u32[]{:S(2)}) %collective-permute-start.19) | collective-permute-done | bytes 458784 | tf_op jit(solution)/shard_map/ppermute | solution.py:58
  252.9 7.6 %collective-permute-done.18 = bf16[64,3584]{1,0:T(8,128)(2,1)S(1)} collective-permute-done((bf16[64,3584]{1,0:T(8,128)(2,1)S(1)}, bf16[64,3584]{1,0:T(8,128)(2,1)S(1)}, u32[]{:S(2)}, u32[]{:S(2)}) %collective-permute-start.18) | collective-permute-done | bytes 458784 | tf_op jit(solution)/shard_map/ppermute | solution.py:58
  266.0 3.8 %collective-permute-start.22 = (bf16[64,3584]{1,0:T(8,128)(2,1)S(1)}, bf16[64,3584]{1,0:T(8,128)(2,1)S(1)}, u32[]{:S(2)}, u32[]{:S(2)}) collective-permute-start(bf16[64,3584]{1,0:T(8,128)(2,1)S(1)} %get-tuple-element.46), channel_id=1, source_target_pairs={{0,32},{16,48},{32,0},{48,16},{1,33},{17,49},{33,1},{49,17},{2,34}... | collective-permute-start | bytes 1376264 | tf_op jit(solution)/shard_map/ppermute | solution.py:58
  269.8 4.2 %collective-permute-start.21 = (bf16[64,3584]{1,0:T(8,128)(2,1)S(1)}, bf16[64,3584]{1,0:T(8,128)(2,1)S(1)}, u32[]{:S(2)}, u32[]{:S(2)}) collective-permute-start(bf16[64,3584]{1,0:T(8,128)(2,1)S(1)} %get-tuple-element.44), channel_id=1, source_target_pairs={{0,48},{16,0},{32,16},{48,32},{1,49},{17,1},{33,17},{49,33},{2,50}... | collective-permute-start | bytes 1376264 | tf_op jit(solution)/shard_map/ppermute | solution.py:58
  274.0 15.3 %collective-permute-done.23 = bf16[64,3584]{1,0:T(8,128)(2,1)S(1)} collective-permute-done((bf16[64,3584]{1,0:T(8,128)(2,1)S(1)}, bf16[64,3584]{1,0:T(8,128)(2,1)S(1)}, u32[]{:S(2)}, u32[]{:S(2)}) %collective-permute-start.23) | collective-permute-done | bytes 458784 | tf_op jit(solution)/shard_map/ppermute | solution.py:58
  293.5 9.6 %all-to-all-start.3 = ((bf16[8,8,3584]{2,1,0:T(8,128)(2,1)}), bf16[8,8,3584]{2,1,0:T(8,128)(2,1)S(1)}, u32[]{:S(2)}, u32[]{:S(2)}) async-start(bf16[8,8,3584]{2,1,0:T(8,128)(2,1)} %fusion.43), calls=%async_computation.3 | async-start | bytes 917504 | tf_op jit(solution)/shard_map/all_to_all | solution.py:161
  305.4 22.7 %all-to-all-done.3 = bf16[8,8,3584]{2,1,0:T(8,128)(2,1)S(1)} async-done(((bf16[8,8,3584]{2,1,0:T(8,128)(2,1)}), bf16[8,8,3584]{2,1,0:T(8,128)(2,1)S(1)}, u32[]{:S(2)}, u32[]{:S(2)}) %all-to-all-start.3) | async-done | bytes 458784 | tf_op jit(solution)/shard_map/all_to_all | solution.py:161
  (109 shorter events, 72.6 us)
Async XLA Ops:
  0.6 22.6 %copy-start = (bf16[1,64,3584]{2,1,0:T(8,128)(2,1)S(1)}, bf16[1,64,3584]{2,1,0:T(8,128)(2,1)}, u32[]{:S(2)}) copy-start(bf16[1,64,3584]{2,1,0:T(8,128)(2,1)} %param.11) | copy-start | bytes 1376260
  2.1 21.5 %collective-permute-start = (f32[4,64]{1,0:T(4,128)S(1)}, f32[4,64]{1,0:T(4,128)S(1)}, u32[]{:S(2)}, u32[]{:S(2)}) collective-permute-start(f32[4,64]{1,0:T(4,128)S(1)} %pad_maximum_fusion.4), channel_id=1, source_target_pairs={{0,64},{64,0},{1,65},{65,1},{2,66},{66,2},{3,67},{67,3},{4,68},{68... | collective-permute-start | bytes 3080 | tf_op jit(solution)/shard_map/ppermute | solution.py:142
  19.0 15.1 %collective-permute-start.1 = (bf16[64,3584]{1,0:T(8,128)(2,1)S(1)}, bf16[64,3584]{1,0:T(8,128)(2,1)S(1)}, u32[]{:S(2)}, u32[]{:S(2)}) collective-permute-start(bf16[64,3584]{1,0:T(8,128)(2,1)S(1)} %bitcast_select_fusion.1), channel_id=1, source_target_pairs={{64,192},{0,384},{192,320},{128,0},{320,448},{256,128},{448,64},{3... | collective-permute-start | bytes 1376264 | tf_op jit(solution)/shard_map/ppermute | solution.py:141
  36.6 49.0 %all-to-all-start = ((bf16[16,8,3712]{2,1,0:T(8,128)(2,1)}), bf16[16,8,3712]{2,1,0:T(8,128)(2,1)S(1)}, u32[]{:S(2)}, u32[]{:S(2)}) async-start(bf16[16,8,3712]{2,1,0:T(8,128)(2,1)} %maximum_bitcast_fusion), calls=%async_computation | async-start | bytes 1900544 | tf_op jit(solution)/shard_map/all_to_all | solution.py:153
  46.7 20.8 %collective-permute-start.2 = (bf16[3,32,3584]{2,1,0:T(8,128)(2,1)}, bf16[3,32,3584]{2,1,0:T(8,128)(2,1)}, u32[]{:S(2)}, u32[]{:S(2)}) collective-permute-start(bf16[3,32,3584]{2,1,0:T(8,128)(2,1)} %get-tuple-element.42), channel_id=1, source_target_pairs={{0,16},{16,32},{32,48},{48,0},{1,17},{17,33},{33,49},{49,1},{2,18}... | collective-permute-start | bytes 2064392 | tf_op jit(solution)/shard_map/ppermute | solution.py:58
  50.1 31.4 %collective-permute-start.3 = (bf16[3,32,3584]{2,1,0:T(8,128)(2,1)}, bf16[3,32,3584]{2,1,0:T(8,128)(2,1)}, u32[]{:S(2)}, u32[]{:S(2)}) collective-permute-start(bf16[3,32,3584]{2,1,0:T(8,128)(2,1)} %get-tuple-element.41), channel_id=1, source_target_pairs={{0,32},{16,48},{32,0},{48,16},{1,33},{17,49},{33,1},{49,17},{2,34}... | collective-permute-start | bytes 2064392 | tf_op jit(solution)/shard_map/ppermute | solution.py:58
  54.7 28.4 %collective-permute-start.4 = (bf16[3,32,3584]{2,1,0:T(8,128)(2,1)S(1)}, bf16[3,32,3584]{2,1,0:T(8,128)(2,1)}, u32[]{:S(2)}, u32[]{:S(2)}) collective-permute-start(bf16[3,32,3584]{2,1,0:T(8,128)(2,1)S(1)} %get-tuple-element.40), channel_id=1, source_target_pairs={{0,48},{16,0},{32,16},{48,32},{1,49},{17,1},{33,17},{49,33},{2,50}... | collective-permute-start | bytes 2064392 | tf_op jit(solution)/shard_map/ppermute | solution.py:58
  86.8 95.3 %collective-permute-start.7 = (bf16[64,3584]{1,0:T(8,128)(2,1)}, bf16[64,3584]{1,0:T(8,128)(2,1)}, u32[]{:S(2)}, u32[]{:S(2)}) collective-permute-start(bf16[64,3584]{1,0:T(8,128)(2,1)} %fusion.30), channel_id=1, source_target_pairs={{0,48},{16,0},{32,16},{48,32},{1,49},{17,1},{33,17},{49,33},{2,50}... | collective-permute-start | bytes 1376264 | tf_op jit(solution)/shard_map/ppermute | solution.py:58
  91.5 93.1 %collective-permute-start.6 = (bf16[64,3584]{1,0:T(8,128)(2,1)}, bf16[64,3584]{1,0:T(8,128)(2,1)}, u32[]{:S(2)}, u32[]{:S(2)}) collective-permute-start(bf16[64,3584]{1,0:T(8,128)(2,1)} %fusion.30), channel_id=1, source_target_pairs={{0,32},{16,48},{32,0},{48,16},{1,33},{17,49},{33,1},{49,17},{2,34}... | collective-permute-start | bytes 1376264 | tf_op jit(solution)/shard_map/ppermute | solution.py:58
  96.2 22.2 %collective-permute-start.8 = (bf16[3,32,3584]{2,1,0:T(8,128)(2,1)S(1)}, bf16[3,32,3584]{2,1,0:T(8,128)(2,1)S(1)}, u32[]{:S(2)}, u32[]{:S(2)}) collective-permute-start(bf16[3,32,3584]{2,1,0:T(8,128)(2,1)S(1)} %get-tuple-element.38), channel_id=1, source_target_pairs={{0,2},{2,4},{4,6},{6,0},{1,3},{3,5},{5,7},{7,1},{8,10},{10,12},{12... | collective-permute-start | bytes 2064392 | tf_op jit(solution)/shard_map/ppermute | solution.py:58
  100.0 44.7 %collective-permute-start.9 = (bf16[3,32,3584]{2,1,0:T(8,128)(2,1)S(1)}, bf16[3,32,3584]{2,1,0:T(8,128)(2,1)S(1)}, u32[]{:S(2)}, u32[]{:S(2)}) collective-permute-start(bf16[3,32,3584]{2,1,0:T(8,128)(2,1)S(1)} %get-tuple-element.37), channel_id=1, source_target_pairs={{0,4},{2,6},{4,0},{6,2},{1,5},{3,7},{5,1},{7,3},{8,12},{10,14},{12... | collective-permute-start | bytes 2064392 | tf_op jit(solution)/shard_map/ppermute | solution.py:58
  103.1 44.4 %collective-permute-start.10 = (bf16[3,32,3584]{2,1,0:T(8,128)(2,1)S(1)}, bf16[3,32,3584]{2,1,0:T(8,128)(2,1)S(1)}, u32[]{:S(2)}, u32[]{:S(2)}) collective-permute-start(bf16[3,32,3584]{2,1,0:T(8,128)(2,1)S(1)} %get-tuple-element.36), channel_id=1, source_target_pairs={{0,6},{2,0},{4,2},{6,4},{1,7},{3,1},{5,3},{7,5},{8,14},{10,8},{12,... | collective-permute-start | bytes 2064392 | tf_op jit(solution)/shard_map/ppermute | solution.py:58
  118.4 66.2 %collective-permute-start.5 = (bf16[64,3584]{1,0:T(8,128)(2,1)}, bf16[64,3584]{1,0:T(8,128)(2,1)}, u32[]{:S(2)}, u32[]{:S(2)}) collective-permute-start(bf16[64,3584]{1,0:T(8,128)(2,1)} %fusion.30), channel_id=1, source_target_pairs={{0,16},{16,32},{32,48},{48,0},{1,17},{17,33},{33,49},{49,1},{2,18}... | collective-permute-start | bytes 1376264 | tf_op jit(solution)/shard_map/ppermute | solution.py:58
  144.7 51.2 %collective-permute-start.17 = (bf16[64,3584]{1,0:T(8,128)(2,1)S(1)}, bf16[64,3584]{1,0:T(8,128)(2,1)}, u32[]{:S(2)}, u32[]{:S(2)}) collective-permute-start(bf16[64,3584]{1,0:T(8,128)(2,1)S(1)} %fusion.20), channel_id=1, source_target_pairs={{0,48},{16,0},{32,16},{48,32},{1,49},{17,1},{33,17},{49,33},{2,50}... | collective-permute-start | bytes 1376264 | tf_op jit(solution)/shard_map/ppermute | solution.py:58
  149.3 27.0 %collective-permute-start.11 = (bf16[3,128,3584]{2,1,0:T(8,128)(2,1)}, bf16[3,128,3584]{2,1,0:T(8,128)(2,1)}, u32[]{:S(2)}, u32[]{:S(2)}) collective-permute-start(bf16[3,128,3584]{2,1,0:T(8,128)(2,1)} %pad_maximum_fusion.2), channel_id=1, source_target_pairs={{0,1},{1,0},{2,3},{3,2},{4,5},{5,4},{6,7},{7,6},{8,9},{9,8},{10,11... | collective-permute-start | bytes 8257544 | tf_op jit(solution)/shard_map/ppermute | solution.py:121
  152.3 70.2 %all-to-all-start.1 = ((bf16[16,8,3712]{2,1,0:T(8,128)(2,1)}), bf16[16,8,3712]{2,1,0:T(8,128)(2,1)}, u32[]{:S(2)}, u32[]{:S(2)}) async-start(bf16[16,8,3712]{2,1,0:T(8,128)(2,1)} %maximum_bitcast_fusion.1), calls=%async_computation.1 | async-start | bytes 1900544 | tf_op jit(solution)/shard_map/all_to_all | solution.py:153
  176.3 23.1 %collective-permute-start.16 = (bf16[64,3584]{1,0:T(8,128)(2,1)S(1)}, bf16[64,3584]{1,0:T(8,128)(2,1)S(1)}, u32[]{:S(2)}, u32[]{:S(2)}) collective-permute-start(bf16[64,3584]{1,0:T(8,128)(2,1)S(1)} %fusion.20), channel_id=1, source_target_pairs={{0,32},{16,48},{32,0},{48,16},{1,33},{17,49},{33,1},{49,17},{2,34}... | collective-permute-start | bytes 1376264 | tf_op jit(solution)/shard_map/ppermute | solution.py:58
  182.1 20.2 %collective-permute-start.15 = (bf16[64,3584]{1,0:T(8,128)(2,1)S(1)}, bf16[64,3584]{1,0:T(8,128)(2,1)S(1)}, u32[]{:S(2)}, u32[]{:S(2)}) collective-permute-start(bf16[64,3584]{1,0:T(8,128)(2,1)S(1)} %fusion.20), channel_id=1, source_target_pairs={{0,16},{16,32},{32,48},{48,0},{1,17},{17,33},{33,49},{49,1},{2,18}... | collective-permute-start | bytes 1376264 | tf_op jit(solution)/shard_map/ppermute | solution.py:58
  188.1 24.5 %collective-permute-start.14 = (bf16[64,3584]{1,0:T(8,128)(2,1)S(1)}, bf16[64,3584]{1,0:T(8,128)(2,1)S(1)}, u32[]{:S(2)}, u32[]{:S(2)}) collective-permute-start(bf16[64,3584]{1,0:T(8,128)(2,1)S(1)} %get-tuple-element.48), channel_id=1, source_target_pairs={{0,16},{16,32},{32,48},{48,0},{1,17},{17,33},{33,49},{49,1},{2,18}... | collective-permute-start | bytes 1376264 | tf_op jit(solution)/shard_map/ppermute | solution.py:58
  191.2 30.7 %collective-permute-start.13 = (bf16[64,3584]{1,0:T(8,128)(2,1)S(1)}, bf16[64,3584]{1,0:T(8,128)(2,1)S(1)}, u32[]{:S(2)}, u32[]{:S(2)}) collective-permute-start(bf16[64,3584]{1,0:T(8,128)(2,1)S(1)} %get-tuple-element.49), channel_id=1, source_target_pairs={{0,32},{16,48},{32,0},{48,16},{1,33},{17,49},{33,1},{49,17},{2,34}... | collective-permute-start | bytes 1376264 | tf_op jit(solution)/shard_map/ppermute | solution.py:58
  195.9 25.9 %collective-permute-start.12 = (bf16[64,3584]{1,0:T(8,128)(2,1)S(1)}, bf16[64,3584]{1,0:T(8,128)(2,1)S(1)}, u32[]{:S(2)}, u32[]{:S(2)}) collective-permute-start(bf16[64,3584]{1,0:T(8,128)(2,1)S(1)} %get-tuple-element.47), channel_id=1, source_target_pairs={{0,48},{16,0},{32,16},{48,32},{1,49},{17,1},{33,17},{49,33},{2,50}... | collective-permute-start | bytes 1376264 | tf_op jit(solution)/shard_map/ppermute | solution.py:58
  225.1 38.7 %all-to-all-start.2 = ((bf16[8,8,3584]{2,1,0:T(8,128)(2,1)}), bf16[8,8,3584]{2,1,0:T(8,128)(2,1)}, u32[]{:S(2)}, u32[]{:S(2)}) async-start(bf16[8,8,3584]{2,1,0:T(8,128)(2,1)} %fusion.42), calls=%async_computation.2 | async-start | bytes 917504 | tf_op jit(solution)/shard_map/all_to_all | solution.py:161
  234.1 15.3 %collective-permute-start.20 = (bf16[64,3584]{1,0:T(8,128)(2,1)S(1)}, bf16[64,3584]{1,0:T(8,128)(2,1)S(1)}, u32[]{:S(2)}, u32[]{:S(2)}) collective-permute-start(bf16[64,3584]{1,0:T(8,128)(2,1)S(1)} %fusion.27), channel_id=1, source_target_pairs={{0,48},{16,0},{32,16},{48,32},{1,49},{17,1},{33,17},{49,33},{2,50}... | collective-permute-start | bytes 1376264 | tf_op jit(solution)/shard_map/ppermute | solution.py:58
  236.0 16.9 %collective-permute-start.19 = (bf16[64,3584]{1,0:T(8,128)(2,1)S(1)}, bf16[64,3584]{1,0:T(8,128)(2,1)S(1)}, u32[]{:S(2)}, u32[]{:S(2)}) collective-permute-start(bf16[64,3584]{1,0:T(8,128)(2,1)S(1)} %fusion.27), channel_id=1, source_target_pairs={{0,32},{16,48},{32,0},{48,16},{1,33},{17,49},{33,1},{49,17},{2,34}... | collective-permute-start | bytes 1376264 | tf_op jit(solution)/shard_map/ppermute | solution.py:58
  239.6 20.9 %collective-permute-start.18 = (bf16[64,3584]{1,0:T(8,128)(2,1)S(1)}, bf16[64,3584]{1,0:T(8,128)(2,1)S(1)}, u32[]{:S(2)}, u32[]{:S(2)}) collective-permute-start(bf16[64,3584]{1,0:T(8,128)(2,1)S(1)} %fusion.27), channel_id=1, source_target_pairs={{0,16},{16,32},{32,48},{48,0},{1,17},{17,33},{33,49},{49,1},{2,18}... | collective-permute-start | bytes 1376264 | tf_op jit(solution)/shard_map/ppermute | solution.py:58
  246.6 16.0 %copy-start.3 = (bf16[2,256,3584]{2,1,0:T(8,128)(2,1)S(1)}, bf16[2,256,3584]{2,1,0:T(8,128)(2,1)}, u32[]{:S(2)}) copy-start(bf16[2,256,3584]{2,1,0:T(8,128)(2,1)} %copy-done.2) | copy-start | bytes 11010052
  263.9 25.4 %collective-permute-start.23 = (bf16[64,3584]{1,0:T(8,128)(2,1)S(1)}, bf16[64,3584]{1,0:T(8,128)(2,1)S(1)}, u32[]{:S(2)}, u32[]{:S(2)}) collective-permute-start(bf16[64,3584]{1,0:T(8,128)(2,1)S(1)} %get-tuple-element.45), channel_id=1, source_target_pairs={{0,16},{16,32},{32,48},{48,0},{1,17},{17,33},{33,49},{49,1},{2,18}... | collective-permute-start | bytes 1376264 | tf_op jit(solution)/shard_map/ppermute | solution.py:58
  266.0 23.2 %collective-permute-start.22 = (bf16[64,3584]{1,0:T(8,128)(2,1)S(1)}, bf16[64,3584]{1,0:T(8,128)(2,1)S(1)}, u32[]{:S(2)}, u32[]{:S(2)}) collective-permute-start(bf16[64,3584]{1,0:T(8,128)(2,1)S(1)} %get-tuple-element.46), channel_id=1, source_target_pairs={{0,32},{16,48},{32,0},{48,16},{1,33},{17,49},{33,1},{49,17},{2,34}... | collective-permute-start | bytes 1376264 | tf_op jit(solution)/shard_map/ppermute | solution.py:58
  269.8 33.3 %copy-start.9 = (s32[1,64,1]{1,2,0:T(1,128)S(1)}, s32[1,64,1]{1,2,0:T(1,128)}, u32[]{:S(2)}) copy-start(s32[1,64,1]{1,2,0:T(1,128)} %param.13) | copy-start | bytes 772
  269.8 22.0 %collective-permute-start.21 = (bf16[64,3584]{1,0:T(8,128)(2,1)S(1)}, bf16[64,3584]{1,0:T(8,128)(2,1)S(1)}, u32[]{:S(2)}, u32[]{:S(2)}) collective-permute-start(bf16[64,3584]{1,0:T(8,128)(2,1)S(1)} %get-tuple-element.44), channel_id=1, source_target_pairs={{0,48},{16,0},{32,16},{48,32},{1,49},{17,1},{33,17},{49,33},{2,50}... | collective-permute-start | bytes 1376264 | tf_op jit(solution)/shard_map/ppermute | solution.py:58
  292.2 37.0 %copy-start.1 = (bf16[1,64,3584]{2,1,0:T(8,128)(2,1)S(1)}, bf16[1,64,3584]{2,1,0:T(8,128)(2,1)}, u32[]{:S(2)}) copy-start(bf16[1,64,3584]{2,1,0:T(8,128)(2,1)} %param.11) | copy-start | bytes 1376260
  293.5 34.7 %all-to-all-start.3 = ((bf16[8,8,3584]{2,1,0:T(8,128)(2,1)}), bf16[8,8,3584]{2,1,0:T(8,128)(2,1)S(1)}, u32[]{:S(2)}, u32[]{:S(2)}) async-start(bf16[8,8,3584]{2,1,0:T(8,128)(2,1)} %fusion.43), calls=%async_computation.3 | async-start | bytes 917504 | tf_op jit(solution)/shard_map/all_to_all | solution.py:161
  (6 other events, 23.9 us)

commit v4 on v3

--- a/solution.py
+++ b/solution.py
@@ -58,16 +58,18 @@
     return lax.ppermute(x, axis, [(i, (i + by) % length) for i in range(length)])
 
 
-def gather_x(rows):
-    return jnp.concatenate([rows] + [rotated(rows, "x", j) for j in (1, 2, 3)], axis=0)
-
-
-def scatter_sum_x(parts):
-    own = parts[:ROWS]
-    sent = parts.astype(jnp.bfloat16)
-    total = own.astype(jnp.bfloat16).astype(jnp.float32)
-    for j in (1, 2, 3):
-        total = total + rotated(sent[j * ROWS : (j + 1) * ROWS], "x", -j).astype(jnp.float32)
+def around_x(rows):
+    return [rows] + [rotated(rows, "x", j) for j in (1, 2, 3)]
+
+
+def scatter_sum_x(first, second):
+    def block(j):
+        rows = slice(j * ROWS, (j + 1) * ROWS)
+        return jnp.concatenate([first[rows], second[rows]], axis=0)
+
+    total = block(0).astype(jnp.float32)
+    for j in (2, 1, 3):
+        total = total + rotated(block(j), "x", -j).astype(jnp.float32)
     return total
 
 
@@ -103,24 +105,22 @@
     def piece(index):
         return lax.dynamic_index_in_dim(pieces, index, axis=1, keepdims=False)
 
-    return [piece(x)] + [rotated(piece((x + k) % 4), "x", k) for k in (1, 2, 3)]
-
-
-def weights_along_z(pieces):
-    x, zr = lax.axis_index("x"), lax.axis_index("zr")
-    along_x = jnp.stack(pieces)
-    blocks = [
+    along_x = jnp.stack(
+        [piece(x)] + [rotated(piece((x + k) % 4), "x", k) for k in (1, 2, 3)]
+    )
+    return [
         lax.dynamic_index_in_dim(along_x, (x - zr - m + 8) % 4, axis=0, keepdims=False)
         for m in range(4)
     ]
+
+
+def weights_along_z(blocks):
     return blocks[:1] + [rotated(blocks[m], "zr", m) for m in (1, 2, 3)]
 
 
-def weights_of_chip(blocks):
+def both_cores(blocks):
     mine = jnp.concatenate(blocks, axis=1)
-    other = lax.ppermute(mine, "c", [(0, 1), (1, 0)])
-    both = jnp.concatenate([mine, other], axis=1)
-    return both[:2].reshape(-1, both.shape[2]), both[2]
+    return [mine, lax.ppermute(mine, "c", [(0, 1), (1, 0)])]
 
 
 def body(
@@ -156,10 +156,6 @@
         got = got.reshape(2, ROWS, features + LANES)
         return jnp.where(is_high, got[1], got[0]), jnp.where(is_high, got[0], got[1])
 
-    def give_back(rows):
-        rows = rows.reshape(EXPERTS, DEPTH, features)
-        return lax.all_to_all(rows, Z8, split_axis=0, concat_axis=0, tiled=True)
-
     home_bwd = slot_matrix(own_bwd)
     send_saved = jnp.pad(reorder(home_bwd, saved[0]), ((0, 0), (0, LANES)))
     send_fwd = reorder(
@@ -168,35 +164,45 @@
     got_first = dispatch(send_saved, send_fwd)
     got_first, blocks = lax.optimization_barrier((got_first, blocks))
     got_saved, got_fwd = sides(got_first)
+    section_input = got_fwd[:, :features]
+    normed_fwd, _ = normalize(section_input)
+    normed_bwd, scale_bwd = normalize(got_saved[:, :features])
+    rows = jnp.concatenate([normed_fwd, normed_bwd], axis=0).astype(jnp.bfloat16)
     blocks = weights_along_z(blocks)
+    rows, blocks[1] = lax.optimization_barrier((rows, blocks[1]))
+    gathered = around_x(rows)
     send_cot = reorder(
         slot_matrix(mid_bwd), jnp.concatenate([cot_rows, gate_lanes(flat[3])], axis=1)
     )
-    send_cot, blocks = lax.optimization_barrier((send_cot, blocks))
     got_cot = dispatch(jnp.zeros_like(send_cot), send_cot)
-    gate_up, down = weights_of_chip(blocks)
-
-    section_input = got_fwd[:, :features]
-    normed_fwd, _ = normalize(section_input)
-    parts = expert_out(gather_x(normed_fwd.astype(jnp.bfloat16)), gate_up, down)
-    normed_bwd, scale_bwd = normalize(got_saved[:, :features])
-    all_normed = gather_x(normed_bwd.astype(jnp.bfloat16))
-    mixed = scatter_sum_x(parts)
-    mixed, all_normed, got_cot = lax.optimization_barrier((mixed, all_normed, got_cot))
+    gathered, got_cot = lax.optimization_barrier((gathered, got_cot))
     _, got_cot = sides(got_cot)
     cotangent = got_cot[:, :features].astype(jnp.float32)
     gated = (gate_of(got_cot[:, features:]) * cotangent).astype(jnp.bfloat16)
-    mixed, gated = lax.optimization_barrier((mixed, gated))
-    mixture = gate_of(got_fwd[:, features:]) * mixed
+    all_gated = around_x(gated)
+    all_gated, late = lax.optimization_barrier((all_gated, blocks[2:]))
+    held = both_cores(blocks[:2]) + both_cores(late)
+    gate_up = jnp.concatenate([part[:2] for part in held], axis=1).reshape(-1, features)
+    down = jnp.concatenate([part[2] for part in held], axis=0)
+
+    all_fwd = jnp.concatenate([rows[:ROWS] for rows in gathered], axis=0)
+    all_bwd = jnp.concatenate([rows[ROWS:] for rows in gathered], axis=0)
+    parts_fwd = expert_out(all_fwd, gate_up, down).astype(jnp.bfloat16)
+    parts_bwd = expert_grad(all_bwd, jnp.concatenate(all_gated, axis=0), gate_up, down).astype(
+        jnp.bfloat16
+    )
+    summed = scatter_sum_x(parts_fwd, parts_bwd)
+    summed_fwd, summed_bwd = summed[:ROWS], summed[ROWS:]
+    mixture = gate_of(got_fwd[:, features:]) * summed_fwd
     acts = (section_input.astype(jnp.float32) + mixture).astype(jnp.bfloat16)
-    got_acts = give_back(acts)
-    parts = expert_grad(all_normed, gather_x(gated), gate_up, down)
-    parts, got_acts = lax.optimization_barrier((parts, got_acts))
-    summed = scatter_sum_x(parts)
-    projection = jnp.mean(normed_bwd * summed, axis=-1, keepdims=True)
-    grads = (cotangent + scale_bwd * (summed - normed_bwd * projection)).astype(jnp.bfloat16)
-    output_grad = reorder(home_bwd.T, give_back(grads).reshape(ROWS, features))
-    output_act = reorder(slot_matrix(own_fwd).T, got_acts.reshape(ROWS, features))
+    projection = jnp.mean(normed_bwd * summed_bwd, axis=-1, keepdims=True)
+    grads = (cotangent + scale_bwd * (summed_bwd - normed_bwd * projection)).astype(jnp.bfloat16)
+    back = jnp.concatenate(
+        [rows.reshape(EXPERTS, DEPTH, features) for rows in (acts, grads)], axis=1
+    )
+    back = lax.all_to_all(back, Z8, split_axis=0, concat_axis=0, tiled=True)
+    output_act = reorder(slot_matrix(own_fwd).T, back[:, :DEPTH].reshape(ROWS, features))
+    output_grad = reorder(home_bwd.T, back[:, DEPTH:].reshape(ROWS, features))
     return (output_act[None], output_grad[None])
 
 

time: 332 us -> 361 us (1.087)
  waiting for transfers between devices: 145 us -> 217 us
  starting transfers between devices: 139 us -> 102 us
  local copies, waits for them, and re-layouts: 7.46 us -> 14.3 us
  matrix products: 15.2 us -> 8.76 us
  other arithmetic: 21.6 us -> 15.9 us
    ppermute x21 -> x15, waiting for transfers between devices: 109 us -> 158 us  [rotated(): lax.ppermute(x, axis, [(i, (i + by) % length) for i in range(length)])]
    ppermute x21 -> x15, starting transfers between devices: 72 us -> 46.1 us  [rotated(): lax.ppermute(x, axis, [(i, (i + by) % length) for i in range(length)])]
    all_to_all x2 -> x1, waiting for transfers between devices: 22.7 us -> 45.6 us  [body(): back = lax.all_to_all(back, Z8, split_axis=0, concat_axis=0, tiled=True)]
    all_to_all x2, starting transfers between devices: 27.9 us -> 16.8 us  [dispatch(): return lax.all_to_all(both, Z16, split_axis=0, concat_axis=0, tiled=True)]
    dot_general x3, matrix products: 8.62 us -> 2.95 us  [nt(): lax.dot_general(a, b, (((1,), (1,)), ((), ())), preferred_element_type=jn...]
    slice x3 -> x10, local copies, waits for them, and re-layouts: 0.43 us -> 5.47 us  [the longest x4 4.98 us: body(): all_fwd = jnp.concatenate([rows[:ROWS] for rows in gathered], axis=0)]
    all_to_all x2 -> x1, starting transfers between devices: 18.6 us -> 17.4 us  [body(): back = lax.all_to_all(back, Z8, split_axis=0, concat_axis=0, tiled=True)]
  transfers between devices with their start and end apart: 28 -> 22, of which waited for: 17 -> 15; matrix products, arithmetic and copies ran while one was open for 10% -> 7% of each run, Pallas kernels for 0% -> 0%
where the time goes in v4:
time: 361 us; the launch traced here: 360 us
  waiting for transfers between devices  217 us (60%)
  starting transfers between devices  102 us (28%)
  other arithmetic  15.9 us (4%)
  local copies, waits for them, and re-layouts  14.3 us (4%)
  matrix products  8.76 us (2%)
    ppermute x15, waiting for transfers between devices, rotated(): lax.ppermute(x, axis, [(i, (i + by) % length) for i in range(length)])  158 us
    ppermute x15, starting transfers between devices, rotated(): lax.ppermute(x, axis, [(i, (i + by) % length) for i in range(length)])  46.1 us
    all_to_all x1, waiting for transfers between devices, body(): back = lax.all_to_all(back, Z8, split_axis=0, concat_axis=0, tiled=True)  45.6 us
    all_to_all x1, starting transfers between devices, body(): back = lax.all_to_all(back, Z8, split_axis=0, concat_axis=0, tiled=True)  17.4 us
    all_to_all x2, starting transfers between devices, dispatch(): return lax.all_to_all(both, Z16, split_axis=0, concat_axis=0, tiled=True)  16.8 us
    ppermute x1, starting transfers between devices, body(): flat = lax.ppermute(flat, 'zh', [(0, 1), (1, 0)])  15.7 us
    ppermute x1, waiting for transfers between devices, body(): along_y = lax.ppermute(along_y, PP, moves)  9.98 us
  transfers between devices with their start and end apart: 22, of which 15 were waited for; matrix products, arithmetic and copies ran while one was open for 7% of the time, Pallas kernels for 0%

profile of v4, /device:TPU:24, one launch (start us, length us, event | category | flops | bytes accessed | tf_op | source)
XLA Modules:
  0.0 359.5 jit_solution(1083344968023620617)
XLA Ops:
  2.1 15.7 %collective-permute-start = (f32[4,64]{1,0:T(4,128)S(1)}, f32[4,64]{1,0:T(4,128)S(1)}, u32[]{:S(2)}, u32[]{:S(2)}) collective-permute-start(f32[4,64]{1,0:T(4,128)S(1)} %pad_maximum_fusion.11), channel_id=1, source_target_pairs={{0,64},{64,0},{1,65},{65,1},{2,66},{66,2},{3,67},{67,3},{4,68},{68... | collective-permute-start | bytes 3080 | tf_op jit(solution)/shard_map/ppermute | solution.py:142
  19.1 2.7 collective-permute-start.1
  24.2 10.0 %collective-permute-done.1 = bf16[64,3584]{1,0:T(8,128)(2,1)S(1)} collective-permute-done((bf16[64,3584]{1,0:T(8,128)(2,1)S(1)}, bf16[64,3584]{1,0:T(8,128)(2,1)S(1)}, u32[]{:S(2)}, u32[]{:S(2)}) %collective-permute-start.1) | collective-permute-done | bytes 458784 | tf_op jit(solution)/shard_map/ppermute | solution.py:141
  36.3 5.1 %all-to-all-start = ((bf16[16,8,3712]{2,1,0:T(8,128)(2,1)}), bf16[16,8,3712]{2,1,0:T(8,128)(2,1)S(1)}, u32[]{:S(2)}, u32[]{:S(2)}) async-start(bf16[16,8,3712]{2,1,0:T(8,128)(2,1)} %maximum_bitcast_fusion), calls=%async_computation | async-start | bytes 1900544 | tf_op jit(solution)/shard_map/all_to_all | solution.py:153
  46.1 4.6 %collective-permute-start.4 = (bf16[3,32,3584]{2,1,0:T(8,128)(2,1)}, bf16[3,32,3584]{2,1,0:T(8,128)(2,1)}, u32[]{:S(2)}, u32[]{:S(2)}) collective-permute-start(bf16[3,32,3584]{2,1,0:T(8,128)(2,1)} %get-tuple-element.43), channel_id=1, source_target_pairs={{0,48},{16,0},{32,16},{48,32},{1,49},{17,1},{33,17},{49,33},{2,50}... | collective-permute-start | bytes 2064392 | tf_op jit(solution)/shard_map/ppermute | solution.py:58
  50.7 2.7 collective-permute-start.3
  53.5 2.8 collective-permute-start.2
  58.8 20.3 %collective-permute-done.4 = bf16[3,32,3584]{2,1,0:T(8,128)(2,1)} collective-permute-done((bf16[3,32,3584]{2,1,0:T(8,128)(2,1)}, bf16[3,32,3584]{2,1,0:T(8,128)(2,1)}, u32[]{:S(2)}, u32[]{:S(2)}) %collective-permute-start.4) | collective-permute-done | bytes 688160 | tf_op jit(solution)/shard_map/ppermute | solution.py:58
  79.0 5.4 %collective-permute-done.2 = bf16[3,32,3584]{2,1,0:T(8,128)(2,1)} collective-permute-done((bf16[3,32,3584]{2,1,0:T(8,128)(2,1)S(1)}, bf16[3,32,3584]{2,1,0:T(8,128)(2,1)}, u32[]{:S(2)}, u32[]{:S(2)}) %collective-permute-start.2) | collective-permute-done | bytes 688160 | tf_op jit(solution)/shard_map/ppermute | solution.py:58
  87.5 11.7 %all-to-all-start.1 = ((bf16[16,8,3712]{2,1,0:T(8,128)(2,1)}), bf16[16,8,3712]{2,1,0:T(8,128)(2,1)S(1)}, u32[]{:S(2)}, u32[]{:S(2)}) async-start(bf16[16,8,3712]{2,1,0:T(8,128)(2,1)} %maximum_bitcast_fusion.1), calls=%async_computation.1 | async-start | bytes 1900544 | tf_op jit(solution)/shard_map/all_to_all | solution.py:153
  100.3 3.8 %collective-permute-start.5 = (bf16[3,32,3584]{2,1,0:T(8,128)(2,1)S(1)}, bf16[3,32,3584]{2,1,0:T(8,128)(2,1)S(1)}, u32[]{:S(2)}, u32[]{:S(2)}) collective-permute-start(bf16[3,32,3584]{2,1,0:T(8,128)(2,1)S(1)} %copy-done.7), channel_id=1, source_target_pairs={{0,2},{2,4},{4,6},{6,0},{1,3},{3,5},{5,7},{7,1},{8,10},{10,12},{12... | collective-permute-start | bytes 2064392 | tf_op jit(solution)/shard_map/ppermute | solution.py:58
  104.1 4.3 %collective-permute-start.13 = (bf16[3,32,3584]{2,1,0:T(8,128)(2,1)}, bf16[3,32,3584]{2,1,0:T(8,128)(2,1)}, u32[]{:S(2)}, u32[]{:S(2)}) collective-permute-start(bf16[3,32,3584]{2,1,0:T(8,128)(2,1)} %get-tuple-element.30), channel_id=1, source_target_pairs={{0,4},{2,6},{4,0},{6,2},{1,5},{3,7},{5,1},{7,3},{8,12},{10,14},{12... | collective-permute-start | bytes 2064392 | tf_op jit(solution)/shard_map/ppermute | solution.py:58
  108.4 3.4 collective-permute-start.14
  113.2 47.1 %collective-permute-done.5 = bf16[3,32,3584]{2,1,0:T(8,128)(2,1)S(1)} collective-permute-done((bf16[3,32,3584]{2,1,0:T(8,128)(2,1)S(1)}, bf16[3,32,3584]{2,1,0:T(8,128)(2,1)S(1)}, u32[]{:S(2)}, u32[]{:S(2)}) %collective-permute-start.5) | collective-permute-done | bytes 688160 | tf_op jit(solution)/shard_map/ppermute | solution.py:58
  162.5 2.7 collective-permute-start.7
  165.3 2.9 collective-permute-start.6
  169.4 16.3 %collective-permute-done.8 = bf16[128,3584]{1,0:T(8,128)(2,1)} collective-permute-done((bf16[128,3584]{1,0:T(8,128)(2,1)}, bf16[128,3584]{1,0:T(8,128)(2,1)}, u32[]{:S(2)}, u32[]{:S(2)}) %collective-permute-start.8) | collective-permute-done | bytes 917536 | tf_op jit(solution)/shard_map/ppermute | solution.py:58
  185.7 3.9 %collective-permute-done.7 = bf16[128,3584]{1,0:T(8,128)(2,1)} collective-permute-done((bf16[128,3584]{1,0:T(8,128)(2,1)}, bf16[128,3584]{1,0:T(8,128)(2,1)}, u32[]{:S(2)}, u32[]{:S(2)}) %collective-permute-start.7) | collective-permute-done | bytes 917536 | tf_op jit(solution)/shard_map/ppermute | solution.py:58
  189.6 16.1 %collective-permute-done.6 = bf16[128,3584]{1,0:T(8,128)(2,1)} collective-permute-done((bf16[128,3584]{1,0:T(8,128)(2,1)}, bf16[128,3584]{1,0:T(8,128)(2,1)}, u32[]{:S(2)}, u32[]{:S(2)}) %collective-permute-start.6) | collective-permute-done | bytes 917536 | tf_op jit(solution)/shard_map/ppermute | solution.py:58
  206.1 2.5 collective-permute-start.12
  208.6 2.7 collective-permute-start.11
  211.3 2.7 collective-permute-start.10
  221.3 4.2 %collective-permute-done.11 = bf16[64,3584]{1,0:T(8,128)(2,1)S(1)} collective-permute-done((bf16[64,3584]{1,0:T(8,128)(2,1)S(1)}, bf16[64,3584]{1,0:T(8,128)(2,1)S(1)}, u32[]{:S(2)}, u32[]{:S(2)}) %collective-permute-start.11) | collective-permute-done | bytes 458784 | tf_op jit(solution)/shard_map/ppermute | solution.py:58
  225.5 8.2 %collective-permute-done.10 = bf16[64,3584]{1,0:T(8,128)(2,1)S(1)} collective-permute-done((bf16[64,3584]{1,0:T(8,128)(2,1)S(1)}, bf16[64,3584]{1,0:T(8,128)(2,1)S(1)}, u32[]{:S(2)}, u32[]{:S(2)}) %collective-permute-start.10) | collective-permute-done | bytes 458784 | tf_op jit(solution)/shard_map/ppermute | solution.py:58
  238.1 2.9 collective-permute-done.15
  246.5 2.7 collective-permute-start.16
  249.3 3.1 collective-permute-start.17
  252.5 2.7 collective-permute-start.18
  255.4 17.7 %collective-permute-done.16 = bf16[128,3584]{1,0:T(8,128)(2,1)S(1)} collective-permute-done((bf16[128,3584]{1,0:T(8,128)(2,1)S(1)}, bf16[128,3584]{1,0:T(8,128)(2,1)S(1)}, u32[]{:S(2)}, u32[]{:S(2)}) %collective-permute-start.16) | collective-permute-done | bytes 917536 | tf_op jit(solution)/shard_map/ppermute | solution.py:58
  273.1 16.8 %collective-permute-done.17 = bf16[128,3584]{1,0:T(8,128)(2,1)S(1)} collective-permute-done((bf16[128,3584]{1,0:T(8,128)(2,1)S(1)}, bf16[128,3584]{1,0:T(8,128)(2,1)S(1)}, u32[]{:S(2)}, u32[]{:S(2)}) %collective-permute-start.17) | collective-permute-done | bytes 917536 | tf_op jit(solution)/shard_map/ppermute | solution.py:58
  294.2 17.4 %all-to-all-start.2 = ((bf16[8,16,3584]{2,1,0:T(8,128)(2,1)}), bf16[8,16,3584]{2,1,0:T(8,128)(2,1)S(1)}, u32[]{:S(2)}, u32[]{:S(2)}) async-start(bf16[8,16,3584]{2,1,0:T(8,128)(2,1)} %pad_maximum_fusion.8), calls=%async_computation.2 | async-start | bytes 1835008 | tf_op jit(solution)/shard_map/all_to_all | solution.py:203
  311.8 45.6 %all-to-all-done.2 = bf16[8,16,3584]{2,1,0:T(8,128)(2,1)S(1)} async-done(((bf16[8,16,3584]{2,1,0:T(8,128)(2,1)}), bf16[8,16,3584]{2,1,0:T(8,128)(2,1)S(1)}, u32[]{:S(2)}, u32[]{:S(2)}) %all-to-all-start.2) | async-done | bytes 917536 | tf_op jit(solution)/shard_map/all_to_all | solution.py:203
  (107 shorter events, 47.6 us)
Async XLA Ops:
  0.6 22.7 %copy-start = (bf16[1,64,3584]{2,1,0:T(8,128)(2,1)S(1)}, bf16[1,64,3584]{2,1,0:T(8,128)(2,1)}, u32[]{:S(2)}) copy-start(bf16[1,64,3584]{2,1,0:T(8,128)(2,1)} %param.11) | copy-start | bytes 1376260
  0.6 33.5 %copy-start.4 = (bf16[1,64,3584]{2,1,0:T(8,128)(2,1)S(1)}, bf16[1,64,3584]{2,1,0:T(8,128)(2,1)}, u32[]{:S(2)}) copy-start(bf16[1,64,3584]{2,1,0:T(8,128)(2,1)} %param.12) | copy-start | bytes 1376260
  0.7 33.5 %copy-start.5 = (bf16[1,64,3584]{2,1,0:T(8,128)(2,1)S(1)}, bf16[1,64,3584]{2,1,0:T(8,128)(2,1)}, u32[]{:S(2)}) copy-start(bf16[1,64,3584]{2,1,0:T(8,128)(2,1)} %param.10) | copy-start | bytes 1376260
  2.1 21.5 %collective-permute-start = (f32[4,64]{1,0:T(4,128)S(1)}, f32[4,64]{1,0:T(4,128)S(1)}, u32[]{:S(2)}, u32[]{:S(2)}) collective-permute-start(f32[4,64]{1,0:T(4,128)S(1)} %pad_maximum_fusion.11), channel_id=1, source_target_pairs={{0,64},{64,0},{1,65},{65,1},{2,66},{66,2},{3,67},{67,3},{4,68},{68... | collective-permute-start | bytes 3080 | tf_op jit(solution)/shard_map/ppermute | solution.py:142
  19.1 15.1 %collective-permute-start.1 = (bf16[64,3584]{1,0:T(8,128)(2,1)S(1)}, bf16[64,3584]{1,0:T(8,128)(2,1)S(1)}, u32[]{:S(2)}, u32[]{:S(2)}) collective-permute-start(bf16[64,3584]{1,0:T(8,128)(2,1)S(1)} %bitcast_select_fusion.1), channel_id=1, source_target_pairs={{64,192},{0,384},{192,320},{128,0},{320,448},{256,128},{448,64},{3... | collective-permute-start | bytes 1376264 | tf_op jit(solution)/shard_map/ppermute | solution.py:141
  35.3 6.2 %copy-start.6 = (bf16[1,1,3584,128]{3,2,1,0:T(8,128)(2,1)S(1)}, bf16[1,1,3584,128]{3,2,1,0:T(8,128)(2,1)}, u32[]{:S(2)}) copy-start(bf16[1,1,3584,128]{3,2,1,0:T(8,128)(2,1)} %param.17) | copy-start | bytes 2752516
  36.3 51.2 %all-to-all-start = ((bf16[16,8,3712]{2,1,0:T(8,128)(2,1)}), bf16[16,8,3712]{2,1,0:T(8,128)(2,1)S(1)}, u32[]{:S(2)}, u32[]{:S(2)}) async-start(bf16[16,8,3712]{2,1,0:T(8,128)(2,1)} %maximum_bitcast_fusion), calls=%async_computation | async-start | bytes 1900544 | tf_op jit(solution)/shard_map/all_to_all | solution.py:153
  46.1 33.0 %collective-permute-start.4 = (bf16[3,32,3584]{2,1,0:T(8,128)(2,1)}, bf16[3,32,3584]{2,1,0:T(8,128)(2,1)}, u32[]{:S(2)}, u32[]{:S(2)}) collective-permute-start(bf16[3,32,3584]{2,1,0:T(8,128)(2,1)} %get-tuple-element.43), channel_id=1, source_target_pairs={{0,48},{16,0},{32,16},{48,32},{1,49},{17,1},{33,17},{49,33},{2,50}... | collective-permute-start | bytes 2064392 | tf_op jit(solution)/shard_map/ppermute | solution.py:58
  50.7 28.3 %collective-permute-start.3 = (bf16[3,32,3584]{2,1,0:T(8,128)(2,1)S(1)}, bf16[3,32,3584]{2,1,0:T(8,128)(2,1)}, u32[]{:S(2)}, u32[]{:S(2)}) collective-permute-start(bf16[3,32,3584]{2,1,0:T(8,128)(2,1)S(1)} %get-tuple-element.44), channel_id=1, source_target_pairs={{0,32},{16,48},{32,0},{48,16},{1,33},{17,49},{33,1},{49,17},{2,34}... | collective-permute-start | bytes 2064392 | tf_op jit(solution)/shard_map/ppermute | solution.py:58
  53.5 31.0 %collective-permute-start.2 = (bf16[3,32,3584]{2,1,0:T(8,128)(2,1)S(1)}, bf16[3,32,3584]{2,1,0:T(8,128)(2,1)}, u32[]{:S(2)}, u32[]{:S(2)}) collective-permute-start(bf16[3,32,3584]{2,1,0:T(8,128)(2,1)S(1)} %get-tuple-element.45), channel_id=1, source_target_pairs={{0,16},{16,32},{32,48},{48,0},{1,17},{17,33},{33,49},{49,1},{2,18}... | collective-permute-start | bytes 2064392 | tf_op jit(solution)/shard_map/ppermute | solution.py:58
  87.5 81.9 %all-to-all-start.1 = ((bf16[16,8,3712]{2,1,0:T(8,128)(2,1)}), bf16[16,8,3712]{2,1,0:T(8,128)(2,1)S(1)}, u32[]{:S(2)}, u32[]{:S(2)}) async-start(bf16[16,8,3712]{2,1,0:T(8,128)(2,1)} %maximum_bitcast_fusion.1), calls=%async_computation.1 | async-start | bytes 1900544 | tf_op jit(solution)/shard_map/all_to_all | solution.py:153
  99.2 1.1 copy-start.7
  100.3 60.0 %collective-permute-start.5 = (bf16[3,32,3584]{2,1,0:T(8,128)(2,1)S(1)}, bf16[3,32,3584]{2,1,0:T(8,128)(2,1)S(1)}, u32[]{:S(2)}, u32[]{:S(2)}) collective-permute-start(bf16[3,32,3584]{2,1,0:T(8,128)(2,1)S(1)} %copy-done.7), channel_id=1, source_target_pairs={{0,2},{2,4},{4,6},{6,0},{1,3},{3,5},{5,7},{7,1},{8,10},{10,12},{12... | collective-permute-start | bytes 2064392 | tf_op jit(solution)/shard_map/ppermute | solution.py:58
  104.1 114.9 %collective-permute-start.13 = (bf16[3,32,3584]{2,1,0:T(8,128)(2,1)}, bf16[3,32,3584]{2,1,0:T(8,128)(2,1)}, u32[]{:S(2)}, u32[]{:S(2)}) collective-permute-start(bf16[3,32,3584]{2,1,0:T(8,128)(2,1)} %get-tuple-element.30), channel_id=1, source_target_pairs={{0,4},{2,6},{4,0},{6,2},{1,5},{3,7},{5,1},{7,3},{8,12},{10,14},{12... | collective-permute-start | bytes 2064392 | tf_op jit(solution)/shard_map/ppermute | solution.py:58
  108.4 112.6 %collective-permute-start.14 = (bf16[3,32,3584]{2,1,0:T(8,128)(2,1)}, bf16[3,32,3584]{2,1,0:T(8,128)(2,1)}, u32[]{:S(2)}, u32[]{:S(2)}) collective-permute-start(bf16[3,32,3584]{2,1,0:T(8,128)(2,1)} %get-tuple-element.31), channel_id=1, source_target_pairs={{0,6},{2,0},{4,2},{6,4},{1,7},{3,1},{5,3},{7,5},{8,14},{10,8},{12,... | collective-permute-start | bytes 2064392 | tf_op jit(solution)/shard_map/ppermute | solution.py:58
  160.2 25.5 %collective-permute-start.8 = (bf16[128,3584]{1,0:T(8,128)(2,1)}, bf16[128,3584]{1,0:T(8,128)(2,1)}, u32[]{:S(2)}, u32[]{:S(2)}) collective-permute-start(bf16[128,3584]{1,0:T(8,128)(2,1)} %pad_maximum_fusion.4), channel_id=1, source_target_pairs={{0,48},{16,0},{32,16},{48,32},{1,49},{17,1},{33,17},{49,33},{2,50}... | collective-permute-start | bytes 2752520 | tf_op jit(solution)/shard_map/ppermute | solution.py:58
  162.5 27.0 %collective-permute-start.7 = (bf16[128,3584]{1,0:T(8,128)(2,1)}, bf16[128,3584]{1,0:T(8,128)(2,1)}, u32[]{:S(2)}, u32[]{:S(2)}) collective-permute-start(bf16[128,3584]{1,0:T(8,128)(2,1)} %pad_maximum_fusion.4), channel_id=1, source_target_pairs={{0,32},{16,48},{32,0},{48,16},{1,33},{17,49},{33,1},{49,17},{2,34}... | collective-permute-start | bytes 2752520 | tf_op jit(solution)/shard_map/ppermute | solution.py:58
  165.3 40.4 %collective-permute-start.6 = (bf16[128,3584]{1,0:T(8,128)(2,1)}, bf16[128,3584]{1,0:T(8,128)(2,1)}, u32[]{:S(2)}, u32[]{:S(2)}) collective-permute-start(bf16[128,3584]{1,0:T(8,128)(2,1)} %pad_maximum_fusion.4), channel_id=1, source_target_pairs={{0,16},{16,32},{32,48},{48,0},{1,17},{17,33},{33,49},{49,1},{2,18}... | collective-permute-start | bytes 2752520 | tf_op jit(solution)/shard_map/ppermute | solution.py:58
  168.3 1.1 copy-start.2
  206.1 15.3 %collective-permute-start.12 = (bf16[64,3584]{1,0:T(8,128)(2,1)S(1)}, bf16[64,3584]{1,0:T(8,128)(2,1)S(1)}, u32[]{:S(2)}, u32[]{:S(2)}) collective-permute-start(bf16[64,3584]{1,0:T(8,128)(2,1)S(1)} %fusion.35), channel_id=1, source_target_pairs={{0,48},{16,0},{32,16},{48,32},{1,49},{17,1},{33,17},{49,33},{2,50}... | collective-permute-start | bytes 1376264 | tf_op jit(solution)/shard_map/ppermute | solution.py:58
  208.6 16.9 %collective-permute-start.11 = (bf16[64,3584]{1,0:T(8,128)(2,1)S(1)}, bf16[64,3584]{1,0:T(8,128)(2,1)S(1)}, u32[]{:S(2)}, u32[]{:S(2)}) collective-permute-start(bf16[64,3584]{1,0:T(8,128)(2,1)S(1)} %fusion.35), channel_id=1, source_target_pairs={{0,32},{16,48},{32,0},{48,16},{1,33},{17,49},{33,1},{49,17},{2,34}... | collective-permute-start | bytes 1376264 | tf_op jit(solution)/shard_map/ppermute | solution.py:58
  211.3 22.4 %collective-permute-start.10 = (bf16[64,3584]{1,0:T(8,128)(2,1)S(1)}, bf16[64,3584]{1,0:T(8,128)(2,1)S(1)}, u32[]{:S(2)}, u32[]{:S(2)}) collective-permute-start(bf16[64,3584]{1,0:T(8,128)(2,1)S(1)} %fusion.35), channel_id=1, source_target_pairs={{0,16},{16,32},{32,48},{48,0},{1,17},{17,33},{33,49},{49,1},{2,18}... | collective-permute-start | bytes 1376264 | tf_op jit(solution)/shard_map/ppermute | solution.py:58
  216.5 2.6 copy-start.3
  219.1 18.9 %collective-permute-start.9 = (bf16[3,64,3584]{2,1,0:T(8,128)(2,1)S(1)}, bf16[3,64,3584]{2,1,0:T(8,128)(2,1)S(1)}, u32[]{:S(2)}, u32[]{:S(2)}) collective-permute-start(bf16[3,64,3584]{2,1,0:T(8,128)(2,1)S(1)} %copy-done.3), channel_id=1, source_target_pairs={{0,1},{1,0},{2,3},{3,2},{4,5},{5,4},{6,7},{7,6},{8,9},{9,8},{10,11... | collective-permute-start | bytes 4128776 | tf_op jit(solution)/shard_map/ppermute | solution.py:123
  236.0 5.0 %collective-permute-start.15 = (bf16[3,64,3584]{2,1,0:T(8,128)(2,1)S(1)}, bf16[3,64,3584]{2,1,0:T(8,128)(2,1)S(1)}, u32[]{:S(2)}, u32[]{:S(2)}) collective-permute-start(bf16[3,64,3584]{2,1,0:T(8,128)(2,1)S(1)} %constant_dynamic-update-slice_fusion.2), channel_id=1, source_target_pairs={{0,1},{1,0},{2,3},{3,2},{4,5},{5,4},{6,7},{7,6},{8,9},{9,8},{10,11... | collective-permute-start | bytes 4128776 | tf_op jit(solution)/shard_map/ppermute | solution.py:123
  246.5 26.6 %collective-permute-start.16 = (bf16[128,3584]{1,0:T(8,128)(2,1)S(1)}, bf16[128,3584]{1,0:T(8,128)(2,1)S(1)}, u32[]{:S(2)}, u32[]{:S(2)}) collective-permute-start(bf16[128,3584]{1,0:T(8,128)(2,1)S(1)} %pad_maximum_fusion.5), channel_id=1, source_target_pairs={{0,32},{16,48},{32,0},{48,16},{1,33},{17,49},{33,1},{49,17},{2,34}... | collective-permute-start | bytes 2752520 | tf_op jit(solution)/shard_map/ppermute | solution.py:58
  249.3 40.6 %collective-permute-start.17 = (bf16[128,3584]{1,0:T(8,128)(2,1)S(1)}, bf16[128,3584]{1,0:T(8,128)(2,1)S(1)}, u32[]{:S(2)}, u32[]{:S(2)}) collective-permute-start(bf16[128,3584]{1,0:T(8,128)(2,1)S(1)} %pad_maximum_fusion.6), channel_id=1, source_target_pairs={{0,48},{16,0},{32,16},{48,32},{1,49},{17,1},{33,17},{49,33},{2,50}... | collective-permute-start | bytes 2752520 | tf_op jit(solution)/shard_map/ppermute | solution.py:58
  252.5 39.5 %collective-permute-start.18 = (bf16[128,3584]{1,0:T(8,128)(2,1)S(1)}, bf16[128,3584]{1,0:T(8,128)(2,1)S(1)}, u32[]{:S(2)}, u32[]{:S(2)}) collective-permute-start(bf16[128,3584]{1,0:T(8,128)(2,1)S(1)} %pad_maximum_fusion.7), channel_id=1, source_target_pairs={{0,16},{16,32},{32,48},{48,0},{1,17},{17,33},{33,49},{49,1},{2,18}... | collective-permute-start | bytes 2752520 | tf_op jit(solution)/shard_map/ppermute | solution.py:58
  293.1 18.4 %copy-start.8 = (s32[1,64,1]{1,2,0:T(1,128)S(1)}, s32[1,64,1]{1,2,0:T(1,128)}, u32[]{:S(2)}) copy-start(s32[1,64,1]{1,2,0:T(1,128)} %param.13) | copy-start | bytes 772
  293.1 66.4 %copy-start.1 = (bf16[1,64,3584]{2,1,0:T(8,128)(2,1)S(1)}, bf16[1,64,3584]{2,1,0:T(8,128)(2,1)}, u32[]{:S(2)}) copy-start(bf16[1,64,3584]{2,1,0:T(8,128)(2,1)} %param.11) | copy-start | bytes 1376260
  294.2 63.2 %all-to-all-start.2 = ((bf16[8,16,3584]{2,1,0:T(8,128)(2,1)}), bf16[8,16,3584]{2,1,0:T(8,128)(2,1)S(1)}, u32[]{:S(2)}, u32[]{:S(2)}) async-start(bf16[8,16,3584]{2,1,0:T(8,128)(2,1)} %pad_maximum_fusion.8), calls=%async_computation.2 | async-start | bytes 1835008 | tf_op jit(solution)/shard_map/all_to_all | solution.py:203

commit v5 on v4

--- a/solution.py
+++ b/solution.py
@@ -62,14 +62,10 @@
     return [rows] + [rotated(rows, "x", j) for j in (1, 2, 3)]
 
 
-def scatter_sum_x(first, second):
-    def block(j):
-        rows = slice(j * ROWS, (j + 1) * ROWS)
-        return jnp.concatenate([first[rows], second[rows]], axis=0)
-
-    total = block(0).astype(jnp.float32)
+def scatter_sum_x(parts):
+    total = parts[:ROWS].astype(jnp.float32)
     for j in (2, 1, 3):
-        total = total + rotated(block(j), "x", -j).astype(jnp.float32)
+        total = total + rotated(parts[j * ROWS : (j + 1) * ROWS], "x", -j).astype(jnp.float32)
     return total
 
 
@@ -168,8 +164,8 @@
     normed_fwd, _ = normalize(section_input)
     normed_bwd, scale_bwd = normalize(got_saved[:, :features])
     rows = jnp.concatenate([normed_fwd, normed_bwd], axis=0).astype(jnp.bfloat16)
+    rows, blocks = lax.optimization_barrier((rows, blocks))
     blocks = weights_along_z(blocks)
-    rows, blocks[1] = lax.optimization_barrier((rows, blocks[1]))
     gathered = around_x(rows)
     send_cot = reorder(
         slot_matrix(mid_bwd), jnp.concatenate([cot_rows, gate_lanes(flat[3])], axis=1)
@@ -191,18 +187,19 @@
     parts_bwd = expert_grad(all_bwd, jnp.concatenate(all_gated, axis=0), gate_up, down).astype(
         jnp.bfloat16
     )
-    summed = scatter_sum_x(parts_fwd, parts_bwd)
-    summed_fwd, summed_bwd = summed[:ROWS], summed[ROWS:]
-    mixture = gate_of(got_fwd[:, features:]) * summed_fwd
+    def give_back(rows):
+        rows = rows.reshape(EXPERTS, DEPTH, features)
+        got = lax.all_to_all(rows, Z8, split_axis=0, concat_axis=0, tiled=True)
+        return got.reshape(ROWS, features)
+
+    summed = scatter_sum_x(parts_bwd)
+    projection = jnp.mean(normed_bwd * summed, axis=-1, keepdims=True)
+    grads = (cotangent + scale_bwd * (summed - normed_bwd * projection)).astype(jnp.bfloat16)
+    output_grad = reorder(home_bwd.T, give_back(grads))
+
+    mixture = gate_of(got_fwd[:, features:]) * scatter_sum_x(parts_fwd)
     acts = (section_input.astype(jnp.float32) + mixture).astype(jnp.bfloat16)
-    projection = jnp.mean(normed_bwd * summed_bwd, axis=-1, keepdims=True)
-    grads = (cotangent + scale_bwd * (summed_bwd - normed_bwd * projection)).astype(jnp.bfloat16)
-    back = jnp.concatenate(
-        [rows.reshape(EXPERTS, DEPTH, features) for rows in (acts, grads)], axis=1
-    )
-    back = lax.all_to_all(back, Z8, split_axis=0, concat_axis=0, tiled=True)
-    output_act = reorder(slot_matrix(own_fwd).T, back[:, :DEPTH].reshape(ROWS, features))
-    output_grad = reorder(home_bwd.T, back[:, DEPTH:].reshape(ROWS, features))
+    output_act = reorder(slot_matrix(own_fwd).T, give_back(acts))
     return (output_act[None], output_grad[None])
 
 

time: 361 us -> 319 us (0.88)
  waiting for transfers between devices: 217 us -> 142 us
  starting transfers between devices: 102 us -> 133 us
    ppermute x15 -> x18, waiting for transfers between devices: 158 us -> 107 us  [rotated(): lax.ppermute(x, axis, [(i, (i + by) % length) for i in range(length)])]
    all_to_all x1 -> x2, waiting for transfers between devices: 45.6 us -> 21.9 us  [give_back(): got = lax.all_to_all(rows, Z8, split_axis=0, concat_axis=0, tiled=True)]
    ppermute x15 -> x18, starting transfers between devices: 46.1 us -> 62 us  [rotated(): lax.ppermute(x, axis, [(i, (i + by) % length) for i in range(length)])]
    all_to_all x1 -> x2, starting transfers between devices: 17.4 us -> 31.7 us  [give_back(): got = lax.all_to_all(rows, Z8, split_axis=0, concat_axis=0, tiled=True)]
  transfers between devices with their start and end apart: 22 -> 26, of which waited for: 15 -> 14; matrix products, arithmetic and copies ran while one was open for 7% -> 9% of each run, Pallas kernels for 0% -> 0%
where the time goes in v5:
time: 319 us; the launch traced here: 316 us
  waiting for transfers between devices  142 us (45%)
  starting transfers between devices  133 us (42%)
  other arithmetic  17.5 us (5%)
  local copies, waits for them, and re-layouts  13.3 us (4%)
  matrix products  8.75 us (3%)
    ppermute x18, waiting for transfers between devices, rotated(): lax.ppermute(x, axis, [(i, (i + by) % length) for i in range(length)])  107 us
    ppermute x18, starting transfers between devices, rotated(): lax.ppermute(x, axis, [(i, (i + by) % length) for i in range(length)])  62 us
    all_to_all x2, starting transfers between devices, give_back(): got = lax.all_to_all(rows, Z8, split_axis=0, concat_axis=0, tiled=True)  31.7 us
    all_to_all x2, waiting for transfers between devices, give_back(): got = lax.all_to_all(rows, Z8, split_axis=0, concat_axis=0, tiled=True)  21.9 us
    all_to_all x2, starting transfers between devices, dispatch(): return lax.all_to_all(both, Z16, split_axis=0, concat_axis=0, tiled=True)  16.8 us
    ppermute x1, starting transfers between devices, body(): flat = lax.ppermute(flat, 'zh', [(0, 1), (1, 0)])  15.7 us
    ppermute x1, waiting for transfers between devices, body(): along_y = lax.ppermute(along_y, PP, moves)  9.99 us
  transfers between devices with their start and end apart: 26, of which 14 were waited for; matrix products, arithmetic and copies ran while one was open for 9% of the time, Pallas kernels for 0%

profile of v5, /device:TPU:24, one launch (start us, length us, event | category | flops | bytes accessed | tf_op | source)
XLA Modules:
  0.0 315.8 jit_solution(14904246639276012622)
XLA Ops:
  2.1 15.7 %collective-permute-start = (f32[4,64]{1,0:T(4,128)S(1)}, f32[4,64]{1,0:T(4,128)S(1)}, u32[]{:S(2)}, u32[]{:S(2)}) collective-permute-start(f32[4,64]{1,0:T(4,128)S(1)} %pad_maximum_fusion.7), channel_id=1, source_target_pairs={{0,64},{64,0},{1,65},{65,1},{2,66},{66,2},{3,67},{67,3},{4,68},{68... | collective-permute-start | bytes 3080 | tf_op jit(solution)/shard_map/ppermute | solution.py:138
  24.1 10.0 %collective-permute-done.1 = bf16[64,3584]{1,0:T(8,128)(2,1)S(1)} collective-permute-done((bf16[64,3584]{1,0:T(8,128)(2,1)S(1)}, bf16[64,3584]{1,0:T(8,128)(2,1)S(1)}, u32[]{:S(2)}, u32[]{:S(2)}) %collective-permute-start.1) | collective-permute-done | bytes 458784 | tf_op jit(solution)/shard_map/ppermute | solution.py:137
  37.4 5.1 %all-to-all-start = ((bf16[16,8,3712]{2,1,0:T(8,128)(2,1)}), bf16[16,8,3712]{2,1,0:T(8,128)(2,1)S(1)}, u32[]{:S(2)}, u32[]{:S(2)}) async-start(bf16[16,8,3712]{2,1,0:T(8,128)(2,1)} %maximum_bitcast_fusion), calls=%async_computation | async-start | bytes 1900544 | tf_op jit(solution)/shard_map/all_to_all | solution.py:149
  47.1 4.7 %collective-permute-start.4 = (bf16[3,32,3584]{2,1,0:T(8,128)(2,1)}, bf16[3,32,3584]{2,1,0:T(8,128)(2,1)}, u32[]{:S(2)}, u32[]{:S(2)}) collective-permute-start(bf16[3,32,3584]{2,1,0:T(8,128)(2,1)} %get-tuple-element.49), channel_id=1, source_target_pairs={{0,48},{16,0},{32,16},{48,32},{1,49},{17,1},{33,17},{49,33},{2,50}... | collective-permute-start | bytes 2064392 | tf_op jit(solution)/shard_map/ppermute | solution.py:58
  54.5 2.8 collective-permute-start.2
  59.8 20.3 %collective-permute-done.4 = bf16[3,32,3584]{2,1,0:T(8,128)(2,1)} collective-permute-done((bf16[3,32,3584]{2,1,0:T(8,128)(2,1)}, bf16[3,32,3584]{2,1,0:T(8,128)(2,1)}, u32[]{:S(2)}, u32[]{:S(2)}) %collective-permute-start.4) | collective-permute-done | bytes 688160 | tf_op jit(solution)/shard_map/ppermute | solution.py:58
  80.1 5.4 %collective-permute-done.2 = bf16[3,32,3584]{2,1,0:T(8,128)(2,1)} collective-permute-done((bf16[3,32,3584]{2,1,0:T(8,128)(2,1)S(1)}, bf16[3,32,3584]{2,1,0:T(8,128)(2,1)}, u32[]{:S(2)}, u32[]{:S(2)}) %collective-permute-start.2) | collective-permute-done | bytes 688160 | tf_op jit(solution)/shard_map/ppermute | solution.py:58
  88.5 11.7 %all-to-all-start.1 = ((bf16[16,8,3712]{2,1,0:T(8,128)(2,1)}), bf16[16,8,3712]{2,1,0:T(8,128)(2,1)S(1)}, u32[]{:S(2)}, u32[]{:S(2)}) async-start(bf16[16,8,3712]{2,1,0:T(8,128)(2,1)} %maximum_bitcast_fusion.1), calls=%async_computation.1 | async-start | bytes 1900544 | tf_op jit(solution)/shard_map/all_to_all | solution.py:149
  102.1 3.8 %collective-permute-start.8 = (bf16[3,32,3584]{2,1,0:T(8,128)(2,1)S(1)}, bf16[3,32,3584]{2,1,0:T(8,128)(2,1)S(1)}, u32[]{:S(2)}, u32[]{:S(2)}) collective-permute-start(bf16[3,32,3584]{2,1,0:T(8,128)(2,1)S(1)} %copy-done.5), channel_id=1, source_target_pairs={{0,2},{2,4},{4,6},{6,0},{1,3},{3,5},{5,7},{7,1},{8,10},{10,12},{12... | collective-permute-start | bytes 2064392 | tf_op jit(solution)/shard_map/ppermute | solution.py:58
  107.8 4.0 %collective-permute-start.6 = (bf16[128,3584]{1,0:T(8,128)(2,1)}, bf16[128,3584]{1,0:T(8,128)(2,1)}, u32[]{:S(2)}, u32[]{:S(2)}) collective-permute-start(bf16[128,3584]{1,0:T(8,128)(2,1)} %pad_maximum_fusion.4), channel_id=1, source_target_pairs={{0,32},{16,48},{32,0},{48,16},{1,33},{17,49},{33,1},{49,17},{2,34}... | collective-permute-start | bytes 2752520 | tf_op jit(solution)/shard_map/ppermute | solution.py:58
  111.8 3.3 %collective-permute-start.7 = (bf16[128,3584]{1,0:T(8,128)(2,1)}, bf16[128,3584]{1,0:T(8,128)(2,1)}, u32[]{:S(2)}, u32[]{:S(2)}) collective-permute-start(bf16[128,3584]{1,0:T(8,128)(2,1)} %pad_maximum_fusion.4), channel_id=1, source_target_pairs={{0,48},{16,0},{32,16},{48,32},{1,49},{17,1},{33,17},{49,33},{2,50}... | collective-permute-start | bytes 2752520 | tf_op jit(solution)/shard_map/ppermute | solution.py:58
  115.1 4.3 %collective-permute-start.13 = (bf16[3,32,3584]{2,1,0:T(8,128)(2,1)}, bf16[3,32,3584]{2,1,0:T(8,128)(2,1)}, u32[]{:S(2)}, u32[]{:S(2)}) collective-permute-start(bf16[3,32,3584]{2,1,0:T(8,128)(2,1)} %get-tuple-element.36), channel_id=1, source_target_pairs={{0,4},{2,6},{4,0},{6,2},{1,5},{3,7},{5,1},{7,3},{8,12},{10,14},{12... | collective-permute-start | bytes 2064392 | tf_op jit(solution)/shard_map/ppermute | solution.py:58
  119.4 41.9 %collective-permute-done.8 = bf16[3,32,3584]{2,1,0:T(8,128)(2,1)S(1)} collective-permute-done((bf16[3,32,3584]{2,1,0:T(8,128)(2,1)S(1)}, bf16[3,32,3584]{2,1,0:T(8,128)(2,1)S(1)}, u32[]{:S(2)}, u32[]{:S(2)}) %collective-permute-start.8) | collective-permute-done | bytes 688160 | tf_op jit(solution)/shard_map/ppermute | solution.py:58
  167.5 3.8 %collective-permute-start.11 = (bf16[64,3584]{1,0:T(8,128)(2,1)S(1)}, bf16[64,3584]{1,0:T(8,128)(2,1)S(1)}, u32[]{:S(2)}, u32[]{:S(2)}) collective-permute-start(bf16[64,3584]{1,0:T(8,128)(2,1)S(1)} %fusion.35), channel_id=1, source_target_pairs={{0,32},{16,48},{32,0},{48,16},{1,33},{17,49},{33,1},{49,17},{2,34}... | collective-permute-start | bytes 1376264 | tf_op jit(solution)/shard_map/ppermute | solution.py:58
  171.3 3.5 %collective-permute-start.12 = (bf16[64,3584]{1,0:T(8,128)(2,1)S(1)}, bf16[64,3584]{1,0:T(8,128)(2,1)S(1)}, u32[]{:S(2)}, u32[]{:S(2)}) collective-permute-start(bf16[64,3584]{1,0:T(8,128)(2,1)S(1)} %fusion.35), channel_id=1, source_target_pairs={{0,48},{16,0},{32,16},{48,32},{1,49},{17,1},{33,17},{49,33},{2,50}... | collective-permute-start | bytes 1376264 | tf_op jit(solution)/shard_map/ppermute | solution.py:58
  179.8 10.1 %collective-permute-done.13 = bf16[3,32,3584]{2,1,0:T(8,128)(2,1)} collective-permute-done((bf16[3,32,3584]{2,1,0:T(8,128)(2,1)}, bf16[3,32,3584]{2,1,0:T(8,128)(2,1)}, u32[]{:S(2)}, u32[]{:S(2)}) %collective-permute-start.13) | collective-permute-done | bytes 688160 | tf_op jit(solution)/shard_map/ppermute | solution.py:58
  195.7 2.9 collective-permute-done.15
  202.1 6.2 %collective-permute-start.21 = (bf16[64,3584]{1,0:T(8,128)(2,1)S(1)}, bf16[64,3584]{1,0:T(8,128)(2,1)S(1)}, u32[]{:S(2)}, u32[]{:S(2)}) collective-permute-start(bf16[64,3584]{1,0:T(8,128)(2,1)S(1)} %get-tuple-element.53), channel_id=1, source_target_pairs={{0,16},{16,32},{32,48},{48,0},{1,17},{17,33},{33,49},{49,1},{2,18}... | collective-permute-start | bytes 1376264 | tf_op jit(solution)/shard_map/ppermute | solution.py:58
  208.2 3.2 %collective-permute-start.20 = (bf16[64,3584]{1,0:T(8,128)(2,1)S(1)}, bf16[64,3584]{1,0:T(8,128)(2,1)S(1)}, u32[]{:S(2)}, u32[]{:S(2)}) collective-permute-start(bf16[64,3584]{1,0:T(8,128)(2,1)S(1)} %get-tuple-element.54), channel_id=1, source_target_pairs={{0,48},{16,0},{32,16},{48,32},{1,49},{17,1},{33,17},{49,33},{2,50}... | collective-permute-start | bytes 1376264 | tf_op jit(solution)/shard_map/ppermute | solution.py:58
  211.4 3.4 %collective-permute-start.19 = (bf16[64,3584]{1,0:T(8,128)(2,1)S(1)}, bf16[64,3584]{1,0:T(8,128)(2,1)S(1)}, u32[]{:S(2)}, u32[]{:S(2)}) collective-permute-start(bf16[64,3584]{1,0:T(8,128)(2,1)S(1)} %get-tuple-element.52), channel_id=1, source_target_pairs={{0,32},{16,48},{32,0},{48,16},{1,33},{17,49},{33,1},{49,17},{2,34}... | collective-permute-start | bytes 1376264 | tf_op jit(solution)/shard_map/ppermute | solution.py:58
  216.6 3.7 %collective-permute-done.21 = bf16[64,3584]{1,0:T(8,128)(2,1)S(1)} collective-permute-done((bf16[64,3584]{1,0:T(8,128)(2,1)S(1)}, bf16[64,3584]{1,0:T(8,128)(2,1)S(1)}, u32[]{:S(2)}, u32[]{:S(2)}) %collective-permute-start.21) | collective-permute-done | bytes 458784 | tf_op jit(solution)/shard_map/ppermute | solution.py:58
  220.3 3.2 %collective-permute-done.20 = bf16[64,3584]{1,0:T(8,128)(2,1)S(1)} collective-permute-done((bf16[64,3584]{1,0:T(8,128)(2,1)S(1)}, bf16[64,3584]{1,0:T(8,128)(2,1)S(1)}, u32[]{:S(2)}, u32[]{:S(2)}) %collective-permute-start.20) | collective-permute-done | bytes 458784 | tf_op jit(solution)/shard_map/ppermute | solution.py:58
  223.5 7.8 %collective-permute-done.19 = bf16[64,3584]{1,0:T(8,128)(2,1)S(1)} collective-permute-done((bf16[64,3584]{1,0:T(8,128)(2,1)S(1)}, bf16[64,3584]{1,0:T(8,128)(2,1)S(1)}, u32[]{:S(2)}, u32[]{:S(2)}) %collective-permute-start.19) | collective-permute-done | bytes 458784 | tf_op jit(solution)/shard_map/ppermute | solution.py:58
  233.0 22.1 %all-to-all-start.3 = ((bf16[8,8,3584]{2,1,0:T(8,128)(2,1)}), bf16[8,8,3584]{2,1,0:T(8,128)(2,1)S(1)}, u32[]{:S(2)}, u32[]{:S(2)}) async-start(bf16[8,8,3584]{2,1,0:T(8,128)(2,1)} %fusion.51), calls=%async_computation.3 | async-start | bytes 917504 | tf_op jit(solution)/shard_map/all_to_all | solution.py:192
  255.1 4.6 %collective-permute-start.18 = (bf16[64,3584]{1,0:T(8,128)(2,1)S(1)}, bf16[64,3584]{1,0:T(8,128)(2,1)S(1)}, u32[]{:S(2)}, u32[]{:S(2)}) collective-permute-start(bf16[64,3584]{1,0:T(8,128)(2,1)S(1)} %get-tuple-element.56), channel_id=1, source_target_pairs={{0,16},{16,32},{32,48},{48,0},{1,17},{17,33},{33,49},{49,1},{2,18}... | collective-permute-start | bytes 1376264 | tf_op jit(solution)/shard_map/ppermute | solution.py:58
  259.7 2.9 collective-permute-start.17
  262.6 3.4 %collective-permute-start.16 = (bf16[64,3584]{1,0:T(8,128)(2,1)S(1)}, bf16[64,3584]{1,0:T(8,128)(2,1)S(1)}, u32[]{:S(2)}, u32[]{:S(2)}) collective-permute-start(bf16[64,3584]{1,0:T(8,128)(2,1)S(1)} %get-tuple-element.55), channel_id=1, source_target_pairs={{0,32},{16,48},{32,0},{48,16},{1,33},{17,49},{33,1},{49,17},{2,34}... | collective-permute-start | bytes 1376264 | tf_op jit(solution)/shard_map/ppermute | solution.py:58
  266.2 5.0 %collective-permute-done.18 = bf16[64,3584]{1,0:T(8,128)(2,1)S(1)} collective-permute-done((bf16[64,3584]{1,0:T(8,128)(2,1)S(1)}, bf16[64,3584]{1,0:T(8,128)(2,1)S(1)}, u32[]{:S(2)}, u32[]{:S(2)}) %collective-permute-start.18) | collective-permute-done | bytes 458784 | tf_op jit(solution)/shard_map/ppermute | solution.py:58
  271.2 3.9 %collective-permute-done.17 = bf16[64,3584]{1,0:T(8,128)(2,1)S(1)} collective-permute-done((bf16[64,3584]{1,0:T(8,128)(2,1)S(1)}, bf16[64,3584]{1,0:T(8,128)(2,1)S(1)}, u32[]{:S(2)}, u32[]{:S(2)}) %collective-permute-start.17) | collective-permute-done | bytes 458784 | tf_op jit(solution)/shard_map/ppermute | solution.py:58
  275.1 5.6 %collective-permute-done.16 = bf16[64,3584]{1,0:T(8,128)(2,1)S(1)} collective-permute-done((bf16[64,3584]{1,0:T(8,128)(2,1)S(1)}, bf16[64,3584]{1,0:T(8,128)(2,1)S(1)}, u32[]{:S(2)}, u32[]{:S(2)}) %collective-permute-start.16) | collective-permute-done | bytes 458784 | tf_op jit(solution)/shard_map/ppermute | solution.py:58
  281.8 9.6 %all-to-all-start.2 = ((bf16[8,8,3584]{2,1,0:T(8,128)(2,1)}), bf16[8,8,3584]{2,1,0:T(8,128)(2,1)S(1)}, u32[]{:S(2)}, u32[]{:S(2)}) async-start(bf16[8,8,3584]{2,1,0:T(8,128)(2,1)} %fusion.50), calls=%async_computation.2 | async-start | bytes 917504 | tf_op jit(solution)/shard_map/all_to_all | solution.py:192
  292.8 21.9 %all-to-all-done.2 = bf16[8,8,3584]{2,1,0:T(8,128)(2,1)S(1)} async-done(((bf16[8,8,3584]{2,1,0:T(8,128)(2,1)}), bf16[8,8,3584]{2,1,0:T(8,128)(2,1)S(1)}, u32[]{:S(2)}, u32[]{:S(2)}) %all-to-all-start.2) | async-done | bytes 458784 | tf_op jit(solution)/shard_map/all_to_all | solution.py:192
  (109 shorter events, 55.0 us)
Async XLA Ops:
  0.6 22.6 %copy-start = (bf16[1,64,3584]{2,1,0:T(8,128)(2,1)S(1)}, bf16[1,64,3584]{2,1,0:T(8,128)(2,1)}, u32[]{:S(2)}) copy-start(bf16[1,64,3584]{2,1,0:T(8,128)(2,1)} %param.11) | copy-start | bytes 1376260
  2.1 21.5 %collective-permute-start = (f32[4,64]{1,0:T(4,128)S(1)}, f32[4,64]{1,0:T(4,128)S(1)}, u32[]{:S(2)}, u32[]{:S(2)}) collective-permute-start(f32[4,64]{1,0:T(4,128)S(1)} %pad_maximum_fusion.7), channel_id=1, source_target_pairs={{0,64},{64,0},{1,65},{65,1},{2,66},{66,2},{3,67},{67,3},{4,68},{68... | collective-permute-start | bytes 3080 | tf_op jit(solution)/shard_map/ppermute | solution.py:138
  19.0 15.1 %collective-permute-start.1 = (bf16[64,3584]{1,0:T(8,128)(2,1)S(1)}, bf16[64,3584]{1,0:T(8,128)(2,1)S(1)}, u32[]{:S(2)}, u32[]{:S(2)}) collective-permute-start(bf16[64,3584]{1,0:T(8,128)(2,1)S(1)} %bitcast_select_fusion.1), channel_id=1, source_target_pairs={{64,192},{0,384},{192,320},{128,0},{320,448},{256,128},{448,64},{3... | collective-permute-start | bytes 1376264 | tf_op jit(solution)/shard_map/ppermute | solution.py:137
  36.1 6.5 %copy-start.4 = (bf16[1,1,3584,128]{3,2,1,0:T(8,128)(2,1)S(1)}, bf16[1,1,3584,128]{3,2,1,0:T(8,128)(2,1)}, u32[]{:S(2)}) copy-start(bf16[1,1,3584,128]{3,2,1,0:T(8,128)(2,1)} %param.18) | copy-start | bytes 2752516
  37.4 51.2 %all-to-all-start = ((bf16[16,8,3712]{2,1,0:T(8,128)(2,1)}), bf16[16,8,3712]{2,1,0:T(8,128)(2,1)S(1)}, u32[]{:S(2)}, u32[]{:S(2)}) async-start(bf16[16,8,3712]{2,1,0:T(8,128)(2,1)} %maximum_bitcast_fusion), calls=%async_computation | async-start | bytes 1900544 | tf_op jit(solution)/shard_map/all_to_all | solution.py:149
  47.1 32.9 %collective-permute-start.4 = (bf16[3,32,3584]{2,1,0:T(8,128)(2,1)}, bf16[3,32,3584]{2,1,0:T(8,128)(2,1)}, u32[]{:S(2)}, u32[]{:S(2)}) collective-permute-start(bf16[3,32,3584]{2,1,0:T(8,128)(2,1)} %get-tuple-element.49), channel_id=1, source_target_pairs={{0,48},{16,0},{32,16},{48,32},{1,49},{17,1},{33,17},{49,33},{2,50}... | collective-permute-start | bytes 2064392 | tf_op jit(solution)/shard_map/ppermute | solution.py:58
  51.8 28.3 %collective-permute-start.3 = (bf16[3,32,3584]{2,1,0:T(8,128)(2,1)S(1)}, bf16[3,32,3584]{2,1,0:T(8,128)(2,1)}, u32[]{:S(2)}, u32[]{:S(2)}) collective-permute-start(bf16[3,32,3584]{2,1,0:T(8,128)(2,1)S(1)} %get-tuple-element.50), channel_id=1, source_target_pairs={{0,32},{16,48},{32,0},{48,16},{1,33},{17,49},{33,1},{49,17},{2,34}... | collective-permute-start | bytes 2064392 | tf_op jit(solution)/shard_map/ppermute | solution.py:58
  54.5 31.0 %collective-permute-start.2 = (bf16[3,32,3584]{2,1,0:T(8,128)(2,1)S(1)}, bf16[3,32,3584]{2,1,0:T(8,128)(2,1)}, u32[]{:S(2)}, u32[]{:S(2)}) collective-permute-start(bf16[3,32,3584]{2,1,0:T(8,128)(2,1)S(1)} %get-tuple-element.51), channel_id=1, source_target_pairs={{0,16},{16,32},{32,48},{48,0},{1,17},{17,33},{33,49},{49,1},{2,18}... | collective-permute-start | bytes 2064392 | tf_op jit(solution)/shard_map/ppermute | solution.py:58
  88.5 76.6 %all-to-all-start.1 = ((bf16[16,8,3712]{2,1,0:T(8,128)(2,1)}), bf16[16,8,3712]{2,1,0:T(8,128)(2,1)S(1)}, u32[]{:S(2)}, u32[]{:S(2)}) async-start(bf16[16,8,3712]{2,1,0:T(8,128)(2,1)} %maximum_bitcast_fusion.1), calls=%async_computation.1 | async-start | bytes 1900544 | tf_op jit(solution)/shard_map/all_to_all | solution.py:149
  100.3 1.7 copy-start.5
  102.1 59.2 %collective-permute-start.8 = (bf16[3,32,3584]{2,1,0:T(8,128)(2,1)S(1)}, bf16[3,32,3584]{2,1,0:T(8,128)(2,1)S(1)}, u32[]{:S(2)}, u32[]{:S(2)}) collective-permute-start(bf16[3,32,3584]{2,1,0:T(8,128)(2,1)S(1)} %copy-done.5), channel_id=1, source_target_pairs={{0,2},{2,4},{4,6},{6,0},{1,3},{3,5},{5,7},{7,1},{8,10},{10,12},{12... | collective-permute-start | bytes 2064392 | tf_op jit(solution)/shard_map/ppermute | solution.py:58
  105.9 59.3 %collective-permute-start.5 = (bf16[128,3584]{1,0:T(8,128)(2,1)}, bf16[128,3584]{1,0:T(8,128)(2,1)}, u32[]{:S(2)}, u32[]{:S(2)}) collective-permute-start(bf16[128,3584]{1,0:T(8,128)(2,1)} %pad_maximum_fusion.4), channel_id=1, source_target_pairs={{0,16},{16,32},{32,48},{48,0},{1,17},{17,33},{33,49},{49,1},{2,18}... | collective-permute-start | bytes 2752520 | tf_op jit(solution)/shard_map/ppermute | solution.py:58
  107.8 57.3 %collective-permute-start.6 = (bf16[128,3584]{1,0:T(8,128)(2,1)}, bf16[128,3584]{1,0:T(8,128)(2,1)}, u32[]{:S(2)}, u32[]{:S(2)}) collective-permute-start(bf16[128,3584]{1,0:T(8,128)(2,1)} %pad_maximum_fusion.4), channel_id=1, source_target_pairs={{0,32},{16,48},{32,0},{48,16},{1,33},{17,49},{33,1},{49,17},{2,34}... | collective-permute-start | bytes 2752520 | tf_op jit(solution)/shard_map/ppermute | solution.py:58
  111.8 53.4 %collective-permute-start.7 = (bf16[128,3584]{1,0:T(8,128)(2,1)}, bf16[128,3584]{1,0:T(8,128)(2,1)}, u32[]{:S(2)}, u32[]{:S(2)}) collective-permute-start(bf16[128,3584]{1,0:T(8,128)(2,1)} %pad_maximum_fusion.4), channel_id=1, source_target_pairs={{0,48},{16,0},{32,16},{48,32},{1,49},{17,1},{33,17},{49,33},{2,50}... | collective-permute-start | bytes 2752520 | tf_op jit(solution)/shard_map/ppermute | solution.py:58
  115.1 74.8 %collective-permute-start.13 = (bf16[3,32,3584]{2,1,0:T(8,128)(2,1)}, bf16[3,32,3584]{2,1,0:T(8,128)(2,1)}, u32[]{:S(2)}, u32[]{:S(2)}) collective-permute-start(bf16[3,32,3584]{2,1,0:T(8,128)(2,1)} %get-tuple-element.36), channel_id=1, source_target_pairs={{0,4},{2,6},{4,0},{6,2},{1,5},{3,7},{5,1},{7,3},{8,12},{10,14},{12... | collective-permute-start | bytes 2064392 | tf_op jit(solution)/shard_map/ppermute | solution.py:58
  161.3 31.1 %collective-permute-start.14 = (bf16[3,32,3584]{2,1,0:T(8,128)(2,1)}, bf16[3,32,3584]{2,1,0:T(8,128)(2,1)S(1)}, u32[]{:S(2)}, u32[]{:S(2)}) collective-permute-start(bf16[3,32,3584]{2,1,0:T(8,128)(2,1)} %get-tuple-element.37), channel_id=1, source_target_pairs={{0,6},{2,0},{4,2},{6,4},{1,7},{3,1},{5,3},{7,5},{8,14},{10,8},{12,... | collective-permute-start | bytes 2064392 | tf_op jit(solution)/shard_map/ppermute | solution.py:58
  165.6 26.7 %collective-permute-start.10 = (bf16[64,3584]{1,0:T(8,128)(2,1)S(1)}, bf16[64,3584]{1,0:T(8,128)(2,1)S(1)}, u32[]{:S(2)}, u32[]{:S(2)}) collective-permute-start(bf16[64,3584]{1,0:T(8,128)(2,1)S(1)} %fusion.35), channel_id=1, source_target_pairs={{0,16},{16,32},{32,48},{48,0},{1,17},{17,33},{33,49},{49,1},{2,18}... | collective-permute-start | bytes 1376264 | tf_op jit(solution)/shard_map/ppermute | solution.py:58
  167.5 24.8 %collective-permute-start.11 = (bf16[64,3584]{1,0:T(8,128)(2,1)S(1)}, bf16[64,3584]{1,0:T(8,128)(2,1)S(1)}, u32[]{:S(2)}, u32[]{:S(2)}) collective-permute-start(bf16[64,3584]{1,0:T(8,128)(2,1)S(1)} %fusion.35), channel_id=1, source_target_pairs={{0,32},{16,48},{32,0},{48,16},{1,33},{17,49},{33,1},{49,17},{2,34}... | collective-permute-start | bytes 1376264 | tf_op jit(solution)/shard_map/ppermute | solution.py:58
  171.3 21.1 %collective-permute-start.12 = (bf16[64,3584]{1,0:T(8,128)(2,1)S(1)}, bf16[64,3584]{1,0:T(8,128)(2,1)S(1)}, u32[]{:S(2)}, u32[]{:S(2)}) collective-permute-start(bf16[64,3584]{1,0:T(8,128)(2,1)S(1)} %fusion.35), channel_id=1, source_target_pairs={{0,48},{16,0},{32,16},{48,32},{1,49},{17,1},{33,17},{49,33},{2,50}... | collective-permute-start | bytes 1376264 | tf_op jit(solution)/shard_map/ppermute | solution.py:58
  176.0 13.9 %copy-start.3 = (bf16[3,64,3584]{2,1,0:T(8,128)(2,1)S(1)}, bf16[3,64,3584]{2,1,0:T(8,128)(2,1)}, u32[]{:S(2)}) copy-start(bf16[3,64,3584]{2,1,0:T(8,128)(2,1)} %copy-done.2) | copy-start | bytes 4128772
  189.9 5.7 %collective-permute-start.9 = (bf16[3,64,3584]{2,1,0:T(8,128)(2,1)S(1)}, bf16[3,64,3584]{2,1,0:T(8,128)(2,1)S(1)}, u32[]{:S(2)}, u32[]{:S(2)}) collective-permute-start(bf16[3,64,3584]{2,1,0:T(8,128)(2,1)S(1)} %copy-done.3), channel_id=1, source_target_pairs={{0,1},{1,0},{2,3},{3,2},{4,5},{5,4},{6,7},{7,6},{8,9},{9,8},{10,11... | collective-permute-start | bytes 4128776 | tf_op jit(solution)/shard_map/ppermute | solution.py:119
  193.6 5.0 %collective-permute-start.15 = (bf16[3,64,3584]{2,1,0:T(8,128)(2,1)S(1)}, bf16[3,64,3584]{2,1,0:T(8,128)(2,1)S(1)}, u32[]{:S(2)}, u32[]{:S(2)}) collective-permute-start(bf16[3,64,3584]{2,1,0:T(8,128)(2,1)S(1)} %constant_dynamic-update-slice_fusion.2), channel_id=1, source_target_pairs={{0,1},{1,0},{2,3},{3,2},{4,5},{5,4},{6,7},{7,6},{8,9},{9,8},{10,11... | collective-permute-start | bytes 4128776 | tf_op jit(solution)/shard_map/ppermute | solution.py:119
  202.1 18.2 %collective-permute-start.21 = (bf16[64,3584]{1,0:T(8,128)(2,1)S(1)}, bf16[64,3584]{1,0:T(8,128)(2,1)S(1)}, u32[]{:S(2)}, u32[]{:S(2)}) collective-permute-start(bf16[64,3584]{1,0:T(8,128)(2,1)S(1)} %get-tuple-element.53), channel_id=1, source_target_pairs={{0,16},{16,32},{32,48},{48,0},{1,17},{17,33},{33,49},{49,1},{2,18}... | collective-permute-start | bytes 1376264 | tf_op jit(solution)/shard_map/ppermute | solution.py:58
  208.2 15.3 %collective-permute-start.20 = (bf16[64,3584]{1,0:T(8,128)(2,1)S(1)}, bf16[64,3584]{1,0:T(8,128)(2,1)S(1)}, u32[]{:S(2)}, u32[]{:S(2)}) collective-permute-start(bf16[64,3584]{1,0:T(8,128)(2,1)S(1)} %get-tuple-element.54), channel_id=1, source_target_pairs={{0,48},{16,0},{32,16},{48,32},{1,49},{17,1},{33,17},{49,33},{2,50}... | collective-permute-start | bytes 1376264 | tf_op jit(solution)/shard_map/ppermute | solution.py:58
  211.4 19.9 %collective-permute-start.19 = (bf16[64,3584]{1,0:T(8,128)(2,1)S(1)}, bf16[64,3584]{1,0:T(8,128)(2,1)S(1)}, u32[]{:S(2)}, u32[]{:S(2)}) collective-permute-start(bf16[64,3584]{1,0:T(8,128)(2,1)S(1)} %get-tuple-element.52), channel_id=1, source_target_pairs={{0,32},{16,48},{32,0},{48,16},{1,33},{17,49},{33,1},{49,17},{2,34}... | collective-permute-start | bytes 1376264 | tf_op jit(solution)/shard_map/ppermute | solution.py:58
  233.0 48.9 %all-to-all-start.3 = ((bf16[8,8,3584]{2,1,0:T(8,128)(2,1)}), bf16[8,8,3584]{2,1,0:T(8,128)(2,1)S(1)}, u32[]{:S(2)}, u32[]{:S(2)}) async-start(bf16[8,8,3584]{2,1,0:T(8,128)(2,1)} %fusion.51), calls=%async_computation.3 | async-start | bytes 917504 | tf_op jit(solution)/shard_map/all_to_all | solution.py:192
  255.0 36.5 %copy-start.7 = (s32[1,64,1]{1,2,0:T(1,128)S(1)}, s32[1,64,1]{1,2,0:T(1,128)}, u32[]{:S(2)}) copy-start(s32[1,64,1]{1,2,0:T(1,128)} %param.13) | copy-start | bytes 772
  255.1 16.1 %collective-permute-start.18 = (bf16[64,3584]{1,0:T(8,128)(2,1)S(1)}, bf16[64,3584]{1,0:T(8,128)(2,1)S(1)}, u32[]{:S(2)}, u32[]{:S(2)}) collective-permute-start(bf16[64,3584]{1,0:T(8,128)(2,1)S(1)} %get-tuple-element.56), channel_id=1, source_target_pairs={{0,16},{16,32},{32,48},{48,0},{1,17},{17,33},{33,49},{49,1},{2,18}... | collective-permute-start | bytes 1376264 | tf_op jit(solution)/shard_map/ppermute | solution.py:58
  259.7 15.3 %collective-permute-start.17 = (bf16[64,3584]{1,0:T(8,128)(2,1)S(1)}, bf16[64,3584]{1,0:T(8,128)(2,1)S(1)}, u32[]{:S(2)}, u32[]{:S(2)}) collective-permute-start(bf16[64,3584]{1,0:T(8,128)(2,1)S(1)} %get-tuple-element.57), channel_id=1, source_target_pairs={{0,48},{16,0},{32,16},{48,32},{1,49},{17,1},{33,17},{49,33},{2,50}... | collective-permute-start | bytes 1376264 | tf_op jit(solution)/shard_map/ppermute | solution.py:58
  262.6 18.1 %collective-permute-start.16 = (bf16[64,3584]{1,0:T(8,128)(2,1)S(1)}, bf16[64,3584]{1,0:T(8,128)(2,1)S(1)}, u32[]{:S(2)}, u32[]{:S(2)}) collective-permute-start(bf16[64,3584]{1,0:T(8,128)(2,1)S(1)} %get-tuple-element.55), channel_id=1, source_target_pairs={{0,32},{16,48},{32,0},{48,16},{1,33},{17,49},{33,1},{49,17},{2,34}... | collective-permute-start | bytes 1376264 | tf_op jit(solution)/shard_map/ppermute | solution.py:58
  266.0 49.8 %copy-start.1 = (bf16[1,64,3584]{2,1,0:T(8,128)(2,1)S(1)}, bf16[1,64,3584]{2,1,0:T(8,128)(2,1)}, u32[]{:S(2)}) copy-start(bf16[1,64,3584]{2,1,0:T(8,128)(2,1)} %param.11) | copy-start | bytes 1376260
  281.8 32.9 %all-to-all-start.2 = ((bf16[8,8,3584]{2,1,0:T(8,128)(2,1)}), bf16[8,8,3584]{2,1,0:T(8,128)(2,1)S(1)}, u32[]{:S(2)}, u32[]{:S(2)}) async-start(bf16[8,8,3584]{2,1,0:T(8,128)(2,1)} %fusion.50), calls=%async_computation.2 | async-start | bytes 917504 | tf_op jit(solution)/shard_map/all_to_all | solution.py:192
  (2 other events, 2.3 us)

commit v6 on v5

--- a/solution.py
+++ b/solution.py
@@ -166,12 +166,16 @@
     rows = jnp.concatenate([normed_fwd, normed_bwd], axis=0).astype(jnp.bfloat16)
     rows, blocks = lax.optimization_barrier((rows, blocks))
     blocks = weights_along_z(blocks)
-    gathered = around_x(rows)
+    gathered = lax.all_gather(rows, "x")
     send_cot = reorder(
         slot_matrix(mid_bwd), jnp.concatenate([cot_rows, gate_lanes(flat[3])], axis=1)
     )
     got_cot = dispatch(jnp.zeros_like(send_cot), send_cot)
     gathered, got_cot = lax.optimization_barrier((gathered, got_cot))
+    x = lax.axis_index("x")
+    gathered = [
+        lax.dynamic_index_in_dim(gathered, (x - j + 4) % 4, axis=0, keepdims=False) for j in range(4)
+    ]
     _, got_cot = sides(got_cot)
     cotangent = got_cot[:, :features].astype(jnp.float32)
     gated = (gate_of(got_cot[:, features:]) * cotangent).astype(jnp.bfloat16)

time: 319 us -> 352 us (1.10)
  waiting for transfers between devices: 142 us -> 162 us
  between operations: 1.39 us -> 14.7 us
    ppermute x18 -> x15, waiting for transfers between devices: 107 us -> 124 us  [rotated(): lax.ppermute(x, axis, [(i, (i + by) % length) for i in range(length)])]
    ppermute x18 -> x15, starting transfers between devices: 62 us -> 49.4 us  [rotated(): lax.ppermute(x, axis, [(i, (i + by) % length) for i in range(length)])]
    all_to_all x2, starting transfers between devices: 31.7 us -> 43 us  [give_back(): got = lax.all_to_all(rows, Z8, split_axis=0, concat_axis=0, tiled=True)]
    slice x4 -> x1, local copies, waits for them, and re-layouts: 4.98 us -> 0.26 us  [body(): all_bwd = jnp.concatenate([rows[ROWS:] for rows in gathered], axis=0)]
  transfers between devices with their start and end apart: 26 -> 24, of which waited for: 14 -> 12; matrix products, arithmetic and copies ran while one was open for 9% -> 8% of each run, Pallas kernels for 0% -> 0%
where the time goes in v6:
time: 352 us; the launch traced here: 350 us
  waiting for transfers between devices  162 us (46%)
  starting transfers between devices  132 us (38%)
  other arithmetic  17.5 us (5%)
  local copies, waits for them, and re-layouts  15.9 us (5%)
  between operations  14.7 us (4%)
  matrix products  8.75 us (2%)
    ppermute x15, waiting for transfers between devices, rotated(): lax.ppermute(x, axis, [(i, (i + by) % length) for i in range(length)])  124 us
    ppermute x15, starting transfers between devices, rotated(): lax.ppermute(x, axis, [(i, (i + by) % length) for i in range(length)])  49.4 us
    all_to_all x2, starting transfers between devices, give_back(): got = lax.all_to_all(rows, Z8, split_axis=0, concat_axis=0, tiled=True)  43 us
    all_to_all x2, waiting for transfers between devices, give_back(): got = lax.all_to_all(rows, Z8, split_axis=0, concat_axis=0, tiled=True)  24.8 us
    all_to_all x2, starting transfers between devices, dispatch(): return lax.all_to_all(both, Z16, split_axis=0, concat_axis=0, tiled=True)  16.9 us
    ppermute x1, starting transfers between devices, body(): flat = lax.ppermute(flat, 'zh', [(0, 1), (1, 0)])  15.7 us
    ppermute x1, waiting for transfers between devices, body(): along_y = lax.ppermute(along_y, PP, moves)  9.99 us
  transfers between devices with their start and end apart: 24, of which 12 were waited for; matrix products, arithmetic and copies ran while one was open for 8% of the time, Pallas kernels for 0%

profile of v6, /device:TPU:24, one launch (start us, length us, event | category | flops | bytes accessed | tf_op | source)
XLA Modules:
  0.0 350.2 jit_solution(3807529089145557750)
XLA Ops:
  8.6 15.7 %collective-permute-start = (f32[4,64]{1,0:T(4,128)S(1)}, f32[4,64]{1,0:T(4,128)S(1)}, u32[]{:S(2)}, u32[]{:S(2)}) collective-permute-start(f32[4,64]{1,0:T(4,128)S(1)} %pad_maximum_fusion.7), channel_id=1, source_target_pairs={{0,64},{64,0},{1,65},{65,1},{2,66},{66,2},{3,67},{67,3},{4,68},{68... | collective-permute-start | bytes 3080 | tf_op jit(solution)/shard_map/ppermute | solution.py:138
  25.5 2.7 collective-permute-start.1
  30.6 10.0 %collective-permute-done.1 = bf16[64,3584]{1,0:T(8,128)(2,1)S(1)} collective-permute-done((bf16[64,3584]{1,0:T(8,128)(2,1)S(1)}, bf16[64,3584]{1,0:T(8,128)(2,1)S(1)}, u32[]{:S(2)}, u32[]{:S(2)}) %collective-permute-start.1) | collective-permute-done | bytes 458784 | tf_op jit(solution)/shard_map/ppermute | solution.py:137
  43.9 5.1 %all-to-all-start = ((bf16[16,8,3712]{2,1,0:T(8,128)(2,1)}), bf16[16,8,3712]{2,1,0:T(8,128)(2,1)S(1)}, u32[]{:S(2)}, u32[]{:S(2)}) async-start(bf16[16,8,3712]{2,1,0:T(8,128)(2,1)} %maximum_bitcast_fusion), calls=%async_computation | async-start | bytes 1900544 | tf_op jit(solution)/shard_map/all_to_all | solution.py:149
  53.8 4.7 %collective-permute-start.4 = (bf16[3,32,3584]{2,1,0:T(8,128)(2,1)}, bf16[3,32,3584]{2,1,0:T(8,128)(2,1)}, u32[]{:S(2)}, u32[]{:S(2)}) collective-permute-start(bf16[3,32,3584]{2,1,0:T(8,128)(2,1)} %get-tuple-element.51), channel_id=1, source_target_pairs={{0,48},{16,0},{32,16},{48,32},{1,49},{17,1},{33,17},{49,33},{2,50}... | collective-permute-start | bytes 2064392 | tf_op jit(solution)/shard_map/ppermute | solution.py:58
  58.4 2.7 collective-permute-start.3
  61.1 2.8 collective-permute-start.2
  64.0 22.7 %collective-permute-done.4 = bf16[3,32,3584]{2,1,0:T(8,128)(2,1)} collective-permute-done((bf16[3,32,3584]{2,1,0:T(8,128)(2,1)}, bf16[3,32,3584]{2,1,0:T(8,128)(2,1)}, u32[]{:S(2)}, u32[]{:S(2)}) %collective-permute-start.4) | collective-permute-done | bytes 688160 | tf_op jit(solution)/shard_map/ppermute | solution.py:58
  86.7 5.4 %collective-permute-done.2 = bf16[3,32,3584]{2,1,0:T(8,128)(2,1)} collective-permute-done((bf16[3,32,3584]{2,1,0:T(8,128)(2,1)S(1)}, bf16[3,32,3584]{2,1,0:T(8,128)(2,1)}, u32[]{:S(2)}, u32[]{:S(2)}) %collective-permute-start.2) | collective-permute-done | bytes 688160 | tf_op jit(solution)/shard_map/ppermute | solution.py:58
  99.5 11.7 %all-to-all-start.1 = ((bf16[16,8,3712]{2,1,0:T(8,128)(2,1)}), bf16[16,8,3712]{2,1,0:T(8,128)(2,1)S(1)}, u32[]{:S(2)}, u32[]{:S(2)}) async-start(bf16[16,8,3712]{2,1,0:T(8,128)(2,1)} %maximum_bitcast_fusion.1), calls=%async_computation.1 | async-start | bytes 1900544 | tf_op jit(solution)/shard_map/all_to_all | solution.py:149
  111.2 3.8 %collective-permute-start.5 = (bf16[3,32,3584]{2,1,0:T(8,128)(2,1)}, bf16[3,32,3584]{2,1,0:T(8,128)(2,1)}, u32[]{:S(2)}, u32[]{:S(2)}) collective-permute-start(bf16[3,32,3584]{2,1,0:T(8,128)(2,1)} %get-tuple-element.28), channel_id=1, source_target_pairs={{0,2},{2,4},{4,6},{6,0},{1,3},{3,5},{5,7},{7,1},{8,10},{10,12},{12... | collective-permute-start | bytes 2064392 | tf_op jit(solution)/shard_map/ppermute | solution.py:58
  115.1 4.3 %collective-permute-start.10 = (bf16[3,32,3584]{2,1,0:T(8,128)(2,1)}, bf16[3,32,3584]{2,1,0:T(8,128)(2,1)}, u32[]{:S(2)}, u32[]{:S(2)}) collective-permute-start(bf16[3,32,3584]{2,1,0:T(8,128)(2,1)} %get-tuple-element.30), channel_id=1, source_target_pairs={{0,4},{2,6},{4,0},{6,2},{1,5},{3,7},{5,1},{7,3},{8,12},{10,14},{12... | collective-permute-start | bytes 2064392 | tf_op jit(solution)/shard_map/ppermute | solution.py:58
  119.4 3.4 collective-permute-start.11
  123.6 48.7 %collective-permute-done.5 = bf16[3,32,3584]{2,1,0:T(8,128)(2,1)} collective-permute-done((bf16[3,32,3584]{2,1,0:T(8,128)(2,1)}, bf16[3,32,3584]{2,1,0:T(8,128)(2,1)}, u32[]{:S(2)}, u32[]{:S(2)}) %collective-permute-start.5) | collective-permute-done | bytes 688160 | tf_op jit(solution)/shard_map/ppermute | solution.py:58
  179.8 2.6 collective-permute-start.9
  182.4 2.7 collective-permute-start.8
  185.1 2.9 collective-permute-start.7
  190.4 10.5 %collective-permute-done.10 = bf16[3,32,3584]{2,1,0:T(8,128)(2,1)} collective-permute-done((bf16[3,32,3584]{2,1,0:T(8,128)(2,1)}, bf16[3,32,3584]{2,1,0:T(8,128)(2,1)}, u32[]{:S(2)}, u32[]{:S(2)}) %collective-permute-start.10) | collective-permute-done | bytes 688160 | tf_op jit(solution)/shard_map/ppermute | solution.py:58
  200.9 7.4 %collective-permute-done.7 = bf16[64,3584]{1,0:T(8,128)(2,1)S(1)} collective-permute-done((bf16[64,3584]{1,0:T(8,128)(2,1)S(1)}, bf16[64,3584]{1,0:T(8,128)(2,1)S(1)}, u32[]{:S(2)}, u32[]{:S(2)}) %collective-permute-start.7) | collective-permute-done | bytes 458784 | tf_op jit(solution)/shard_map/ppermute | solution.py:58
  212.9 2.7 collective-permute-done.12
  219.1 2.7 collective-permute-start.16
  221.8 2.6 collective-permute-start.18
  224.4 4.5 %collective-permute-start.17 = (bf16[64,3584]{1,0:T(8,128)(2,1)S(1)}, bf16[64,3584]{1,0:T(8,128)(2,1)S(1)}, u32[]{:S(2)}, u32[]{:S(2)}) collective-permute-start(bf16[64,3584]{1,0:T(8,128)(2,1)S(1)} %get-tuple-element.56), channel_id=1, source_target_pairs={{0,48},{16,0},{32,16},{48,32},{1,49},{17,1},{33,17},{49,33},{2,50}... | collective-permute-start | bytes 1376264 | tf_op jit(solution)/shard_map/ppermute | solution.py:58
  230.7 5.2 %collective-permute-done.16 = bf16[64,3584]{1,0:T(8,128)(2,1)S(1)} collective-permute-done((bf16[64,3584]{1,0:T(8,128)(2,1)S(1)}, bf16[64,3584]{1,0:T(8,128)(2,1)S(1)}, u32[]{:S(2)}, u32[]{:S(2)}) %collective-permute-start.16) | collective-permute-done | bytes 458784 | tf_op jit(solution)/shard_map/ppermute | solution.py:58
  235.9 9.0 %collective-permute-done.18 = bf16[64,3584]{1,0:T(8,128)(2,1)S(1)} collective-permute-done((bf16[64,3584]{1,0:T(8,128)(2,1)S(1)}, bf16[64,3584]{1,0:T(8,128)(2,1)S(1)}, u32[]{:S(2)}, u32[]{:S(2)}) %collective-permute-start.18) | collective-permute-done | bytes 458784 | tf_op jit(solution)/shard_map/ppermute | solution.py:58
  246.5 33.4 %all-to-all-start.3 = ((bf16[8,8,3584]{2,1,0:T(8,128)(2,1)}), bf16[8,8,3584]{2,1,0:T(8,128)(2,1)S(1)}, u32[]{:S(2)}, u32[]{:S(2)}) async-start(bf16[8,8,3584]{2,1,0:T(8,128)(2,1)} %fusion.51), calls=%async_computation.3 | async-start | bytes 917504 | tf_op jit(solution)/shard_map/all_to_all | solution.py:196
  280.0 2.7 collective-permute-start.13
  285.3 4.5 %collective-permute-start.14 = (bf16[64,3584]{1,0:T(8,128)(2,1)S(1)}, bf16[64,3584]{1,0:T(8,128)(2,1)S(1)}, u32[]{:S(2)}, u32[]{:S(2)}) collective-permute-start(bf16[64,3584]{1,0:T(8,128)(2,1)S(1)} %get-tuple-element.59), channel_id=1, source_target_pairs={{0,48},{16,0},{32,16},{48,32},{1,49},{17,1},{33,17},{49,33},{2,50}... | collective-permute-start | bytes 1376264 | tf_op jit(solution)/shard_map/ppermute | solution.py:58
  290.0 6.9 %collective-permute-done.13 = bf16[64,3584]{1,0:T(8,128)(2,1)S(1)} collective-permute-done((bf16[64,3584]{1,0:T(8,128)(2,1)S(1)}, bf16[64,3584]{1,0:T(8,128)(2,1)S(1)}, u32[]{:S(2)}, u32[]{:S(2)}) %collective-permute-start.13) | collective-permute-done | bytes 458784 | tf_op jit(solution)/shard_map/ppermute | solution.py:58
  296.9 8.5 %collective-permute-done.15 = bf16[64,3584]{1,0:T(8,128)(2,1)S(1)} collective-permute-done((bf16[64,3584]{1,0:T(8,128)(2,1)S(1)}, bf16[64,3584]{1,0:T(8,128)(2,1)S(1)}, u32[]{:S(2)}, u32[]{:S(2)}) %collective-permute-start.15) | collective-permute-done | bytes 458784 | tf_op jit(solution)/shard_map/ppermute | solution.py:58
  306.5 9.6 %all-to-all-start.2 = ((bf16[8,8,3584]{2,1,0:T(8,128)(2,1)}), bf16[8,8,3584]{2,1,0:T(8,128)(2,1)S(1)}, u32[]{:S(2)}, u32[]{:S(2)}) async-start(bf16[8,8,3584]{2,1,0:T(8,128)(2,1)} %fusion.50), calls=%async_computation.2 | async-start | bytes 917504 | tf_op jit(solution)/shard_map/all_to_all | solution.py:196
  317.4 24.8 %all-to-all-done.2 = bf16[8,8,3584]{2,1,0:T(8,128)(2,1)S(1)} async-done(((bf16[8,8,3584]{2,1,0:T(8,128)(2,1)}), bf16[8,8,3584]{2,1,0:T(8,128)(2,1)S(1)}, u32[]{:S(2)}, u32[]{:S(2)}) %all-to-all-start.2) | async-done | bytes 458784 | tf_op jit(solution)/shard_map/all_to_all | solution.py:196
  (99 shorter events, 48.7 us)
Async XLA Ops:
  7.2 22.6 %copy-start = (bf16[1,64,3584]{2,1,0:T(8,128)(2,1)S(1)}, bf16[1,64,3584]{2,1,0:T(8,128)(2,1)}, u32[]{:S(2)}) copy-start(bf16[1,64,3584]{2,1,0:T(8,128)(2,1)} %param.11) | copy-start | bytes 1376260
  8.6 21.5 %collective-permute-start = (f32[4,64]{1,0:T(4,128)S(1)}, f32[4,64]{1,0:T(4,128)S(1)}, u32[]{:S(2)}, u32[]{:S(2)}) collective-permute-start(f32[4,64]{1,0:T(4,128)S(1)} %pad_maximum_fusion.7), channel_id=1, source_target_pairs={{0,64},{64,0},{1,65},{65,1},{2,66},{66,2},{3,67},{67,3},{4,68},{68... | collective-permute-start | bytes 3080 | tf_op jit(solution)/shard_map/ppermute | solution.py:138
  25.5 15.1 %collective-permute-start.1 = (bf16[64,3584]{1,0:T(8,128)(2,1)S(1)}, bf16[64,3584]{1,0:T(8,128)(2,1)S(1)}, u32[]{:S(2)}, u32[]{:S(2)}) collective-permute-start(bf16[64,3584]{1,0:T(8,128)(2,1)S(1)} %bitcast_select_fusion.1), channel_id=1, source_target_pairs={{64,192},{0,384},{192,320},{128,0},{320,448},{256,128},{448,64},{3... | collective-permute-start | bytes 1376264 | tf_op jit(solution)/shard_map/ppermute | solution.py:137
  42.6 6.5 %copy-start.3 = (bf16[1,1,3584,128]{3,2,1,0:T(8,128)(2,1)S(1)}, bf16[1,1,3584,128]{3,2,1,0:T(8,128)(2,1)}, u32[]{:S(2)}) copy-start(bf16[1,1,3584,128]{3,2,1,0:T(8,128)(2,1)} %param.17) | copy-start | bytes 2752516
  43.9 51.3 %all-to-all-start = ((bf16[16,8,3712]{2,1,0:T(8,128)(2,1)}), bf16[16,8,3712]{2,1,0:T(8,128)(2,1)S(1)}, u32[]{:S(2)}, u32[]{:S(2)}) async-start(bf16[16,8,3712]{2,1,0:T(8,128)(2,1)} %maximum_bitcast_fusion), calls=%async_computation | async-start | bytes 1900544 | tf_op jit(solution)/shard_map/all_to_all | solution.py:149
  49.0 130.3 %all-gather.3.cloned.1.call-start = ((), (), s32[]{:S(2)}) async-start(), calls=%async_computation.4 | async-start | bytes 4587520 | tf_op jit(solution)/shard_map/all_gather | solution.py:169
  53.8 32.9 %collective-permute-start.4 = (bf16[3,32,3584]{2,1,0:T(8,128)(2,1)}, bf16[3,32,3584]{2,1,0:T(8,128)(2,1)}, u32[]{:S(2)}, u32[]{:S(2)}) collective-permute-start(bf16[3,32,3584]{2,1,0:T(8,128)(2,1)} %get-tuple-element.51), channel_id=1, source_target_pairs={{0,48},{16,0},{32,16},{48,32},{1,49},{17,1},{33,17},{49,33},{2,50}... | collective-permute-start | bytes 2064392 | tf_op jit(solution)/shard_map/ppermute | solution.py:58
  58.4 28.3 %collective-permute-start.3 = (bf16[3,32,3584]{2,1,0:T(8,128)(2,1)S(1)}, bf16[3,32,3584]{2,1,0:T(8,128)(2,1)}, u32[]{:S(2)}, u32[]{:S(2)}) collective-permute-start(bf16[3,32,3584]{2,1,0:T(8,128)(2,1)S(1)} %get-tuple-element.52), channel_id=1, source_target_pairs={{0,32},{16,48},{32,0},{48,16},{1,33},{17,49},{33,1},{49,17},{2,34}... | collective-permute-start | bytes 2064392 | tf_op jit(solution)/shard_map/ppermute | solution.py:58
  61.1 31.0 %collective-permute-start.2 = (bf16[3,32,3584]{2,1,0:T(8,128)(2,1)S(1)}, bf16[3,32,3584]{2,1,0:T(8,128)(2,1)}, u32[]{:S(2)}, u32[]{:S(2)}) collective-permute-start(bf16[3,32,3584]{2,1,0:T(8,128)(2,1)S(1)} %get-tuple-element.53), channel_id=1, source_target_pairs={{0,16},{16,32},{32,48},{48,0},{1,17},{17,33},{33,49},{49,1},{2,18}... | collective-permute-start | bytes 2064392 | tf_op jit(solution)/shard_map/ppermute | solution.py:58
  99.5 79.9 %all-to-all-start.1 = ((bf16[16,8,3712]{2,1,0:T(8,128)(2,1)}), bf16[16,8,3712]{2,1,0:T(8,128)(2,1)S(1)}, u32[]{:S(2)}, u32[]{:S(2)}) async-start(bf16[16,8,3712]{2,1,0:T(8,128)(2,1)} %maximum_bitcast_fusion.1), calls=%async_computation.1 | async-start | bytes 1900544 | tf_op jit(solution)/shard_map/all_to_all | solution.py:149
  111.2 61.2 %collective-permute-start.5 = (bf16[3,32,3584]{2,1,0:T(8,128)(2,1)}, bf16[3,32,3584]{2,1,0:T(8,128)(2,1)}, u32[]{:S(2)}, u32[]{:S(2)}) collective-permute-start(bf16[3,32,3584]{2,1,0:T(8,128)(2,1)} %get-tuple-element.28), channel_id=1, source_target_pairs={{0,2},{2,4},{4,6},{6,0},{1,3},{3,5},{5,7},{7,1},{8,10},{10,12},{12... | collective-permute-start | bytes 2064392 | tf_op jit(solution)/shard_map/ppermute | solution.py:58
  115.1 85.8 %collective-permute-start.10 = (bf16[3,32,3584]{2,1,0:T(8,128)(2,1)}, bf16[3,32,3584]{2,1,0:T(8,128)(2,1)}, u32[]{:S(2)}, u32[]{:S(2)}) collective-permute-start(bf16[3,32,3584]{2,1,0:T(8,128)(2,1)} %get-tuple-element.30), channel_id=1, source_target_pairs={{0,4},{2,6},{4,0},{6,2},{1,5},{3,7},{5,1},{7,3},{8,12},{10,14},{12... | collective-permute-start | bytes 2064392 | tf_op jit(solution)/shard_map/ppermute | solution.py:58
  119.4 81.5 %collective-permute-start.11 = (bf16[3,32,3584]{2,1,0:T(8,128)(2,1)S(1)}, bf16[3,32,3584]{2,1,0:T(8,128)(2,1)}, u32[]{:S(2)}, u32[]{:S(2)}) collective-permute-start(bf16[3,32,3584]{2,1,0:T(8,128)(2,1)S(1)} %get-tuple-element.31), channel_id=1, source_target_pairs={{0,6},{2,0},{4,2},{6,4},{1,7},{3,1},{5,3},{7,5},{8,14},{10,8},{12,... | collective-permute-start | bytes 2064392 | tf_op jit(solution)/shard_map/ppermute | solution.py:58
  175.6 9.5 %collective-permute-start.6 = (bf16[3,64,3584]{2,1,0:T(8,128)(2,1)}, bf16[3,64,3584]{2,1,0:T(8,128)(2,1)}, u32[]{:S(2)}, u32[]{:S(2)}) collective-permute-start(bf16[3,64,3584]{2,1,0:T(8,128)(2,1)} %constant_dynamic-update-slice_fusion), channel_id=1, source_target_pairs={{0,1},{1,0},{2,3},{3,2},{4,5},{5,4},{6,7},{7,6},{8,9},{9,8},{10,11... | collective-permute-start | bytes 4128776 | tf_op jit(solution)/shard_map/ppermute | solution.py:119
  179.8 32.7 %copy-start.2 = (bf16[512,3584]{1,0:T(8,128)(2,1)S(1)}, bf16[512,3584]{1,0:T(8,128)(2,1)}, u32[]{:S(2)}) copy-start(bf16[512,3584]{1,0:T(8,128)(2,1)} %all-gather.3.cloned.1.call-done) | copy-start | bytes 11010052
  179.8 21.0 %collective-permute-start.9 = (bf16[64,3584]{1,0:T(8,128)(2,1)S(1)}, bf16[64,3584]{1,0:T(8,128)(2,1)S(1)}, u32[]{:S(2)}, u32[]{:S(2)}) collective-permute-start(bf16[64,3584]{1,0:T(8,128)(2,1)S(1)} %fusion.35), channel_id=1, source_target_pairs={{0,48},{16,0},{32,16},{48,32},{1,49},{17,1},{33,17},{49,33},{2,50}... | collective-permute-start | bytes 1376264 | tf_op jit(solution)/shard_map/ppermute | solution.py:58
  182.4 18.5 %collective-permute-start.8 = (bf16[64,3584]{1,0:T(8,128)(2,1)S(1)}, bf16[64,3584]{1,0:T(8,128)(2,1)S(1)}, u32[]{:S(2)}, u32[]{:S(2)}) collective-permute-start(bf16[64,3584]{1,0:T(8,128)(2,1)S(1)} %fusion.35), channel_id=1, source_target_pairs={{0,32},{16,48},{32,0},{48,16},{1,33},{17,49},{33,1},{49,17},{2,34}... | collective-permute-start | bytes 1376264 | tf_op jit(solution)/shard_map/ppermute | solution.py:58
  185.1 23.1 %collective-permute-start.7 = (bf16[64,3584]{1,0:T(8,128)(2,1)S(1)}, bf16[64,3584]{1,0:T(8,128)(2,1)S(1)}, u32[]{:S(2)}, u32[]{:S(2)}) collective-permute-start(bf16[64,3584]{1,0:T(8,128)(2,1)S(1)} %fusion.35), channel_id=1, source_target_pairs={{0,16},{16,32},{32,48},{48,0},{1,17},{17,33},{33,49},{49,1},{2,18}... | collective-permute-start | bytes 1376264 | tf_op jit(solution)/shard_map/ppermute | solution.py:58
  210.6 5.0 %collective-permute-start.12 = (bf16[3,64,3584]{2,1,0:T(8,128)(2,1)S(1)}, bf16[3,64,3584]{2,1,0:T(8,128)(2,1)S(1)}, u32[]{:S(2)}, u32[]{:S(2)}) collective-permute-start(bf16[3,64,3584]{2,1,0:T(8,128)(2,1)S(1)} %constant_dynamic-update-slice_fusion.2), channel_id=1, source_target_pairs={{0,1},{1,0},{2,3},{3,2},{4,5},{5,4},{6,7},{7,6},{8,9},{9,8},{10,11... | collective-permute-start | bytes 4128776 | tf_op jit(solution)/shard_map/ppermute | solution.py:119
  215.9 1.2 copy-start.4
  219.1 16.8 %collective-permute-start.16 = (bf16[64,3584]{1,0:T(8,128)(2,1)S(1)}, bf16[64,3584]{1,0:T(8,128)(2,1)S(1)}, u32[]{:S(2)}, u32[]{:S(2)}) collective-permute-start(bf16[64,3584]{1,0:T(8,128)(2,1)S(1)} %get-tuple-element.54), channel_id=1, source_target_pairs={{0,32},{16,48},{32,0},{48,16},{1,33},{17,49},{33,1},{49,17},{2,34}... | collective-permute-start | bytes 1376264 | tf_op jit(solution)/shard_map/ppermute | solution.py:58
  221.8 23.1 %collective-permute-start.18 = (bf16[64,3584]{1,0:T(8,128)(2,1)S(1)}, bf16[64,3584]{1,0:T(8,128)(2,1)S(1)}, u32[]{:S(2)}, u32[]{:S(2)}) collective-permute-start(bf16[64,3584]{1,0:T(8,128)(2,1)S(1)} %get-tuple-element.55), channel_id=1, source_target_pairs={{0,16},{16,32},{32,48},{48,0},{1,17},{17,33},{33,49},{49,1},{2,18}... | collective-permute-start | bytes 1376264 | tf_op jit(solution)/shard_map/ppermute | solution.py:58
  224.4 20.5 %collective-permute-start.17 = (bf16[64,3584]{1,0:T(8,128)(2,1)S(1)}, bf16[64,3584]{1,0:T(8,128)(2,1)S(1)}, u32[]{:S(2)}, u32[]{:S(2)}) collective-permute-start(bf16[64,3584]{1,0:T(8,128)(2,1)S(1)} %get-tuple-element.56), channel_id=1, source_target_pairs={{0,48},{16,0},{32,16},{48,32},{1,49},{17,1},{33,17},{49,33},{2,50}... | collective-permute-start | bytes 1376264 | tf_op jit(solution)/shard_map/ppermute | solution.py:58
  246.5 60.0 %all-to-all-start.3 = ((bf16[8,8,3584]{2,1,0:T(8,128)(2,1)}), bf16[8,8,3584]{2,1,0:T(8,128)(2,1)S(1)}, u32[]{:S(2)}, u32[]{:S(2)}) async-start(bf16[8,8,3584]{2,1,0:T(8,128)(2,1)} %fusion.51), calls=%async_computation.3 | async-start | bytes 917504 | tf_op jit(solution)/shard_map/all_to_all | solution.py:196
  279.9 36.2 %copy-start.5 = (s32[1,64,1]{1,2,0:T(1,128)S(1)}, s32[1,64,1]{1,2,0:T(1,128)}, u32[]{:S(2)}) copy-start(s32[1,64,1]{1,2,0:T(1,128)} %param.13) | copy-start | bytes 772
  280.0 16.9 %collective-permute-start.13 = (bf16[64,3584]{1,0:T(8,128)(2,1)S(1)}, bf16[64,3584]{1,0:T(8,128)(2,1)S(1)}, u32[]{:S(2)}, u32[]{:S(2)}) collective-permute-start(bf16[64,3584]{1,0:T(8,128)(2,1)S(1)} %get-tuple-element.57), channel_id=1, source_target_pairs={{0,32},{16,48},{32,0},{48,16},{1,33},{17,49},{33,1},{49,17},{2,34}... | collective-permute-start | bytes 1376264 | tf_op jit(solution)/shard_map/ppermute | solution.py:58
  282.7 22.7 %collective-permute-start.15 = (bf16[64,3584]{1,0:T(8,128)(2,1)S(1)}, bf16[64,3584]{1,0:T(8,128)(2,1)S(1)}, u32[]{:S(2)}, u32[]{:S(2)}) collective-permute-start(bf16[64,3584]{1,0:T(8,128)(2,1)S(1)} %get-tuple-element.58), channel_id=1, source_target_pairs={{0,16},{16,32},{32,48},{48,0},{1,17},{17,33},{33,49},{49,1},{2,18}... | collective-permute-start | bytes 1376264 | tf_op jit(solution)/shard_map/ppermute | solution.py:58
  285.3 20.1 %collective-permute-start.14 = (bf16[64,3584]{1,0:T(8,128)(2,1)S(1)}, bf16[64,3584]{1,0:T(8,128)(2,1)S(1)}, u32[]{:S(2)}, u32[]{:S(2)}) collective-permute-start(bf16[64,3584]{1,0:T(8,128)(2,1)S(1)} %get-tuple-element.59), channel_id=1, source_target_pairs={{0,48},{16,0},{32,16},{48,32},{1,49},{17,1},{33,17},{49,33},{2,50}... | collective-permute-start | bytes 1376264 | tf_op jit(solution)/shard_map/ppermute | solution.py:58
  289.8 53.5 %copy-start.1 = (bf16[1,64,3584]{2,1,0:T(8,128)(2,1)S(1)}, bf16[1,64,3584]{2,1,0:T(8,128)(2,1)}, u32[]{:S(2)}) copy-start(bf16[1,64,3584]{2,1,0:T(8,128)(2,1)} %param.11) | copy-start | bytes 1376260
  306.5 35.7 %all-to-all-start.2 = ((bf16[8,8,3584]{2,1,0:T(8,128)(2,1)}), bf16[8,8,3584]{2,1,0:T(8,128)(2,1)S(1)}, u32[]{:S(2)}, u32[]{:S(2)}) async-start(bf16[8,8,3584]{2,1,0:T(8,128)(2,1)} %fusion.50), calls=%async_computation.2 | async-start | bytes 917504 | tf_op jit(solution)/shard_map/all_to_all | solution.py:196
Sparse Core Ops, SparseCore 0:
  97.2 49.8 all-gather.2
